TPU v7x, 32 devices: a whole 2x2x4 slice. The times are simulated.
32 devices in a mesh: lat: 4 (over x, core), lon: 8 (over z, y).
Axes of the slice: x: 2, y: 2, z: 4, core: 2. Of those that a mesh axis runs over, the one named last changes fastest.
Arguments:
- latent: bfloat16 [64, 128, 641], P('lat', 'lon'), may hold values from -6 to 6
- filters: bfloat16 [9, 64, 9, 33], P(None, 'lat'), may hold values from -0.59765625 to 0.59765625
- widths: int32 [64, 9], P('lat'), may hold values from 0 to 16, as said below
- mix_weight: bfloat16 [9, 641, 512], P(None, None, ('lat', 'lon')), may hold values from -0.078125 to 0.078125
- mix_bias: float32 [512], replicated, may hold values from -3 to 3
Outputs:
- convolved: bfloat16 [64, 128, 512], P('lat', 'lon')
Inputs may be any that keep to these rules, and one draw needn't show every extreme that they name: widths grow toward the poles and are at most 16, reached in rows next to a pole.
All inputs are finite; a program needn't handle non-finite values.
Results may differ from a plain program's by a relative error of at most 0.0048.
Values may be sent and summed in bfloat16 or wider, within the bound.
No kernel may reach another device: no remote copies, remote signals or barrier semaphores. Data moves between devices by JAX's collectives and lax.ppermute only.
A program may use at most 64 MiB of HBM per device.

v0:
```python
import jax
import jax.numpy as jnp
from jax import lax
from jax.sharding import PartitionSpec as P

RADIUS = 4
LON_REACH = 16


def padded(cells, sides, width, closed):
    for axis, dim in sides:
        count = lax.axis_size(axis)
        ends = count if closed else count - 1
        head = lax.slice_in_dim(cells, 0, width, axis=dim)
        tail = lax.slice_in_dim(cells, cells.shape[dim] - width, cells.shape[dim], axis=dim)
        cells = jnp.concatenate(
            [
                lax.ppermute(tail, axis, [(i, (i + 1) % count) for i in range(ends)]),
                cells,
                lax.ppermute(head, axis, [((i + 1) % count, i) for i in range(ends)]),
            ],
            axis=dim,
        )
    return cells


def passed_along(block, axis, distance):
    devices = range(lax.axis_size(axis))
    route = [((i - distance) % len(devices), i) for i in devices]
    return lax.ppermute(block, axis, route)


def mend_poles(banded, polar_pair, lat_index, lat_count):
    upper_rim = jnp.where(lat_index == 0, polar_pair[0], banded[:RADIUS])
    lower_rim = jnp.where(lat_index == lat_count - 1, polar_pair[1], banded[-RADIUS:])
    return jnp.concatenate([upper_rim, banded[RADIUS:-RADIUS], lower_rim], 0)


def body(latent, filters, widths, mix_weight, mix_bias):
    lat_count = lax.axis_size("lat")
    lon_count = lax.axis_size("lon")
    lat_index = lax.axis_index("lat")
    banded = padded(latent, (("lat", 0),), RADIUS, False)
    polar_pair = passed_along(
        (latent[:RADIUS][::-1], latent[-RADIUS:][::-1]), "lon", lon_count // 2
    )
    banded = mend_poles(banded, polar_pair, lat_index, lat_count)
    extended = padded(banded, (("lon", 1),), LON_REACH, True)
    lat_dev, lon_dev, channels = latent.shape
    stencil_span = 2 * LON_REACH + 1
    lookup_table_shape = (lon_dev, lon_dev + 2 * LON_REACH, stencil_span)
    column = lax.broadcasted_iota(jnp.int32, lookup_table_shape, 0)
    source = lax.broadcasted_iota(jnp.int32, lookup_table_shape, 1)
    offset = lax.broadcasted_iota(jnp.int32, lookup_table_shape, 2)
    basis_selector = (source == column + offset).astype(jnp.bfloat16)
    shifts = jnp.arange(stencil_span, dtype=jnp.int32) - LON_REACH
    inside = jnp.abs(shifts)[None, None, :] <= widths[:, :, None]
    coefficients = jnp.where(inside[None], filters, jnp.zeros((), filters.dtype))
    per_row = jnp.transpose(coefficients, (1, 0, 2, 3))

    def one_row(packed):
        row_coefficient, row_index = packed
        banded_matrix = jnp.einsum(
            "blw,ocw->bolc", row_coefficient, basis_selector, preferred_element_type=jnp.float32
        ).astype(jnp.bfloat16)
        slab_rows = lax.dynamic_slice_in_dim(extended, row_index, 2 * RADIUS + 1, 0)
        return jnp.einsum(
            "kjdp,dpc->kjc", banded_matrix, slab_rows, preferred_element_type=jnp.float32
        ).astype(jnp.bfloat16)

    features = lax.map(one_row, (per_row, jnp.arange(lat_dev, dtype=jnp.int32)))
    channel_mixed_output = lax.dot_general(
        features,
        lax.all_gather(mix_weight, ("lat", "lon"), axis=2, tiled=True),
        (((1, 3), (0, 1)), ((), ())),
        preferred_element_type=jnp.float32,
    )
    return jax.nn.gelu(channel_mixed_output + mix_bias, approximate=False).astype(jnp.bfloat16)


def solution(mesh):
    placed = (
        P("lat", "lon", None),
        P(None, "lat", None, None),
        P("lat", None),
        P(None, None, ("lat", "lon")),
        P(),
    )
    return jax.shard_map(
        body, mesh=mesh, in_specs=placed, out_specs=P("lat", "lon", None), check_vma=False
    )
```

profile of v0, /device:TPU:0, one launch (start us, length us, event | category | flops | bytes accessed | tf_op | source)
XLA Modules:
  0.0 138.4 jit_solution(269963921856012646)
XLA Ops:
  6.5 0.7 all-gather.2.cloned.1.call-update
  7.3 1.0 fusion.38
  8.2 4.1 %collective-permute-start.2 = (bf16[4,16,641]{2,1,0:T(8,128)(2,1)S(1)}, bf16[4,16,641]{2,1,0:T(8,128)(2,1)S(1)}, u32[]{:S(2)}, u32[]{:S(2)}) collective-permute-start(bf16[4,16,641]{2,1,0:T(8,128)(2,1)S(1)} %rev.7), channel_id=1, source_target_pairs={{4,0},{5,1},{6,2},{7,3},{0,4},{1,5},{2,6},{3,7},{12,8},{13,9},{14,... | collective-permute-start | bytes 246152 | tf_op jit(solution)/shard_map/ppermute | solution.py:30
  12.3 1.3 collective-permute-start.3
  13.6 3.0 %collective-permute-start.1 = (bf16[4,16,641]{2,1,0:T(8,128)(2,1)S(1)}, bf16[4,16,641]{2,1,0:T(8,128)(2,1)S(1)}, u32[]{:S(2)}, u32[]{:S(2)}) collective-permute-start(bf16[4,16,641]{2,1,0:T(8,128)(2,1)S(1)} %get-tuple-element.61), channel_id=1, source_target_pairs={{0,8},{8,16},{16,24},{1,9},{9,17},{17,25},{2,10},{10,18},{18,26},{... | collective-permute-start | bytes 246152 | tf_op jit(solution)/shard_map/ppermute | solution.py:18
  17.3 8.1 %collective-permute-done = bf16[4,16,641]{2,1,0:T(8,128)(2,1)S(1)} collective-permute-done((bf16[4,16,641]{2,1,0:T(8,128)(2,1)S(1)}, bf16[4,16,641]{2,1,0:T(8,128)(2,1)S(1)}, u32[]{:S(2)}, u32[]{:S(2)}) %collective-permute-start) | collective-permute-done | bytes 82080 | tf_op jit(solution)/shard_map/ppermute | solution.py:30
  25.4 1.1 pad_maximum_fusion.1
  26.5 1.6 %collective-permute-start.4 = (bf16[24,16,641]{2,1,0:T(8,128)(2,1)S(1)}, bf16[24,16,641]{2,1,0:T(8,128)(2,1)S(1)}, u32[]{:S(2)}, u32[]{:S(2)}) collective-permute-start(bf16[24,16,641]{2,1,0:T(8,128)(2,1)S(1)} %pad_maximum_fusion.1), channel_id=1, source_target_pairs={{0,1},{1,2},{2,3},{3,4},{4,5},{5,6},{6,7},{7,0},{8,9},{9,10},{10,1... | collective-permute-start | bytes 1476872 | tf_op jit(solution)/shard_map/ppermute | solution.py:18
  28.0 3.2 %collective-permute-start.5 = (bf16[24,16,641]{2,1,0:T(8,128)(2,1)S(1)}, bf16[24,16,641]{2,1,0:T(8,128)(2,1)}, u32[]{:S(2)}, u32[]{:S(2)}) collective-permute-start(bf16[24,16,641]{2,1,0:T(8,128)(2,1)S(1)} %pad_maximum_fusion.1), channel_id=1, source_target_pairs={{1,0},{2,1},{3,2},{4,3},{5,4},{6,5},{7,6},{0,7},{9,8},{10,9},{11,1... | collective-permute-start | bytes 1476872 | tf_op jit(solution)/shard_map/ppermute | solution.py:20
  31.2 0.8 broadcast_compare_fusion
  32.0 1.1 fusion.25
  33.1 23.5 %collective-permute-done.4 = bf16[24,16,641]{2,1,0:T(8,128)(2,1)S(1)} collective-permute-done((bf16[24,16,641]{2,1,0:T(8,128)(2,1)S(1)}, bf16[24,16,641]{2,1,0:T(8,128)(2,1)S(1)}, u32[]{:S(2)}, u32[]{:S(2)}) %collective-permute-start.4) | collective-permute-done | bytes 492320 | tf_op jit(solution)/shard_map/ppermute | solution.py:18
  56.7 2.3 %collective-permute-done.5 = bf16[24,16,641]{2,1,0:T(8,128)(2,1)} collective-permute-done((bf16[24,16,641]{2,1,0:T(8,128)(2,1)S(1)}, bf16[24,16,641]{2,1,0:T(8,128)(2,1)}, u32[]{:S(2)}, u32[]{:S(2)}) %collective-permute-start.5) | collective-permute-done | bytes 492320 | tf_op jit(solution)/shard_map/ppermute | solution.py:20
  59.0 1.2 pad_maximum_fusion
  60.2 63.4 %while.11 = (s32[]{:T(128)}, bf16[16,9,16,641]{3,2,1,0:T(8,128)(2,1)}, bf16[16,9,9,33]{3,2,1,0:T(8,128)(2,1)S(1)}, s32[16]{0:T(128)S(1)}, bf16[24,48,641]{2,1,0:...) while((s32[]{:T(128)}, bf16[16,9,16,641]{3,2,1,0:T(8,128)(2,1)}, ...), condition=%wide.region_1.2_spmd.clone, body=%wide.region_0.1_spmd.clone.sunk | while | flops 84024720 | bytes 1636491 | solution.py:71
  63.2 1.1 fusion.51
  67.1 1.0 fusion.51
  71.1 1.0 fusion.51
  75.0 1.1 fusion.51
  79.0 1.1 fusion.51
  82.9 1.0 fusion.51
  86.9 1.1 fusion.51
  90.9 1.1 fusion.51
  94.8 1.1 fusion.51
  98.8 1.1 fusion.51
  102.8 1.0 fusion.51
  106.7 1.1 fusion.51
  110.7 1.0 fusion.51
  114.7 1.0 fusion.51
  118.6 1.0 fusion.51
  122.6 1.1 fusion.51
  123.6 7.9 %fusion.28 = bf16[16,16,512]{2,1,0:T(8,128)(2,1)} fusion(bf16[16,9,16,641]{3,2,1,0:T(8,128)(2,1)} %get-tuple-element.37, bf16[9,641,512]{1,2,0:T(8,128)(2,1)} %all-gather.2.cloned.1.call-done, f32[512]{0:T(512)S(1)} %copy-done.1), kind=kOutput, calls=%fused_computation.28 | convolution fusion | flops 1520959488 | bytes 9125376 | tf_op jit(solution)/shard_map/dot_general | solution.py:72
  (49 shorter events, 16.5 us)
Async XLA Ops:
  6.5 52.4 %copy-start = (bf16[16,16,641]{2,1,0:T(8,128)(2,1)S(1)}, bf16[16,16,641]{2,1,0:T(8,128)(2,1)}, u32[]{:S(2)}) copy-start(bf16[16,16,641]{2,1,0:T(8,128)(2,1)} %param.7) | copy-start | bytes 984580
  6.5 117.1 %all-gather.2.cloned.1.call-start = ((), (), s32[]{:S(2)}) async-start(), calls=%async_computation | async-start | bytes 7299072 | tf_op jit(solution)/shard_map/all_gather | solution.py:74
  8.2 9.0 %collective-permute-start.2 = (bf16[4,16,641]{2,1,0:T(8,128)(2,1)S(1)}, bf16[4,16,641]{2,1,0:T(8,128)(2,1)S(1)}, u32[]{:S(2)}, u32[]{:S(2)}) collective-permute-start(bf16[4,16,641]{2,1,0:T(8,128)(2,1)S(1)} %rev.7), channel_id=1, source_target_pairs={{4,0},{5,1},{6,2},{7,3},{0,4},{1,5},{2,6},{3,7},{12,8},{13,9},{14,... | collective-permute-start | bytes 246152 | tf_op jit(solution)/shard_map/ppermute | solution.py:30
  12.3 4.9 %collective-permute-start.3 = (bf16[4,16,641]{2,1,0:T(8,128)(2,1)S(1)}, bf16[4,16,641]{2,1,0:T(8,128)(2,1)S(1)}, u32[]{:S(2)}, u32[]{:S(2)}) collective-permute-start(bf16[4,16,641]{2,1,0:T(8,128)(2,1)S(1)} %get-tuple-element.60), channel_id=1, source_target_pairs={{8,0},{16,8},{24,16},{9,1},{17,9},{25,17},{10,2},{18,10},{26,18},{... | collective-permute-start | bytes 246152 | tf_op jit(solution)/shard_map/ppermute | solution.py:20
  13.6 11.7 %collective-permute-start.1 = (bf16[4,16,641]{2,1,0:T(8,128)(2,1)S(1)}, bf16[4,16,641]{2,1,0:T(8,128)(2,1)S(1)}, u32[]{:S(2)}, u32[]{:S(2)}) collective-permute-start(bf16[4,16,641]{2,1,0:T(8,128)(2,1)S(1)} %get-tuple-element.61), channel_id=1, source_target_pairs={{0,8},{8,16},{16,24},{1,9},{9,17},{17,25},{2,10},{10,18},{18,26},{... | collective-permute-start | bytes 246152 | tf_op jit(solution)/shard_map/ppermute | solution.py:18
  16.7 8.7 %collective-permute-start = (bf16[4,16,641]{2,1,0:T(8,128)(2,1)S(1)}, bf16[4,16,641]{2,1,0:T(8,128)(2,1)S(1)}, u32[]{:S(2)}, u32[]{:S(2)}) collective-permute-start(bf16[4,16,641]{2,1,0:T(8,128)(2,1)S(1)} %rev.6), channel_id=1, source_target_pairs={{4,0},{5,1},{6,2},{7,3},{0,4},{1,5},{2,6},{3,7},{12,8},{13,9},{14,... | collective-permute-start | bytes 246152 | tf_op jit(solution)/shard_map/ppermute | solution.py:30
  26.5 30.2 %collective-permute-start.4 = (bf16[24,16,641]{2,1,0:T(8,128)(2,1)S(1)}, bf16[24,16,641]{2,1,0:T(8,128)(2,1)S(1)}, u32[]{:S(2)}, u32[]{:S(2)}) collective-permute-start(bf16[24,16,641]{2,1,0:T(8,128)(2,1)S(1)} %pad_maximum_fusion.1), channel_id=1, source_target_pairs={{0,1},{1,2},{2,3},{3,4},{4,5},{5,6},{6,7},{7,0},{8,9},{9,10},{10,1... | collective-permute-start | bytes 1476872 | tf_op jit(solution)/shard_map/ppermute | solution.py:18
  28.0 30.9 %collective-permute-start.5 = (bf16[24,16,641]{2,1,0:T(8,128)(2,1)S(1)}, bf16[24,16,641]{2,1,0:T(8,128)(2,1)}, u32[]{:S(2)}, u32[]{:S(2)}) collective-permute-start(bf16[24,16,641]{2,1,0:T(8,128)(2,1)S(1)} %pad_maximum_fusion.1), channel_id=1, source_target_pairs={{1,0},{2,1},{3,2},{4,3},{5,4},{6,5},{7,6},{0,7},{9,8},{10,9},{11,1... | collective-permute-start | bytes 1476872 | tf_op jit(solution)/shard_map/ppermute | solution.py:20
  60.2 63.4 %copy-start.1 = (f32[512]{0:T(512)S(1)}, f32[512]{0:T(512)}, u32[]{:S(2)}) copy-start(f32[512]{0:T(512)} %param.11) | copy-start | bytes 6148
Sparse Core Ops, SparseCore 0:
  10.2 86.7 all-gather.1
where the time goes:
time: 139 us; the launch traced here: 138 us
  waiting for transfers between devices  35.1 us (25%)
  matrix products  30.9 us (22%)
  loops' own time  30.7 us (22%)
  between operations  13.5 us (10%)
  starting transfers between devices  13.3 us (10%)
  local copies, waits for them, and re-layouts  10.7 us (8%)
  other arithmetic  4.22 us (3%)
    another operation x1, loops' own time, body(): features = lax.map(one_row, (per_row, jnp.arange(lat_dev, dtype=jnp.int32)))  30.7 us
    ppermute x2, waiting for transfers between devices, padded(): lax.ppermute(tail, axis, [(i, (i + 1) % count) for i in range(ends)])  23.5 us
    dot_general x16, matrix products, one_row(): jnp.einsum('kjdp,dpc->kjc', banded_matrix, slab_rows, preferred_element_t...  16.8 us
    dynamic_slice x16, local copies, waits for them, and re-layouts, body(): features = lax.map(one_row, (per_row, jnp.arange(lat_dev, dtype=jnp.int32)))  9.67 us
    ppermute x2, waiting for transfers between devices, passed_along(): return lax.ppermute(block, axis, route)  8.56 us
    dot_general x1, matrix products, body(): lax.dot_general(features, lax.all_gather(mix_weight, ('lat', 'lon'), axis...  7.88 us
    dot_general x16, matrix products, one_row(): jnp.einsum('blw,ocw->bolc', row_coefficient, basis_selector, preferred_el...  6.16 us
    ppermute x2, starting transfers between devices, padded(): lax.ppermute(tail, axis, [(i, (i + 1) % count) for i in range(ends)])  4.61 us
  transfers between devices with their start and end apart: 7, of which 4 were waited for; matrix products, arithmetic and copies ran while one was open for 27% of the time, Pallas kernels for 0%

commit v1 on v0

v1 whole, which is shorter than its diff:
```python
import functools

import jax
import jax.numpy as jnp
from jax import lax
from jax.experimental import pallas as pl
from jax.experimental.pallas import tpu as pltpu
from jax.sharding import PartitionSpec as P

AXES = ("lat", "lon")
LANES = 128
VMEM_BYTES = 48 * 1024 * 1024


def whole(count):
    return [pl.BlockSpec(memory_space=pltpu.VMEM)] * count


def call(kernel, outs, scratch, cost, *args):
    return pl.pallas_call(
        kernel,
        out_shape=outs,
        in_specs=whole(len(args)),
        out_specs=jax.tree.map(lambda _: pl.BlockSpec(memory_space=pltpu.VMEM), outs),
        scratch_shapes=scratch,
        compiler_params=pltpu.CompilerParams(vmem_limit_bytes=VMEM_BYTES),
        cost_estimate=pl.CostEstimate(flops=cost, bytes_accessed=2_000_000, transcendentals=0),
    )(*args)


def shape(dims, dtype=jnp.bfloat16):
    return jax.ShapeDtypeStruct(dims, dtype)


def route(move):
    lats, lons = lax.axis_size("lat"), lax.axis_size("lon")
    pairs = []
    for lat in range(lats):
        for lon in range(lons):
            to_lat, to_lon = move(lat, lon, lats, lons)
            pairs.append((lat * lons + lon, to_lat * lons + to_lon))
    return pairs


def swap(block, lat_bits, lon_bits):
    return lax.ppermute(
        block, AXES, route(lambda lat, lon, lats, lons: (lat ^ lat_bits, lon ^ lon_bits))
    )


def outer_move(lat, lon, lats, lons):
    if lat == 0 or lat == lats - 1:
        return lat, (lon + lons // 2) % lons
    return (lat - 1 if lat % 2 == 0 else lat + 1), lon


def along_move(lat, lon, lats, lons):
    return lat, (lon + 2 if lon % 2 else lon - 2) % lons


def across_move(lat, lon, lats, lons):
    return lat, (lon + 1 if lon % 2 else lon - 1) % lons


def halves_of(value, half, rest):
    low = value[..., :half]
    high = value[..., half:]
    pad = jnp.zeros(value.shape[:-1] + (2 * half - value.shape[-1],), value.dtype)
    return low, jnp.concatenate([high, pad], axis=-1) if rest else high


def split_kernel(half, w_ref, mine_ref, other_ref, pad_ref):
    odd = lax.axis_index("lon") % 2
    filled = w_ref.shape[2] - half
    pad_ref[...] = jnp.zeros_like(pad_ref)
    pad_ref[:, :, :filled] = w_ref[:, :, half:]
    low, high = w_ref[:, :, :half], pad_ref[...]
    mine_ref[...] = jnp.where(odd == 1, high, low)
    other_ref[...] = jnp.where(odd == 1, low, high)


def strip_kernel(half, x_ref, outer_ref, inner_ref, mine_ref, other_ref, rows_ref):
    lat, lon = lax.axis_index("lat"), lax.axis_index("lon")
    pole = (lat == 0) | (lat == lax.axis_size("lat") - 1)
    radius, rows = outer_ref.shape[0], x_ref.shape[0]
    channels = x_ref.shape[2]
    rows_ref[:, :, 2 * half - LANES :] = jnp.zeros_like(rows_ref[:, :, 2 * half - LANES :])
    rows_ref[radius : radius + rows, :, :channels] = x_ref[...]
    at_outer = jnp.where(lat % 2 == 0, 0, radius + rows)
    at_inner = jnp.where(lat % 2 == 0, radius + rows, 0)
    for r in range(radius):
        from_row = jnp.where(pole, radius - 1 - r, r)
        rows_ref[at_outer + r, :, :channels] = outer_ref[from_row]
        rows_ref[at_inner + r, :, :channels] = inner_ref[r]
    low, high = rows_ref[:, :, :half], rows_ref[:, :, half:]
    mine_ref[...] = jnp.where(lon % 2 == 1, high, low)
    other_ref[...] = jnp.where(lon % 2 == 1, low, high)


def band_kernel(reach, f_ref, w_ref, band_ref, row_ref):
    bases, span, rows, taps = f_ref.shape
    columns = band_ref.shape[1] // bases
    pitch = columns + taps - 1
    wide = band_ref.shape[2]
    offset = jnp.abs(lax.broadcasted_iota(jnp.int32, (rows, taps), 1) - reach)
    row_ref[...] = jnp.zeros_like(row_ref)
    for d in range(span):
        inside = offset <= w_ref[:, d : d + 1]
        for k in range(bases):
            tap = jnp.where(inside, f_ref[k, d].astype(jnp.float32), 0.0)
            row_ref[k, :, d * pitch : d * pitch + taps] = tap

    def one_row(i, _):
        for k in range(bases):
            same = jnp.broadcast_to(row_ref[k, pl.ds(i, 1), :], (columns, wide))
            band = pltpu.roll(same, 0, 1, stride=1, stride_axis=0)
            band_ref[i, k * columns : (k + 1) * columns, :] = band.astype(jnp.bfloat16)
        return 0

    lax.fori_loop(0, rows, one_row, 0)


def feature_kernel(span, band_ref, mine_ref, pair_ref, along_ref, across_ref, out_ref, slab_ref):
    odd = lax.axis_index("lon") % 2
    slab_ref[:, 1 + odd] = mine_ref[...]
    slab_ref[:, 2 - odd] = pair_ref[...]
    slab_ref[:, 3 * (1 - odd)] = along_ref[...]
    slab_ref[:, 3 * odd] = across_ref[...]
    bases, strips, rows, columns, half = out_ref.shape
    depth = span * 3 * columns

    def one_row(i, _):
        band = band_ref[i][:, :depth]
        for strip in range(strips):
            source = slab_ref[pl.ds(i, span), strip : strip + 3].reshape(depth, half)
            summed = jnp.dot(band, source, preferred_element_type=jnp.float32)
            out_ref[:, strip, i] = summed.astype(jnp.bfloat16).reshape(bases, columns, half)
        return 0

    lax.fori_loop(0, rows, one_row, 0)


def mix_kernel(masks, *refs):
    feature_ref, block_refs = refs[0], refs[1 : 1 + 2 * masks]
    keep_ref, send_ref, weight_ref = refs[1 + 2 * masks :]
    lat, lon = lax.axis_index("lat"), lax.axis_index("lon")
    odd = lon % 2
    bases, strips, points, half = feature_ref.shape
    for core in range(2):
        for mask in range(masks):
            place = (lat % 2 ^ core) * masks + ((lon // 2) ^ mask)
            weight_ref[:, place] = block_refs[core * masks + mask][...]
    wide = keep_ref.shape[1]

    def strip_sum(strip):
        total = jnp.zeros((points, wide), jnp.float32)
        for k in range(bases):
            total += lax.dot_general(
                feature_ref[k, strip],
                weight_ref[k].reshape(wide, half),
                (((1,), (1,)), ((), ())),
                preferred_element_type=jnp.float32,
            )
        return total

    send_ref[...] = strip_sum(1 - odd).astype(send_ref.dtype)
    keep_ref[...] = strip_sum(odd)


def body(latent, filters, widths, mix_weight, mix_bias):
    lats, lons = lax.axis_size("lat"), lax.axis_size("lon")
    lat, lon = lax.axis_index("lat"), lax.axis_index("lon")
    rows, columns, channels = latent.shape
    bases, _, span, taps = filters.shape
    radius, reach = span // 2, taps // 2
    assert reach == columns and lats % 2 == 0 and lons % 2 == 0
    half = -(-channels // (2 * LANES)) * LANES
    out_columns = mix_bias.shape[0]
    share = mix_weight.shape[2]

    even = lat % 2 == 0
    outer = lax.ppermute(
        jnp.where(even, latent[:radius], latent[-radius:]), AXES, route(outer_move)
    )
    inner = swap(jnp.where(even, latent[-radius:], latent[:radius]), 1, 0)

    weight = jnp.transpose(mix_weight, (0, 2, 1))
    halves = shape((bases, share, half))
    own_weight, pair_weight = call(
        functools.partial(split_kernel, half),
        (halves, halves),
        [pltpu.VMEM((bases, share, half), jnp.bfloat16)],
        100_000,
        weight,
    )
    got_weight = swap(pair_weight, 0, 1)
    odd = lon % 2 == 1
    first = jnp.concatenate(
        [jnp.where(odd, got_weight, own_weight), jnp.where(odd, own_weight, got_weight)], axis=1
    )

    strip = shape((rows + 2 * radius, columns, half))
    mine, other = call(
        functools.partial(strip_kernel, half),
        (strip, strip),
        [pltpu.VMEM((rows + 2 * radius, columns, 2 * half), jnp.bfloat16)],
        100_000,
        latent,
        outer,
        inner,
    )
    pair_strip = swap(other, 0, 1)
    along = lax.ppermute(mine, AXES, route(along_move))
    across = lax.ppermute(other, AXES, route(across_move))

    lon_masks, lat_masks = lons // 2, lats // 2
    blocks = {(0, 0): first}
    bit = lon_masks // 2
    while bit:
        for low, mask in list(blocks):
            blocks[low, mask ^ bit] = swap(blocks[low, mask], 0, 2 * bit)
        bit //= 2
    bit = 1
    while bit < lat_masks:
        for low, mask in list(blocks):
            blocks[low ^ bit, mask] = swap(blocks[low, mask], 2 * bit, 0)
        bit *= 2
    crossed = {key: swap(block, 1, 0) for key, block in blocks.items()}

    depth = span * (columns + taps - 1)
    deep = -(-depth // LANES) * LANES
    band = call(
        functools.partial(band_kernel, reach),
        shape((rows, bases * columns, deep)),
        [pltpu.VMEM((bases, rows, deep), jnp.float32)],
        1_000_000_000,
        jnp.transpose(filters, (0, 2, 1, 3)),
        widths,
    )
    features = call(
        functools.partial(feature_kernel, span),
        shape((bases, 2, rows, columns, half)),
        [pltpu.VMEM((rows + 2 * radius, 4, columns, half), jnp.bfloat16)],
        4_000_000_000,
        band,
        mine,
        pair_strip,
        along,
        across,
    ).reshape(bases, 2, rows * columns, half)

    width = out_columns // lat_masks
    pieces = []
    for low in range(lat_masks):
        operands = [blocks[low, mask] for mask in range(lon_masks)]
        operands += [crossed[low, mask] for mask in range(lon_masks)]
        keep, send = call(
            functools.partial(mix_kernel, lon_masks),
            (shape((rows * columns, width), jnp.float32), shape((rows * columns, width))),
            [pltpu.VMEM((bases, 2 * lon_masks, 2 * share, half), jnp.bfloat16)],
            2_000_000_000,
            features,
            *operands,
        )
        pieces.append(keep + swap(send, 0, 1).astype(jnp.float32))
    mixed = jnp.stack(pieces, 1)
    order = jnp.arange(lat_masks) ^ (lat // 2)
    if lat_masks == 2:
        mixed = jnp.where(lat // 2 == 0, mixed, mixed[:, ::-1])
    else:
        mixed = jnp.take(mixed, order, axis=1)
    mixed = mixed.reshape(rows, columns, out_columns) + mix_bias
    return jax.nn.gelu(mixed, approximate=False).astype(jnp.bfloat16)


def solution(mesh):
    placed = (
        P("lat", "lon", None),
        P(None, "lat", None, None),
        P("lat", None),
        P(None, None, ("lat", "lon")),
        P(),
    )
    return jax.shard_map(
        body, mesh=mesh, in_specs=placed, out_specs=P("lat", "lon", None), check_vma=False
    )
```

time: 139 us -> 77.5 us (0.56)
  matrix products: 30.9 us -> 0 us
  loops' own time: 30.7 us -> 0 us
  between operations: 13.5 us -> 0.2 us
  Pallas kernels: 0 us -> 13.2 us
  starting transfers between devices: 13.3 us -> 22.7 us
  local copies, waits for them, and re-layouts: 10.7 us -> 6.44 us
  waiting for transfers between devices: 35.1 us -> 31.7 us
    dot_general x33 -> x0, matrix products: 30.9 us -> none  [the longest x16 16.8 us: one_row(): jnp.einsum('kjdp,dpc->kjc', banded_matrix, slab_rows, preferred_element_t...]
    another operation x1 -> x0, loops' own time: 30.7 us -> none  [body(): features = lax.map(one_row, (per_row, jnp.arange(lat_dev, dtype=jnp.int32)))]
    pallas_call x0 -> x6, Pallas kernels: none -> 13.2 us  [call(): pl.pallas_call(kernel, out_shape=outs, in_specs=whole(len(args)), out_spe...]
    dynamic_slice x16 -> x0, local copies, waits for them, and re-layouts: 9.67 us -> none  [body(): features = lax.map(one_row, (per_row, jnp.arange(lat_dev, dtype=jnp.int32)))]
    ppermute x6 -> x23, starting transfers between devices: 13.3 us -> 22.7 us  [the longest x20 14.8 us: swap(): lax.ppermute(block, AXES, route(lambda lat, lon, lats, lons: (lat ^ lat_b...]
    unnamed x4 -> x12, local copies, waits for them, and re-layouts: 0.01 us -> 5.61 us
    ppermute x6 -> x23, waiting for transfers between devices: 34.4 us -> 31.7 us  [the longest x20 20.6 us: swap(): lax.ppermute(block, AXES, route(lambda lat, lon, lats, lons: (lat ^ lat_b...]
    concatenate x2 -> x1, other arithmetic: 2.32 us -> 0.03 us  [body(): jnp.concatenate([jnp.where(odd, got_weight, own_weight), jnp.where(odd, o...]
  transfers between devices with their start and end apart: 7 -> 23, of which waited for: 4 -> 8; matrix products, arithmetic and copies ran while one was open for 27% -> 1% of each run, Pallas kernels for 0% -> 17%
where the time goes in v1:
time: 77.5 us; the launch traced here: 77.2 us
  waiting for transfers between devices  31.7 us (41%)
  starting transfers between devices  22.7 us (29%)
  Pallas kernels  13.2 us (17%)
  local copies, waits for them, and re-layouts  6.44 us (8%)
  other arithmetic  3 us (4%)
    ppermute x20, waiting for transfers between devices, swap(): lax.ppermute(block, AXES, route(lambda lat, lon, lats, lons: (lat ^ lat_b...  20.6 us
    ppermute x20, starting transfers between devices, swap(): lax.ppermute(block, AXES, route(lambda lat, lon, lats, lons: (lat ^ lat_b...  14.8 us
    pallas_call x6, Pallas kernels, call(): pl.pallas_call(kernel, out_shape=outs, in_specs=whole(len(args)), out_spe...  13.2 us
    ppermute x1, waiting for transfers between devices, body(): lax.ppermute(jnp.where(even, latent[:radius], latent[-radius:]), AXES, ro...  7.38 us
    ppermute x1, starting transfers between devices, body(): along = lax.ppermute(mine, AXES, route(along_move))  6.14 us
    unnamed x12, local copies, waits for them, and re-layouts  5.61 us
    ppermute x1, waiting for transfers between devices, body(): across = lax.ppermute(other, AXES, route(across_move))  3.71 us
    convert_element_type x1, other arithmetic, body(): return jax.nn.gelu(mixed, approximate=False).astype(jnp.bfloat16)  1.86 us
  transfers between devices with their start and end apart: 23, of which 8 were waited for; matrix products, arithmetic and copies ran while one was open for 1% of the time, Pallas kernels for 17%

profile of v1, /device:TPU:0, one launch (start us, length us, event | category | flops | bytes accessed | tf_op | source)
XLA Modules:
  0.0 77.2 jit_solution(16162875327167000229)
XLA Ops:
  0.0 0.9 %copy-done.1 = bf16[9,641,16]{1,2,0:T(8,128)(2,1)S(1)} copy-done((bf16[9,641,16]{1,2,0:T(8,128)(2,1)S(1)}, bf16[9,641,16]{1,2,0:T(8,128)(2,1)}, u32[]{:S(2)}) %copy-start.1) | copy-done | bytes 184632
  1.0 3.0 %collective-permute-start.5 = (bf16[9,16,384]{2,1,0:T(8,128)(2,1)S(1)}, bf16[9,16,384]{2,1,0:T(8,128)(2,1)S(1)}, u32[]{:S(2)}, u32[]{:S(2)}) collective-permute-start(bf16[9,16,384]{2,1,0:T(8,128)(2,1)S(1)} %get-tuple-element.15), channel_id=1, source_target_pairs={{0,1},{1,0},{2,3},{3,2},{4,5},{5,4},{6,7},{7,6},{8,9},{9,8},{10,11... | collective-permute-start | bytes 331784 | tf_op jit(solution)/shard_map/ppermute | solution.py:46
  4.0 3.1 %collective-permute-done.5 = bf16[9,16,384]{2,1,0:T(8,128)(2,1)S(1)} collective-permute-done((bf16[9,16,384]{2,1,0:T(8,128)(2,1)S(1)}, bf16[9,16,384]{2,1,0:T(8,128)(2,1)S(1)}, u32[]{:S(2)}, u32[]{:S(2)}) %collective-permute-start.5) | collective-permute-done | bytes 110624 | tf_op jit(solution)/shard_map/ppermute | solution.py:46
  7.1 2.9 %collective-permute-start.7 = (bf16[9,32,384]{2,1,0:T(8,128)(2,1)S(1)}, bf16[9,32,384]{2,1,0:T(8,128)(2,1)S(1)}, u32[]{:S(2)}, u32[]{:S(2)}) collective-permute-start(bf16[9,32,384]{2,1,0:T(8,128)(2,1)S(1)} %pad_maximum_fusion.1.refs_1_), channel_id=1, source_target_pairs={{0,4},{1,5},{2,6},{3,7},{4,0},{5,1},{6,2},{7,3},{8,12},{9,13},{10,... | collective-permute-start | bytes 663560 | tf_op jit(solution)/shard_map/ppermute | solution.py:46
  10.0 1.6 %collective-permute-start.6 = (bf16[9,32,384]{2,1,0:T(8,128)(2,1)S(1)}, bf16[9,32,384]{2,1,0:T(8,128)(2,1)S(1)}, u32[]{:S(2)}, u32[]{:S(2)}) collective-permute-start(bf16[9,32,384]{2,1,0:T(8,128)(2,1)S(1)} %pad_maximum_fusion.1.refs_1_), channel_id=1, source_target_pairs={{0,2},{1,3},{2,0},{3,1},{4,6},{5,7},{6,4},{7,5},{8,10},{9,11},{10,... | collective-permute-start | bytes 663560 | tf_op jit(solution)/shard_map/ppermute | solution.py:46
  11.6 1.0 %broadcast_select_fusion.2 = (bf16[4,16,641]{2,1,0:T(8,128)(2,1)S(1)}, bf16[4,16,641]{2,1,0:T(8,128)(2,1)S(1)}) fusion(pred[]{:T(512)S(6)} %eq.13, bf16[16,16,641]{2,1,0:T(8,128)(2,1)} %x_ref.1), kind=kLoop, calls=%fused_computation.26 | loop fusion | flops 82048 | bytes 328193 | tf_op jit(solution)/shard_map/jit(_where)/select_n | solution.py:185
  13.0 1.3 %collective-permute-start.1 = (bf16[4,16,641]{2,1,0:T(8,128)(2,1)S(1)}, bf16[4,16,641]{2,1,0:T(8,128)(2,1)S(1)}, u32[]{:S(2)}, u32[]{:S(2)}) collective-permute-start(bf16[4,16,641]{2,1,0:T(8,128)(2,1)S(1)} %get-tuple-element.21), channel_id=1, source_target_pairs={{0,8},{1,9},{2,10},{3,11},{4,12},{5,13},{6,14},{7,15},{8,0},{9,1},... | collective-permute-start | bytes 246152 | tf_op jit(solution)/shard_map/ppermute | solution.py:46
  14.2 7.4 %collective-permute-done.outer_ref = bf16[4,16,641]{2,1,0:T(8,128)(2,1)S(1)} collective-permute-done((bf16[4,16,641]{2,1,0:T(8,128)(2,1)S(1)}, bf16[4,16,641]{2,1,0:T(8,128)(2,1)S(1)}, u32[]{:S(2)}, u32[]{:S(2)}) %collective-permute-start) | collective-permute-done | bytes 82080 | tf_op jit(solution)/shard_map/ppermute | solution.py:182
  21.6 1.0 %copy-done = bf16[16,16,641]{2,1,0:T(8,128)(2,1)S(1)} copy-done((bf16[16,16,641]{2,1,0:T(8,128)(2,1)S(1)}, bf16[16,16,641]{2,1,0:T(8,128)(2,1)}, u32[]{:S(2)}) %copy-start) | copy-done | bytes 328216
  22.7 0.5 collective-permute-start.2
  23.2 6.1 %collective-permute-start.3 = (bf16[24,16,384]{2,1,0:T(8,128)(2,1)S(1)}, bf16[24,16,384]{2,1,0:T(8,128)(2,1)S(1)}, u32[]{:S(2)}, u32[]{:S(2)}) collective-permute-start(bf16[24,16,384]{2,1,0:T(8,128)(2,1)S(1)} %get-tuple-element.13.mine_ref), channel_id=1, source_target_pairs={{0,6},{1,3},{2,0},{3,5},{4,2},{5,7},{6,4},{7,1},{8,14},{9,11},{10,... | collective-permute-start | bytes 884744 | tf_op jit(solution)/shard_map/ppermute | solution.py:213
  29.4 1.4 %collective-permute-start.4 = (bf16[24,16,384]{2,1,0:T(8,128)(2,1)S(1)}, bf16[24,16,384]{2,1,0:T(8,128)(2,1)S(1)}, u32[]{:S(2)}, u32[]{:S(2)}) collective-permute-start(bf16[24,16,384]{2,1,0:T(8,128)(2,1)S(1)} %get-tuple-element.14), channel_id=1, source_target_pairs={{0,7},{1,2},{2,1},{3,4},{4,3},{5,6},{6,5},{7,0},{8,15},{9,10},{10,... | collective-permute-start | bytes 884744 | tf_op jit(solution)/shard_map/ppermute | solution.py:214
  30.9 5.8 %collective-permute-done.14.refs_1_ = bf16[9,32,384]{2,1,0:T(8,128)(2,1)S(1)} collective-permute-done((bf16[9,32,384]{2,1,0:T(8,128)(2,1)S(1)}, bf16[9,32,384]{2,1,0:T(8,128)(2,1)S(1)}, u32[]{:S(2)}, u32[]{:S(2)}) %collective-permute-start.14) | collective-permute-done | bytes 221216 | tf_op jit(solution)/shard_map/ppermute | solution.py:46
  36.7 0.5 collective-permute-start.11
  37.4 3.7 %collective-permute-done.4.across_ref = bf16[24,16,384]{2,1,0:T(8,128)(2,1)S(1)} collective-permute-done((bf16[24,16,384]{2,1,0:T(8,128)(2,1)S(1)}, bf16[24,16,384]{2,1,0:T(8,128)(2,1)S(1)}, u32[]{:S(2)}, u32[]{:S(2)}) %collective-permute-start.4) | collective-permute-done | bytes 294944 | tf_op jit(solution)/shard_map/ppermute | solution.py:214
  41.1 2.0 %collective-permute-start.17 = (bf16[9,32,384]{2,1,0:T(8,128)(2,1)S(1)}, bf16[9,32,384]{2,1,0:T(8,128)(2,1)S(1)}, u32[]{:S(2)}, u32[]{:S(2)}) collective-permute-start(bf16[9,32,384]{2,1,0:T(8,128)(2,1)S(1)} %collective-permute-done.8.refs_4_), channel_id=1, source_target_pairs={{0,16},{1,17},{2,18},{3,19},{4,20},{5,21},{6,22},{7,23},{8,24},{9,... | collective-permute-start | bytes 663560 | tf_op jit(solution)/shard_map/ppermute | solution.py:46
  43.1 1.0 %copy-done.2 = bf16[9,16,9,33]{3,1,2,0:T(8,128)(2,1)S(1)} copy-done((bf16[9,16,9,33]{3,1,2,0:T(8,128)(2,1)S(1)}, bf16[9,16,9,33]{3,1,2,0:T(8,128)(2,1)}, u32[]{:S(2)}) %copy-start.2) | copy-done | bytes 85560
  44.1 0.7 copy-done.3
  44.8 2.0 %shard_map.55.band_ref = bf16[16,144,512]{2,1,0:T(8,128)(2,1)S(1)} custom-call(bf16[9,9,16,33]{3,2,1,0:T(8,128)(2,1)S(1)} %bitcast.8, s32[16,9]{1,0:T(8,128)S(1)} %copy-done.3), custom_call_target="tpu_custom_call" | custom-call | flops 1000000000 | bytes 2000000 | tf_op jit(solution)/shard_map/pallas_call | solution.py:20
  46.9 0.5 collective-permute-start.12
  47.4 2.8 %collective-permute-done.16.refs_3_ = bf16[9,32,384]{2,1,0:T(8,128)(2,1)S(1)} collective-permute-done((bf16[9,32,384]{2,1,0:T(8,128)(2,1)S(1)}, bf16[9,32,384]{2,1,0:T(8,128)(2,1)S(1)}, u32[]{:S(2)}, u32[]{:S(2)}) %collective-permute-start.16) | collective-permute-done | bytes 221216 | tf_op jit(solution)/shard_map/ppermute | solution.py:46
  50.3 3.9 %collective-permute-done.17.refs_4_ = bf16[9,32,384]{2,1,0:T(8,128)(2,1)S(1)} collective-permute-done((bf16[9,32,384]{2,1,0:T(8,128)(2,1)S(1)}, bf16[9,32,384]{2,1,0:T(8,128)(2,1)S(1)}, u32[]{:S(2)}, u32[]{:S(2)}) %collective-permute-start.17) | collective-permute-done | bytes 221216 | tf_op jit(solution)/shard_map/ppermute | solution.py:46
  54.1 6.9 %shard_map.57 = bf16[9,2,16,16,384]{4,3,2,1,0:T(8,128)(2,1)} custom-call(bf16[16,144,512]{2,1,0:T(8,128)(2,1)S(1)} %shard_map.55.band_ref, bf16[24,16,384]{2,1,0:T(8,128)(2,1)S(1)} %get-tuple-element.13.mine_ref, bf16[24,16,384]{2,1,0:T(8,128)(2,1)S(1)} %collective-permute-done.2.pair_ref, bf16[24,16,384]{2,1,0:T(8,128)(2,1)S(1)} %collective-permute-done.3.along_ref, ...), custom_call_target="tpu_custom_call" | custom-call | flops 4000000000 | bytes 2000000 | tf_op jit(solution)/shard_map/pallas_call | solution.py:20
  61.0 2.0 %copy-done.4 = bf16[9,2,16,16,384]{4,3,2,1,0:T(8,128)(2,1)S(1)} copy-done((bf16[9,2,16,16,384]{4,3,2,1,0:T(8,128)(2,1)S(1)}, bf16[9,2,16,16,384]{4,3,2,1,0:T(8,128)(2,1)}, u32[]{:S(2)}) %copy-start.4) | copy-done | bytes 3538968
  63.0 2.5 %shard_map.59 = (f32[256,256]{1,0:T(8,128)S(1)}, bf16[256,256]{1,0:T(8,128)(2,1)S(1)}) custom-call(bf16[9,2,256,384]{3,2,1,0:T(8,128)(2,1)S(1)} %bitcast.9, bf16[9,32,384]{2,1,0:T(8,128)(2,1)S(1)} %pad_maximum_fusion.1.refs_1_, bf16[9,32,384]{2,1,0:T(8,128)(2,1)S(1)} %collective-permute-done.6.refs_2_, ...), custom_call_target="tpu_custom_call" | custom-call | flops 2000000000 | bytes 2000000 | tf_op jit(solution)/shard_map/pallas_call | solution.py:20
  65.7 1.6 %shard_map.60 = (f32[256,256]{1,0:T(8,128)S(1)}, bf16[256,256]{1,0:T(8,128)(2,1)S(1)}) custom-call(bf16[9,2,256,384]{3,2,1,0:T(8,128)(2,1)S(1)} %bitcast.10, bf16[9,32,384]{2,1,0:T(8,128)(2,1)S(1)} %collective-permute-done.14.refs_1_, bf16[9,32,384]{2,1,0:T(8,128)(2,1)S(1)} %collective-permute-done.15.refs_2_, ...), custom_call_target="tpu_custom_call" | custom-call | flops 2000000000 | bytes 2000000 | tf_op jit(solution)/shard_map/pallas_call | solution.py:20
  67.3 2.1 %collective-permute-start.22 = (bf16[256,256]{1,0:T(8,128)(2,1)S(1)}, bf16[256,256]{1,0:T(8,128)(2,1)S(1)}, u32[]{:S(2)}, u32[]{:S(2)}) collective-permute-start(bf16[256,256]{1,0:T(8,128)(2,1)S(1)} %get-tuple-element.20), channel_id=1, source_target_pairs={{0,1},{1,0},{2,3},{3,2},{4,5},{5,4},{6,7},{7,6},{8,9},{9,8},{10,11... | collective-permute-start | bytes 393224 | tf_op jit(solution)/shard_map/ppermute | solution.py:46
  69.3 2.6 %collective-permute-done.13 = bf16[256,256]{1,0:T(8,128)(2,1)S(1)} collective-permute-done((bf16[256,256]{1,0:T(8,128)(2,1)S(1)}, bf16[256,256]{1,0:T(8,128)(2,1)S(1)}, u32[]{:S(2)}, u32[]{:S(2)}) %collective-permute-start.13) | collective-permute-done | bytes 131104 | tf_op jit(solution)/shard_map/ppermute | solution.py:46
  72.0 2.4 %collective-permute-done.22 = bf16[256,256]{1,0:T(8,128)(2,1)S(1)} collective-permute-done((bf16[256,256]{1,0:T(8,128)(2,1)S(1)}, bf16[256,256]{1,0:T(8,128)(2,1)S(1)}, u32[]{:S(2)}, u32[]{:S(2)}) %collective-permute-start.22) | collective-permute-done | bytes 131104 | tf_op jit(solution)/shard_map/ppermute | solution.py:46
  74.5 0.4 copy.6
  74.9 0.4 reshape.8
  75.3 1.9 %fusion.2 = bf16[16,16,512]{2,1,0:T(8,128)(2,1)} fusion(f32[16,16,512]{2,1,0:T(8,128)S(1)} %reshape.8, f32[512]{0:T(512)S(1)} %copy-done.5), kind=kLoop, calls=%fused_computation.4 | loop fusion | flops 8650752 | bytes 788480 | tf_op jit(solution)/shard_map/convert_element_type | solution.py:273
  (42 shorter events, 1.2 us)
Async XLA Ops:
  0.0 0.9 %copy-start.1 = (bf16[9,641,16]{1,2,0:T(8,128)(2,1)S(1)}, bf16[9,641,16]{1,2,0:T(8,128)(2,1)}, u32[]{:S(2)}) copy-start(bf16[9,641,16]{1,2,0:T(8,128)(2,1)} %param.8) | copy-start | bytes 553828
  1.0 6.1 %collective-permute-start.5 = (bf16[9,16,384]{2,1,0:T(8,128)(2,1)S(1)}, bf16[9,16,384]{2,1,0:T(8,128)(2,1)S(1)}, u32[]{:S(2)}, u32[]{:S(2)}) collective-permute-start(bf16[9,16,384]{2,1,0:T(8,128)(2,1)S(1)} %get-tuple-element.15), channel_id=1, source_target_pairs={{0,1},{1,0},{2,3},{3,2},{4,5},{5,4},{6,7},{7,6},{8,9},{9,8},{10,11... | collective-permute-start | bytes 331784 | tf_op jit(solution)/shard_map/ppermute | solution.py:46
  7.1 22.2 %collective-permute-start.7 = (bf16[9,32,384]{2,1,0:T(8,128)(2,1)S(1)}, bf16[9,32,384]{2,1,0:T(8,128)(2,1)S(1)}, u32[]{:S(2)}, u32[]{:S(2)}) collective-permute-start(bf16[9,32,384]{2,1,0:T(8,128)(2,1)S(1)} %pad_maximum_fusion.1.refs_1_), channel_id=1, source_target_pairs={{0,4},{1,5},{2,6},{3,7},{4,0},{5,1},{6,2},{7,3},{8,12},{9,13},{10,... | collective-permute-start | bytes 663560 | tf_op jit(solution)/shard_map/ppermute | solution.py:46
  10.0 20.8 %collective-permute-start.6 = (bf16[9,32,384]{2,1,0:T(8,128)(2,1)S(1)}, bf16[9,32,384]{2,1,0:T(8,128)(2,1)S(1)}, u32[]{:S(2)}, u32[]{:S(2)}) collective-permute-start(bf16[9,32,384]{2,1,0:T(8,128)(2,1)S(1)} %pad_maximum_fusion.1.refs_1_), channel_id=1, source_target_pairs={{0,2},{1,3},{2,0},{3,1},{4,6},{5,7},{6,4},{7,5},{8,10},{9,11},{10,... | collective-permute-start | bytes 663560 | tf_op jit(solution)/shard_map/ppermute | solution.py:46
  11.6 19.2 %collective-permute-start.9 = (bf16[9,32,384]{2,1,0:T(8,128)(2,1)S(1)}, bf16[9,32,384]{2,1,0:T(8,128)(2,1)S(1)}, u32[]{:S(2)}, u32[]{:S(2)}) collective-permute-start(bf16[9,32,384]{2,1,0:T(8,128)(2,1)S(1)} %pad_maximum_fusion.1.refs_1_), channel_id=1, source_target_pairs={{0,8},{1,9},{2,10},{3,11},{4,12},{5,13},{6,14},{7,15},{8,0},{9,1},... | collective-permute-start | bytes 663560 | tf_op jit(solution)/shard_map/ppermute | solution.py:46
  12.5 9.1 %collective-permute-start = (bf16[4,16,641]{2,1,0:T(8,128)(2,1)S(1)}, bf16[4,16,641]{2,1,0:T(8,128)(2,1)S(1)}, u32[]{:S(2)}, u32[]{:S(2)}) collective-permute-start(bf16[4,16,641]{2,1,0:T(8,128)(2,1)S(1)} %get-tuple-element.22), channel_id=1, source_target_pairs={{0,4},{1,5},{2,6},{3,7},{4,0},{5,1},{6,2},{7,3},{8,16},{9,17},{10,... | collective-permute-start | bytes 246152 | tf_op jit(solution)/shard_map/ppermute | solution.py:182
  13.0 8.7 %collective-permute-start.1 = (bf16[4,16,641]{2,1,0:T(8,128)(2,1)S(1)}, bf16[4,16,641]{2,1,0:T(8,128)(2,1)S(1)}, u32[]{:S(2)}, u32[]{:S(2)}) collective-permute-start(bf16[4,16,641]{2,1,0:T(8,128)(2,1)S(1)} %get-tuple-element.21), channel_id=1, source_target_pairs={{0,8},{1,9},{2,10},{3,11},{4,12},{5,13},{6,14},{7,15},{8,0},{9,1},... | collective-permute-start | bytes 246152 | tf_op jit(solution)/shard_map/ppermute | solution.py:46
  21.6 1.0 %copy-start = (bf16[16,16,641]{2,1,0:T(8,128)(2,1)S(1)}, bf16[16,16,641]{2,1,0:T(8,128)(2,1)}, u32[]{:S(2)}) copy-start(bf16[16,16,641]{2,1,0:T(8,128)(2,1)} %x_ref.1) | copy-start | bytes 984580
  22.7 14.0 %collective-permute-start.2 = (bf16[24,16,384]{2,1,0:T(8,128)(2,1)S(1)}, bf16[24,16,384]{2,1,0:T(8,128)(2,1)S(1)}, u32[]{:S(2)}, u32[]{:S(2)}) collective-permute-start(bf16[24,16,384]{2,1,0:T(8,128)(2,1)S(1)} %get-tuple-element.14), channel_id=1, source_target_pairs={{0,1},{1,0},{2,3},{3,2},{4,5},{5,4},{6,7},{7,6},{8,9},{9,8},{10,11... | collective-permute-start | bytes 884744 | tf_op jit(solution)/shard_map/ppermute | solution.py:46
  23.2 14.0 %collective-permute-start.3 = (bf16[24,16,384]{2,1,0:T(8,128)(2,1)S(1)}, bf16[24,16,384]{2,1,0:T(8,128)(2,1)S(1)}, u32[]{:S(2)}, u32[]{:S(2)}) collective-permute-start(bf16[24,16,384]{2,1,0:T(8,128)(2,1)S(1)} %get-tuple-element.13.mine_ref), channel_id=1, source_target_pairs={{0,6},{1,3},{2,0},{3,5},{4,2},{5,7},{6,4},{7,1},{8,14},{9,11},{10,... | collective-permute-start | bytes 884744 | tf_op jit(solution)/shard_map/ppermute | solution.py:213
  29.4 11.7 %collective-permute-start.4 = (bf16[24,16,384]{2,1,0:T(8,128)(2,1)S(1)}, bf16[24,16,384]{2,1,0:T(8,128)(2,1)S(1)}, u32[]{:S(2)}, u32[]{:S(2)}) collective-permute-start(bf16[24,16,384]{2,1,0:T(8,128)(2,1)S(1)} %get-tuple-element.14), channel_id=1, source_target_pairs={{0,7},{1,2},{2,1},{3,4},{4,3},{5,6},{6,5},{7,0},{8,15},{9,10},{10,... | collective-permute-start | bytes 884744 | tf_op jit(solution)/shard_map/ppermute | solution.py:214
  30.8 5.9 %collective-permute-start.14 = (bf16[9,32,384]{2,1,0:T(8,128)(2,1)S(1)}, bf16[9,32,384]{2,1,0:T(8,128)(2,1)S(1)}, u32[]{:S(2)}, u32[]{:S(2)}) collective-permute-start(bf16[9,32,384]{2,1,0:T(8,128)(2,1)S(1)} %pad_maximum_fusion.1.refs_1_), channel_id=1, source_target_pairs={{0,16},{1,17},{2,18},{3,19},{4,20},{5,21},{6,22},{7,23},{8,24},{9,... | collective-permute-start | bytes 663560 | tf_op jit(solution)/shard_map/ppermute | solution.py:46
  30.8 10.3 %collective-permute-start.8 = (bf16[9,32,384]{2,1,0:T(8,128)(2,1)S(1)}, bf16[9,32,384]{2,1,0:T(8,128)(2,1)S(1)}, u32[]{:S(2)}, u32[]{:S(2)}) collective-permute-start(bf16[9,32,384]{2,1,0:T(8,128)(2,1)S(1)} %collective-permute-done.7.refs_3_), channel_id=1, source_target_pairs={{0,2},{1,3},{2,0},{3,1},{4,6},{5,7},{6,4},{7,5},{8,10},{9,11},{10,... | collective-permute-start | bytes 663560 | tf_op jit(solution)/shard_map/ppermute | solution.py:46
  36.7 10.0 %collective-permute-start.10 = (bf16[9,32,384]{2,1,0:T(8,128)(2,1)S(1)}, bf16[9,32,384]{2,1,0:T(8,128)(2,1)S(1)}, u32[]{:S(2)}, u32[]{:S(2)}) collective-permute-start(bf16[9,32,384]{2,1,0:T(8,128)(2,1)S(1)} %collective-permute-done.6.refs_2_), channel_id=1, source_target_pairs={{0,8},{1,9},{2,10},{3,11},{4,12},{5,13},{6,14},{7,15},{8,0},{9,1},... | collective-permute-start | bytes 663560 | tf_op jit(solution)/shard_map/ppermute | solution.py:46
  36.7 10.1 %collective-permute-start.11 = (bf16[9,32,384]{2,1,0:T(8,128)(2,1)S(1)}, bf16[9,32,384]{2,1,0:T(8,128)(2,1)}, u32[]{:S(2)}, u32[]{:S(2)}) collective-permute-start(bf16[9,32,384]{2,1,0:T(8,128)(2,1)S(1)} %collective-permute-done.7.refs_3_), channel_id=1, source_target_pairs={{0,8},{1,9},{2,10},{3,11},{4,12},{5,13},{6,14},{7,15},{8,0},{9,1},... | collective-permute-start | bytes 663560 | tf_op jit(solution)/shard_map/ppermute | solution.py:46
  37.2 10.1 %collective-permute-start.15 = (bf16[9,32,384]{2,1,0:T(8,128)(2,1)S(1)}, bf16[9,32,384]{2,1,0:T(8,128)(2,1)S(1)}, u32[]{:S(2)}, u32[]{:S(2)}) collective-permute-start(bf16[9,32,384]{2,1,0:T(8,128)(2,1)S(1)} %collective-permute-done.6.refs_2_), channel_id=1, source_target_pairs={{0,16},{1,17},{2,18},{3,19},{4,20},{5,21},{6,22},{7,23},{8,24},{9,... | collective-permute-start | bytes 663560 | tf_op jit(solution)/shard_map/ppermute | solution.py:46
  41.1 9.2 %collective-permute-start.16 = (bf16[9,32,384]{2,1,0:T(8,128)(2,1)S(1)}, bf16[9,32,384]{2,1,0:T(8,128)(2,1)S(1)}, u32[]{:S(2)}, u32[]{:S(2)}) collective-permute-start(bf16[9,32,384]{2,1,0:T(8,128)(2,1)S(1)} %collective-permute-done.7.refs_3_), channel_id=1, source_target_pairs={{0,16},{1,17},{2,18},{3,19},{4,20},{5,21},{6,22},{7,23},{8,24},{9,... | collective-permute-start | bytes 663560 | tf_op jit(solution)/shard_map/ppermute | solution.py:46
  41.1 13.1 %collective-permute-start.17 = (bf16[9,32,384]{2,1,0:T(8,128)(2,1)S(1)}, bf16[9,32,384]{2,1,0:T(8,128)(2,1)S(1)}, u32[]{:S(2)}, u32[]{:S(2)}) collective-permute-start(bf16[9,32,384]{2,1,0:T(8,128)(2,1)S(1)} %collective-permute-done.8.refs_4_), channel_id=1, source_target_pairs={{0,16},{1,17},{2,18},{3,19},{4,20},{5,21},{6,22},{7,23},{8,24},{9,... | collective-permute-start | bytes 663560 | tf_op jit(solution)/shard_map/ppermute | solution.py:46
  43.1 1.0 %copy-start.2 = (bf16[9,16,9,33]{3,1,2,0:T(8,128)(2,1)S(1)}, bf16[9,16,9,33]{3,1,2,0:T(8,128)(2,1)}, u32[]{:S(2)}) copy-start(bf16[9,16,9,33]{3,1,2,0:T(8,128)(2,1)} %param.6) | copy-start | bytes 256612
  44.1 0.7 copy-start.3
  46.8 18.9 %collective-permute-start.18 = (bf16[9,32,384]{2,1,0:T(8,128)(2,1)S(1)}, bf16[9,32,384]{2,1,0:T(8,128)(2,1)S(1)}, u32[]{:S(2)}, u32[]{:S(2)}) collective-permute-start(bf16[9,32,384]{2,1,0:T(8,128)(2,1)S(1)} %collective-permute-done.14.refs_1_), channel_id=1, source_target_pairs={{0,8},{1,9},{2,10},{3,11},{4,12},{5,13},{6,14},{7,15},{8,0},{9,1},... | collective-permute-start | bytes 663560 | tf_op jit(solution)/shard_map/ppermute | solution.py:46
  46.9 14.2 %collective-permute-start.12 = (bf16[9,32,384]{2,1,0:T(8,128)(2,1)S(1)}, bf16[9,32,384]{2,1,0:T(8,128)(2,1)S(1)}, u32[]{:S(2)}, u32[]{:S(2)}) collective-permute-start(bf16[9,32,384]{2,1,0:T(8,128)(2,1)S(1)} %collective-permute-done.8.refs_4_), channel_id=1, source_target_pairs={{0,8},{1,9},{2,10},{3,11},{4,12},{5,13},{6,14},{7,15},{8,0},{9,1},... | collective-permute-start | bytes 663560 | tf_op jit(solution)/shard_map/ppermute | solution.py:46
  47.4 18.3 %collective-permute-start.19 = (bf16[9,32,384]{2,1,0:T(8,128)(2,1)S(1)}, bf16[9,32,384]{2,1,0:T(8,128)(2,1)S(1)}, u32[]{:S(2)}, u32[]{:S(2)}) collective-permute-start(bf16[9,32,384]{2,1,0:T(8,128)(2,1)S(1)} %collective-permute-done.15.refs_2_), channel_id=1, source_target_pairs={{0,8},{1,9},{2,10},{3,11},{4,12},{5,13},{6,14},{7,15},{8,0},{9,1},... | collective-permute-start | bytes 663560 | tf_op jit(solution)/shard_map/ppermute | solution.py:46
  50.3 15.4 %collective-permute-start.20 = (bf16[9,32,384]{2,1,0:T(8,128)(2,1)S(1)}, bf16[9,32,384]{2,1,0:T(8,128)(2,1)S(1)}, u32[]{:S(2)}, u32[]{:S(2)}) collective-permute-start(bf16[9,32,384]{2,1,0:T(8,128)(2,1)S(1)} %collective-permute-done.16.refs_3_), channel_id=1, source_target_pairs={{0,8},{1,9},{2,10},{3,11},{4,12},{5,13},{6,14},{7,15},{8,0},{9,1},... | collective-permute-start | bytes 663560 | tf_op jit(solution)/shard_map/ppermute | solution.py:46
  54.1 11.6 %collective-permute-start.21 = (bf16[9,32,384]{2,1,0:T(8,128)(2,1)S(1)}, bf16[9,32,384]{2,1,0:T(8,128)(2,1)S(1)}, u32[]{:S(2)}, u32[]{:S(2)}) collective-permute-start(bf16[9,32,384]{2,1,0:T(8,128)(2,1)S(1)} %collective-permute-done.17.refs_4_), channel_id=1, source_target_pairs={{0,8},{1,9},{2,10},{3,11},{4,12},{5,13},{6,14},{7,15},{8,0},{9,1},... | collective-permute-start | bytes 663560 | tf_op jit(solution)/shard_map/ppermute | solution.py:46
  61.0 2.0 %copy-start.4 = (bf16[9,2,16,16,384]{4,3,2,1,0:T(8,128)(2,1)S(1)}, bf16[9,2,16,16,384]{4,3,2,1,0:T(8,128)(2,1)}, u32[]{:S(2)}) copy-start(bf16[9,2,16,16,384]{4,3,2,1,0:T(8,128)(2,1)} %shard_map.57) | copy-start | bytes 10616836
  65.6 6.4 %collective-permute-start.13 = (bf16[256,256]{1,0:T(8,128)(2,1)S(1)}, bf16[256,256]{1,0:T(8,128)(2,1)S(1)}, u32[]{:S(2)}, u32[]{:S(2)}) collective-permute-start(bf16[256,256]{1,0:T(8,128)(2,1)S(1)} %get-tuple-element.18), channel_id=1, source_target_pairs={{0,1},{1,0},{2,3},{3,2},{4,5},{5,4},{6,7},{7,6},{8,9},{9,8},{10,11... | collective-permute-start | bytes 393224 | tf_op jit(solution)/shard_map/ppermute | solution.py:46
  67.3 8.0 %copy-start.5 = (f32[512]{0:T(512)S(1)}, f32[512]{0:T(512)}, u32[]{:S(2)}) copy-start(f32[512]{0:T(512)} %param.9) | copy-start | bytes 6148
  67.3 7.0 %collective-permute-start.22 = (bf16[256,256]{1,0:T(8,128)(2,1)S(1)}, bf16[256,256]{1,0:T(8,128)(2,1)S(1)}, u32[]{:S(2)}, u32[]{:S(2)}) collective-permute-start(bf16[256,256]{1,0:T(8,128)(2,1)S(1)} %get-tuple-element.20), channel_id=1, source_target_pairs={{0,1},{1,0},{2,3},{3,2},{4,5},{5,4},{6,7},{7,6},{8,9},{9,8},{10,11... | collective-permute-start | bytes 393224 | tf_op jit(solution)/shard_map/ppermute | solution.py:46

commit v2 on v1

v2 whole, which is shorter than its diff:
```python
import functools

import jax
import jax.numpy as jnp
from jax import lax
from jax.experimental import pallas as pl
from jax.experimental.pallas import tpu as pltpu
from jax.sharding import PartitionSpec as P

AXES = ("lat", "lon")
LANES = 128
VMEM_BYTES = 20 * 1024 * 1024


def call(kernel, outs, scratch, cost, *args, after=(), place=pltpu.VMEM):
    held = pl.BlockSpec(memory_space=pltpu.VMEM)
    count = len(args)

    def ordered(*refs):
        kernel(*refs[:count], *refs[count + len(after) :])

    return pl.pallas_call(
        ordered,
        out_shape=outs,
        in_specs=[pl.BlockSpec(memory_space=place)] * count + [pl.BlockSpec(memory_space=pl.ANY)] * len(after),
        out_specs=jax.tree.map(lambda _: held, outs),
        scratch_shapes=scratch,
        compiler_params=pltpu.CompilerParams(vmem_limit_bytes=VMEM_BYTES),
        cost_estimate=pl.CostEstimate(flops=cost, bytes_accessed=2_000_000, transcendentals=0),
    )(*args, *after)


def shape(dims, dtype=jnp.bfloat16):
    return jax.ShapeDtypeStruct(dims, dtype)


def route(move):
    lats, lons = lax.axis_size("lat"), lax.axis_size("lon")
    pairs = []
    for lat in range(lats):
        for lon in range(lons):
            to_lat, to_lon = move(lat, lon, lats, lons)
            pairs.append((lat * lons + lon, to_lat * lons + to_lon))
    return pairs


def swap(block, lat_bits, lon_bits):
    return lax.ppermute(
        block, AXES, route(lambda lat, lon, lats, lons: (lat ^ lat_bits, lon ^ lon_bits))
    )


def outer_move(lat, lon, lats, lons):
    if lat == 0 or lat == lats - 1:
        return lat, (lon + lons // 2) % lons
    return (lat - 1 if lat % 2 == 0 else lat + 1), lon


def along_move(lat, lon, lats, lons):
    return lat, (lon + 2 if lon % 2 else lon - 2) % lons


def across_move(lat, lon, lats, lons):
    return lat, (lon + 1 if lon % 2 else lon - 1) % lons


def start_kernel(w_hbm, x_hbm, f_hbm, own_ref, pair_ref, outer_ref, inner_ref, x_ref, f_ref, w_ref, sems):
    copies = [
        pltpu.make_async_copy(source, target, sems.at[at])
        for at, (source, target) in enumerate([(w_hbm, w_ref), (x_hbm, x_ref), (f_hbm, f_ref)])
    ]
    for copy in copies:
        copy.start()
    copies[0].wait()
    odd = lax.axis_index("lon") % 2
    half = own_ref.shape[2]
    filled = w_ref.shape[2] - half
    low, high = w_ref[:, :, :half], w_ref[:, :, half:]
    own_ref[...] = jnp.zeros_like(own_ref)
    pair_ref[...] = jnp.zeros_like(pair_ref)

    @pl.when(odd == 0)
    def _():
        own_ref[...] = low
        pair_ref[:, :, :filled] = high

    @pl.when(odd == 1)
    def _():
        own_ref[:, :, :filled] = high
        pair_ref[...] = low

    copies[1].wait()
    radius = outer_ref.shape[0]
    odd = lax.axis_index("lat") % 2
    low, high = x_ref[:radius], x_ref[-radius:]
    outer_ref[...] = jnp.where(odd == 1, high, low)
    inner_ref[...] = jnp.where(odd == 1, low, high)
    copies[2].wait()


def join_kernel(mine_ref, other_ref, out_ref):
    odd = lax.axis_index("lon") % 2
    share = mine_ref.shape[1]
    low, high = mine_ref[...], other_ref[...]
    out_ref[:, :share] = jnp.where(odd == 1, high, low)
    out_ref[:, share:] = jnp.where(odd == 1, low, high)


def stack_kernel(*refs):
    for at, ref in enumerate(refs[:-1]):
        refs[-1][at] = ref[...]


def strip_kernel(half, x_ref, outer_ref, inner_ref, mine_ref, other_ref, rows_ref):
    lat, lon = lax.axis_index("lat"), lax.axis_index("lon")
    pole = (lat == 0) | (lat == lax.axis_size("lat") - 1)
    radius, rows = outer_ref.shape[0], x_ref.shape[0]
    channels = x_ref.shape[2]
    rows_ref[:, :, 2 * half - LANES :] = jnp.zeros_like(rows_ref[:, :, 2 * half - LANES :])
    rows_ref[radius : radius + rows, :, :channels] = x_ref[...]
    at_outer = jnp.where(lat % 2 == 0, 0, radius + rows)
    at_inner = jnp.where(lat % 2 == 0, radius + rows, 0)
    for r in range(radius):
        from_row = jnp.where(pole, radius - 1 - r, r)
        rows_ref[at_outer + r, :, :channels] = outer_ref[from_row]
        rows_ref[at_inner + r, :, :channels] = inner_ref[r]
    low, high = rows_ref[:, :, :half], rows_ref[:, :, half:]
    mine_ref[...] = jnp.where(lon % 2 == 1, high, low)
    other_ref[...] = jnp.where(lon % 2 == 1, low, high)


def band_kernel(reach, f_ref, w_ref, band_ref, row_ref):
    bases, span, rows, taps = f_ref.shape
    columns = band_ref.shape[1] // (2 * bases)
    pitch = columns + taps - 1
    wide = band_ref.shape[2]
    offset = jnp.abs(lax.broadcasted_iota(jnp.int32, (rows, taps), 1) - reach)
    row_ref[...] = jnp.zeros_like(row_ref)
    for d in range(span):
        inside = offset <= w_ref[:, d : d + 1]
        for k in range(bases):
            tap = jnp.where(inside, f_ref[k, d].astype(jnp.float32), 0.0)
            row_ref[k, :, d * pitch : d * pitch + taps] = tap

    def one_pair(pair, _):
        for e in range(2):
            for k in range(bases):
                same = jnp.broadcast_to(row_ref[k, pl.ds(2 * pair + e, 1), :], (columns, wide))
                band = pltpu.roll(same, e * pitch, 1, stride=1, stride_axis=0)
                at = (e * bases + k) * columns
                band_ref[pair, at : at + columns, :] = band.astype(jnp.bfloat16)
        return 0

    lax.fori_loop(0, rows // 2, one_pair, 0)


def feature_kernel(span, band_ref, mine_ref, pair_ref, along_ref, across_ref, out_ref, slab_ref):
    odd = lax.axis_index("lon") % 2
    slab_ref[:, 1 + odd] = mine_ref[...]
    slab_ref[:, 2 - odd] = pair_ref[...]
    slab_ref[:, 3 * (1 - odd)] = along_ref[...]
    slab_ref[:, 3 * odd] = across_ref[...]
    bases, strips, rows, columns, half = out_ref.shape
    depth = (span + 1) * 3 * columns

    def one_pair(pair, _):
        band = band_ref[pair][:, :depth]
        source = [
            slab_ref[pl.ds(2 * pair, span + 1), strip : strip + 3].reshape(depth, half)
            for strip in range(strips)
        ]
        summed = jnp.dot(
            band, jnp.concatenate(source, axis=1), preferred_element_type=jnp.float32
        ).astype(jnp.bfloat16)
        for e in range(2):
            for strip in range(strips):
                part = summed[e * bases * columns : (e + 1) * bases * columns]
                part = part[:, strip * half : (strip + 1) * half]
                out_ref[:, strip, 2 * pair + e] = part.reshape(bases, columns, half)
        return 0

    lax.fori_loop(0, rows // 2, one_pair, 0)


def mix_kernel(sources, feature_ref, *refs):
    piece_refs = refs[: len(sources)]
    keep_ref, send_ref, weight_ref = refs[len(sources) :]
    lat, lon = lax.axis_index("lat"), lax.axis_index("lon")
    odd = lon % 2
    bases, strips, points, half = feature_ref.shape
    masks = weight_ref.shape[1] // 2
    for (core, held), ref in zip(sources, piece_refs):
        for at, mask in enumerate(held):
            place = (lat % 2 ^ core) * masks + ((lon // 2) ^ mask)
            weight_ref[:, place] = ref[at]
    wide = keep_ref.shape[1]

    def strip_sum(strip):
        total = jnp.zeros((points, wide), jnp.float32)
        for k in range(bases):
            total += lax.dot_general(
                feature_ref[k, strip],
                weight_ref[k].reshape(wide, half),
                (((1,), (1,)), ((), ())),
                preferred_element_type=jnp.float32,
            )
        return total

    send_ref[...] = strip_sum(1 - odd).astype(send_ref.dtype)
    keep_ref[...] = strip_sum(odd)


def finish_kernel(count, *refs):
    bias_ref, out_ref = refs[2 * count :]
    share = lax.axis_index("lat") // 2
    for low in range(count):
        keep_ref, got_ref = refs[2 * low : 2 * low + 2]
        wide = keep_ref.shape[1]
        at = pl.ds(pl.multiple_of((share ^ low) * wide, LANES), wide)
        total = keep_ref[...] + got_ref[...].astype(jnp.float32) + bias_ref[:, at]
        grown = 0.5 * total * (1.0 + lax.erf(total * 0.5**0.5))
        out_ref[:, at] = grown.astype(out_ref.dtype)


def body(latent, filters, widths, mix_weight, mix_bias):
    lats, lons = lax.axis_size("lat"), lax.axis_size("lon")
    rows, columns, channels = latent.shape
    bases, _, span, taps = filters.shape
    radius, reach = span // 2, taps // 2
    assert reach == columns and rows % 2 == lats % 2 == lons % 2 == 0
    half = -(-channels // (2 * LANES)) * LANES
    out_columns, share = mix_bias.shape[0], mix_weight.shape[2]

    edge, halves = shape((radius, columns, channels)), shape((bases, share, half))
    weights = jnp.transpose(mix_weight, (0, 2, 1))
    taps_first = jnp.transpose(filters, (0, 2, 1, 3))
    own_weight, pair_weight, outer, inner, held_latent, held_filters = call(
        start_kernel,
        (halves, halves, edge, edge, shape(latent.shape), shape(taps_first.shape)),
        [pltpu.VMEM(weights.shape, jnp.bfloat16), pltpu.SemaphoreType.DMA((3,))],
        100_000,
        weights,
        latent,
        taps_first,
        place=pltpu.HBM,
    )
    got_weight = swap(pair_weight, 0, 1)
    from_outer = lax.ppermute(outer, AXES, route(outer_move))
    from_inner = swap(inner, 1, 0)
    block = shape((bases, 2 * share, half))
    first = call(
        join_kernel, block, [], 100_000, own_weight, got_weight, after=(from_outer, from_inner)
    )

    strip = shape((rows + 2 * radius, columns, half))
    mine, other = call(
        functools.partial(strip_kernel, half),
        (strip, strip),
        [pltpu.VMEM((rows + 2 * radius, columns, 2 * half), jnp.bfloat16)],
        100_000,
        held_latent,
        from_outer,
        from_inner,
        after=(first,),
    )
    pair_strip = swap(other, 0, 1)
    along = lax.ppermute(mine, AXES, route(along_move))
    across = lax.ppermute(other, AXES, route(across_move))

    lon_masks, lat_masks = lons // 2, lats // 2
    blocks = {(0, 0): first}
    bit = lon_masks // 2
    while bit:
        for low, mask in list(blocks):
            blocks[low, mask ^ bit] = swap(blocks[low, mask], 0, 2 * bit)
        bit //= 2
    bit = 1
    while bit < lat_masks:
        for low, mask in list(blocks):
            blocks[low ^ bit, mask] = swap(blocks[low, mask], 2 * bit, 0)
        bit *= 2

    early = [block for (low, _), block in list(blocks.items())[:-1] if low == 1]
    deep = -(-(span + 1) * 3 * columns // LANES) * LANES
    band = call(
        functools.partial(band_kernel, reach),
        shape((rows // 2, 2 * bases * columns, deep)),
        [pltpu.VMEM((bases, rows, deep), jnp.float32)],
        1_000_000_000,
        held_filters,
        widths,
        after=(mine, *early[:1]),
    )
    features = call(
        functools.partial(feature_kernel, span),
        shape((bases, 2, rows, columns, half)),
        [pltpu.VMEM((rows + 2 * radius, 4, columns, half), jnp.bfloat16)],
        4_000_000_000,
        band,
        mine,
        pair_strip,
        along,
        across,
        after=early[1:],
    )
    features = features.reshape(bases, 2, rows * columns, half)

    points, width = rows * columns, out_columns // lat_masks
    keeps, gots = [], []
    for low in range(lat_masks):
        masks = [mask for held, mask in blocks if held == low]
        groups = [masks] if low == 0 else [masks[:-1], masks[-1:]]
        sources, pieces = [], []
        for held in groups:
            if not held:
                continue
            piece = call(
                stack_kernel,
                shape((len(held),) + block.shape),
                [],
                100_000,
                *[blocks[low, mask] for mask in held],
                after=(keeps[-1] if keeps and held == groups[-1] else features,),
            )
            sources += [(0, held), (1, held)]
            pieces += [piece, swap(piece, 1, 0)]
        keep, send = call(
            functools.partial(mix_kernel, sources),
            (shape((points, width), jnp.float32), shape((points, width))),
            [pltpu.VMEM((bases, 2 * lon_masks) + block.shape[1:], jnp.bfloat16)],
            2_000_000_000,
            features,
            *pieces,
        )
        keeps.append(keep)
        gots.append(swap(send, 0, 1))
    if width % LANES == 0:
        parts = [part for pair in zip(keeps, gots) for part in pair]
        out = call(
            functools.partial(finish_kernel, lat_masks),
            shape((points, out_columns)),
            [],
            10_000_000,
            *parts,
            mix_bias[None],
        )
        return out.reshape(rows, columns, out_columns)
    mixed = jnp.stack([keep + got.astype(jnp.float32) for keep, got in zip(keeps, gots)], 1)
    mixed = jnp.take(mixed, jnp.arange(lat_masks) ^ (lax.axis_index("lat") // 2), axis=1)
    mixed = mixed.reshape(rows, columns, out_columns) + mix_bias
    return jax.nn.gelu(mixed, approximate=False).astype(jnp.bfloat16)


def solution(mesh):
    placed = (
        P("lat", "lon", None),
        P(None, "lat", None, None),
        P("lat", None),
        P(None, None, ("lat", "lon")),
        P(),
    )
    return jax.shard_map(
        body, mesh=mesh, in_specs=placed, out_specs=P("lat", "lon", None), check_vma=False
    )
```

time: 77.5 us -> 61.9 us (0.80)
  waiting for transfers between devices: 31.7 us -> 25.8 us
  Pallas kernels: 13.2 us -> 9.69 us
  other arithmetic: 3 us -> 0 us
  local copies, waits for them, and re-layouts: 6.44 us -> 3.61 us
    ppermute x20 -> x15, waiting for transfers between devices: 20.6 us -> 13.2 us  [swap(): lax.ppermute(block, AXES, route(lambda lat, lon, lats, lons: (lat ^ lat_b...]
    ppermute x1, starting transfers between devices: 6.14 us -> 0.06 us  [body(): along = lax.ppermute(mine, AXES, route(along_move))]
    ppermute x1, waiting for transfers between devices: 7.38 us -> 2.93 us  [body(): from_outer = lax.ppermute(outer, AXES, route(outer_move))]
    ppermute x1, waiting for transfers between devices: 3.71 us -> 7.28 us  [body(): across = lax.ppermute(other, AXES, route(across_move))]
    pallas_call x6 -> x11, Pallas kernels: 13.2 us -> 9.69 us  [call(): pl.pallas_call(ordered, out_shape=outs, in_specs=[pl.BlockSpec(memory_spa...]
    ppermute x1, starting transfers between devices: 1.4 us -> 4.46 us  [body(): across = lax.ppermute(other, AXES, route(across_move))]
    ppermute x1, waiting for transfers between devices: 0.01 us -> 2.42 us  [body(): along = lax.ppermute(mine, AXES, route(along_move))]
    ppermute x1, starting transfers between devices: 0.4 us -> 2.59 us  [body(): from_outer = lax.ppermute(outer, AXES, route(outer_move))]
  transfers between devices with their start and end apart: 23 -> 18, of which waited for: 8 -> 9; matrix products, arithmetic and copies ran while one was open for 1% -> 0% of each run, Pallas kernels for 17% -> 13%
where the time goes in v2:
time: 61.9 us; the launch traced here: 61.7 us
  waiting for transfers between devices  25.8 us (42%)
  starting transfers between devices  22.5 us (36%)
  Pallas kernels  9.69 us (16%)
  local copies, waits for them, and re-layouts  3.61 us (6%)
    ppermute x15, starting transfers between devices, swap(): lax.ppermute(block, AXES, route(lambda lat, lon, lats, lons: (lat ^ lat_b...  15.4 us
    ppermute x15, waiting for transfers between devices, swap(): lax.ppermute(block, AXES, route(lambda lat, lon, lats, lons: (lat ^ lat_b...  13.2 us
    pallas_call x11, Pallas kernels, call(): pl.pallas_call(ordered, out_shape=outs, in_specs=[pl.BlockSpec(memory_spa...  9.69 us
    ppermute x1, waiting for transfers between devices, body(): across = lax.ppermute(other, AXES, route(across_move))  7.28 us
    ppermute x1, starting transfers between devices, body(): across = lax.ppermute(other, AXES, route(across_move))  4.46 us
    unnamed x10, local copies, waits for them, and re-layouts  3.61 us
    ppermute x1, waiting for transfers between devices, body(): from_outer = lax.ppermute(outer, AXES, route(outer_move))  2.93 us
    ppermute x1, starting transfers between devices, body(): from_outer = lax.ppermute(outer, AXES, route(outer_move))  2.59 us
  transfers between devices with their start and end apart: 18, of which 9 were waited for; matrix products, arithmetic and copies ran while one was open for 0% of the time, Pallas kernels for 13%

profile of v2, /device:TPU:0, one launch (start us, length us, event | category | flops | bytes accessed | tf_op | source)
XLA Modules:
  0.0 61.7 jit_solution(17967742035164760849)
XLA Ops:
  0.0 1.0 %copy-done = bf16[16,16,641]{2,1,0:T(8,128)(2,1)S(1)} copy-done((bf16[16,16,641]{2,1,0:T(8,128)(2,1)S(1)}, bf16[16,16,641]{2,1,0:T(8,128)(2,1)}, u32[]{:S(2)}) %copy-start) | copy-done | bytes 328216
  1.0 1.0 %copy-done.1 = bf16[9,16,9,33]{3,1,2,0:T(8,128)(2,1)S(1)} copy-done((bf16[9,16,9,33]{3,1,2,0:T(8,128)(2,1)S(1)}, bf16[9,16,9,33]{3,1,2,0:T(8,128)(2,1)}, u32[]{:S(2)}) %copy-start.1) | copy-done | bytes 85560
  2.0 0.9 %copy-done.2 = bf16[9,641,16]{1,2,0:T(8,128)(2,1)S(1)} copy-done((bf16[9,641,16]{1,2,0:T(8,128)(2,1)S(1)}, bf16[9,641,16]{1,2,0:T(8,128)(2,1)}, u32[]{:S(2)}) %copy-start.2) | copy-done | bytes 184632
  2.9 0.6 %shard_map.55 = (bf16[9,16,384]{2,1,0:T(8,128)(2,1)S(1)}, bf16[9,16,384]{2,1,0:T(8,128)(2,1)S(1)}, bf16[4,16,641]{2,1,0:T(8,128)(2,1)S(1)}, bf16[4,16,641]{2,1,0...) custom-call(bf16[9,16,641]{2,1,0:T(8,128)(2,1)S(1)} %bitcast.10, ...), custom_call_target="tpu_custom_call" | custom-call | flops 100000 | bytes 2000000 | tf_op jit(solution)/shard_map/pallas_call | solution.py:22
  3.6 3.0 %collective-permute-start.2 = (bf16[9,16,384]{2,1,0:T(8,128)(2,1)S(1)}, bf16[9,16,384]{2,1,0:T(8,128)(2,1)S(1)}, u32[]{:S(2)}, u32[]{:S(2)}) collective-permute-start(bf16[9,16,384]{2,1,0:T(8,128)(2,1)S(1)} %get-tuple-element.22), channel_id=1, source_target_pairs={{0,1},{1,0},{2,3},{3,2},{4,5},{5,4},{6,7},{7,6},{8,9},{9,8},{10,11... | collective-permute-start | bytes 331784 | tf_op jit(solution)/shard_map/ppermute | solution.py:48
  6.6 2.6 %collective-permute-start = (bf16[4,16,641]{2,1,0:T(8,128)(2,1)S(1)}, bf16[4,16,641]{2,1,0:T(8,128)(2,1)S(1)}, u32[]{:S(2)}, u32[]{:S(2)}) collective-permute-start(bf16[4,16,641]{2,1,0:T(8,128)(2,1)S(1)} %get-tuple-element.19), channel_id=1, source_target_pairs={{0,4},{1,5},{2,6},{3,7},{4,0},{5,1},{6,2},{7,3},{8,16},{9,17},{10,... | collective-permute-start | bytes 246152 | tf_op jit(solution)/shard_map/ppermute | solution.py:248
  9.2 2.9 %collective-permute-done.refs_2_.refs_1_ = bf16[4,16,641]{2,1,0:T(8,128)(2,1)S(1)} collective-permute-done((bf16[4,16,641]{2,1,0:T(8,128)(2,1)S(1)}, bf16[4,16,641]{2,1,0:T(8,128)(2,1)S(1)}, u32[]{:S(2)}, u32[]{:S(2)}) %collective-permute-start) | collective-permute-done | bytes 82080 | tf_op jit(solution)/shard_map/ppermute | solution.py:248
  12.2 2.7 %collective-permute-start.7 = (bf16[9,32,384]{2,1,0:T(8,128)(2,1)S(1)}, bf16[9,32,384]{2,1,0:T(8,128)(2,1)S(1)}, u32[]{:S(2)}, u32[]{:S(2)}) collective-permute-start(bf16[9,32,384]{2,1,0:T(8,128)(2,1)S(1)} %shard_map.56.refs_3_.refs_0_), channel_id=1, source_target_pairs={{0,4},{1,5},{2,6},{3,7},{4,0},{5,1},{6,2},{7,3},{8,12},{9,13},{10,... | collective-permute-start | bytes 663560 | tf_op jit(solution)/shard_map/ppermute | solution.py:48
  15.0 2.4 %collective-permute-start.9 = (bf16[9,32,384]{2,1,0:T(8,128)(2,1)S(1)}, bf16[9,32,384]{2,1,0:T(8,128)(2,1)S(1)}, u32[]{:S(2)}, u32[]{:S(2)}) collective-permute-start(bf16[9,32,384]{2,1,0:T(8,128)(2,1)S(1)} %shard_map.56.refs_3_.refs_0_), channel_id=1, source_target_pairs={{0,2},{1,3},{2,0},{3,1},{4,6},{5,7},{6,4},{7,5},{8,10},{9,11},{10,... | collective-permute-start | bytes 663560 | tf_op jit(solution)/shard_map/ppermute | solution.py:48
  17.6 0.6 collective-permute-start.4
  18.2 4.5 %collective-permute-start.6 = (bf16[24,16,384]{2,1,0:T(8,128)(2,1)S(1)}, bf16[24,16,384]{2,1,0:T(8,128)(2,1)S(1)}, u32[]{:S(2)}, u32[]{:S(2)}) collective-permute-start(bf16[24,16,384]{2,1,0:T(8,128)(2,1)S(1)} %get-tuple-element.24), channel_id=1, source_target_pairs={{0,7},{1,2},{2,1},{3,4},{4,3},{5,6},{6,5},{7,0},{8,15},{9,10},{10,... | collective-permute-start | bytes 884744 | tf_op jit(solution)/shard_map/ppermute | solution.py:268
  22.6 3.7 %collective-permute-done.7.refs_1_ = bf16[9,32,384]{2,1,0:T(8,128)(2,1)S(1)} collective-permute-done((bf16[9,32,384]{2,1,0:T(8,128)(2,1)S(1)}, bf16[9,32,384]{2,1,0:T(8,128)(2,1)S(1)}, u32[]{:S(2)}, u32[]{:S(2)}) %collective-permute-start.7) | collective-permute-done | bytes 221216 | tf_op jit(solution)/shard_map/ppermute | solution.py:48
  26.3 0.9 %collective-permute-start.8 = (bf16[9,32,384]{2,1,0:T(8,128)(2,1)S(1)}, bf16[9,32,384]{2,1,0:T(8,128)(2,1)S(1)}, u32[]{:S(2)}, u32[]{:S(2)}) collective-permute-start(bf16[9,32,384]{2,1,0:T(8,128)(2,1)S(1)} %collective-permute-done.7.refs_1_), channel_id=1, source_target_pairs={{0,16},{1,17},{2,18},{3,19},{4,20},{5,21},{6,22},{7,23},{8,24},{9,... | collective-permute-start | bytes 663560 | tf_op jit(solution)/shard_map/ppermute | solution.py:48
  27.2 1.1 %collective-permute-start.10 = (bf16[9,32,384]{2,1,0:T(8,128)(2,1)S(1)}, bf16[9,32,384]{2,1,0:T(8,128)(2,1)S(1)}, u32[]{:S(2)}, u32[]{:S(2)}) collective-permute-start(bf16[9,32,384]{2,1,0:T(8,128)(2,1)S(1)} %collective-permute-done.9.refs_2_), channel_id=1, source_target_pairs={{0,16},{1,17},{2,18},{3,19},{4,20},{5,21},{6,22},{7,23},{8,24},{9,... | collective-permute-start | bytes 663560 | tf_op jit(solution)/shard_map/ppermute | solution.py:48
  28.3 0.7 %copy-done.4 = s32[16,9]{1,0:T(8,128)S(1)} copy-done((s32[16,9]{1,0:T(8,128)S(1)}, s32[16,9]{1,0:T(8,128)}, u32[]{:S(2)}) %copy-start.4) | copy-done | bytes 600
  29.0 1.4 %shard_map.58.refs_0_ = bf16[8,288,512]{2,1,0:T(8,128)(2,1)S(1)} custom-call(bf16[9,9,16,33]{3,2,1,0:T(8,128)(2,1)S(1)} %get-tuple-element.17.refs_0_, s32[16,9]{1,0:T(8,128)S(1)} %copy-done.4, bf16[24,16,384]{2,1,0:T(8,128)(2,1)S(1)} %get-tuple-element.23.refs_2_.refs_1_, bf16[9,32,384]{2,1,0:T(8,128)(2,1)S(1)} %collective-permute-done.3.refs_3_.refs_0_), custom_call_target="tpu_custom_call" | custom-call | flops 1000000000 | bytes 2000000 | tf_op jit(solution)/shard_map/pallas_call | solution.py:22
  30.4 2.4 %collective-permute-done.5.refs_3_ = bf16[24,16,384]{2,1,0:T(8,128)(2,1)S(1)} collective-permute-done((bf16[24,16,384]{2,1,0:T(8,128)(2,1)S(1)}, bf16[24,16,384]{2,1,0:T(8,128)(2,1)S(1)}, u32[]{:S(2)}, u32[]{:S(2)}) %collective-permute-start.5) | collective-permute-done | bytes 294944 | tf_op jit(solution)/shard_map/ppermute | solution.py:267
  32.9 0.3 collective-permute-start.11
  33.2 7.3 %collective-permute-done.6.refs_4_ = bf16[24,16,384]{2,1,0:T(8,128)(2,1)S(1)} collective-permute-done((bf16[24,16,384]{2,1,0:T(8,128)(2,1)S(1)}, bf16[24,16,384]{2,1,0:T(8,128)(2,1)S(1)}, u32[]{:S(2)}, u32[]{:S(2)}) %collective-permute-start.6) | collective-permute-done | bytes 294944 | tf_op jit(solution)/shard_map/ppermute | solution.py:268
  40.5 3.3 %shard_map.59 = bf16[9,2,16,16,384]{4,3,2,1,0:T(8,128)(2,1)S(1)} custom-call(bf16[8,288,512]{2,1,0:T(8,128)(2,1)S(1)} %shard_map.58.refs_0_, bf16[24,16,384]{2,1,0:T(8,128)(2,1)S(1)} %get-tuple-element.23.refs_2_.refs_1_, bf16[24,16,384]{2,1,0:T(8,128)(2,1)S(1)} %collective-permute-done.4.refs_2_, bf16[24,16,384]{2,1,0:T(8,128)(2,1)S(1)} %collective-permute-done.5.refs_3_, ...), custom_call_target="tpu_custom_call" | custom-call | flops 4000000000 | bytes 2000000 | tf_op jit(solution)/shard_map/pallas_call | solution.py:22
  44.0 0.6 collective-permute-start.14
  44.6 1.6 %collective-permute-start.15 = (bf16[9,32,384]{2,1,0:T(8,128)(2,1)S(1)}, bf16[9,32,384]{2,1,0:T(8,128)(2,1)S(1)}, u32[]{:S(2)}, u32[]{:S(2)}) collective-permute-start(bf16[9,32,384]{2,1,0:T(8,128)(2,1)S(1)} %collective-permute-done.11.refs_3_), channel_id=1, source_target_pairs={{0,16},{1,17},{2,18},{3,19},{4,20},{5,21},{6,22},{7,23},{8,24},{9,... | collective-permute-start | bytes 663560 | tf_op jit(solution)/shard_map/ppermute | solution.py:48
  46.2 0.1 collective-permute-done.12.refs_2_
  46.4 1.6 %shard_map.61 = (f32[256,256]{1,0:T(8,128)S(1)}, bf16[256,256]{1,0:T(8,128)(2,1)S(1)}) custom-call(bf16[9,2,256,384]{3,2,1,0:T(8,128)(2,1)S(1)} %bitcast.7, bf16[4,9,32,384]{3,2,1,0:T(8,128)(2,1)S(1)} %shard_map.60.refs_1_, bf16[4,9,32,384]{3,2,1,0:T(8,128)(2,1)S(1)} %collective-permute-done.12.refs_2_), custom_call_target="tpu_custom_call" | custom-call | flops 2000000000 | bytes 2000000 | tf_op jit(solution)/shard_map/pallas_call | solution.py:22
  48.0 4.0 %collective-permute-done.15.refs_0_ = bf16[9,32,384]{2,1,0:T(8,128)(2,1)S(1)} collective-permute-done((bf16[9,32,384]{2,1,0:T(8,128)(2,1)S(1)}, bf16[9,32,384]{2,1,0:T(8,128)(2,1)S(1)}, u32[]{:S(2)}, u32[]{:S(2)}) %collective-permute-start.15) | collective-permute-done | bytes 221216 | tf_op jit(solution)/shard_map/ppermute | solution.py:48
  52.1 0.9 %collective-permute-start.13 = (bf16[256,256]{1,0:T(8,128)(2,1)S(1)}, bf16[256,256]{1,0:T(8,128)(2,1)S(1)}, u32[]{:S(2)}, u32[]{:S(2)}) collective-permute-start(bf16[256,256]{1,0:T(8,128)(2,1)S(1)} %get-tuple-element.26), channel_id=1, source_target_pairs={{0,1},{1,0},{2,3},{3,2},{4,5},{5,4},{6,7},{7,6},{8,9},{9,8},{10,11... | collective-permute-start | bytes 393224 | tf_op jit(solution)/shard_map/ppermute | solution.py:48
  53.0 0.5 collective-permute-done.16.refs_4_
  53.6 1.6 %shard_map.64 = (f32[256,256]{1,0:T(8,128)S(1)}, bf16[256,256]{1,0:T(8,128)(2,1)S(1)}) custom-call(bf16[9,2,256,384]{3,2,1,0:T(8,128)(2,1)S(1)} %bitcast.8, bf16[3,9,32,384]{3,2,1,0:T(8,128)(2,1)S(1)} %shard_map.62.refs_1_, bf16[3,9,32,384]{3,2,1,0:T(8,128)(2,1)S(1)} %collective-permute-done.14.refs_2_, bf16[1,9,32,384]{3,2,1,0:T(8,128)(2,1)S(1)} %shard_map.63.refs_3_, ...), custom_call_target="tpu_custom_call" | custom-call | flops 2000000000 | bytes 2000000 | tf_op jit(solution)/shard_map/pallas_call | solution.py:22
  55.2 0.9 %collective-permute-start.17 = (bf16[256,256]{1,0:T(8,128)(2,1)S(1)}, bf16[256,256]{1,0:T(8,128)(2,1)S(1)}, u32[]{:S(2)}, u32[]{:S(2)}) collective-permute-start(bf16[256,256]{1,0:T(8,128)(2,1)S(1)} %get-tuple-element.28), channel_id=1, source_target_pairs={{0,1},{1,0},{2,3},{3,2},{4,5},{5,4},{6,7},{7,6},{8,9},{9,8},{10,11... | collective-permute-start | bytes 393224 | tf_op jit(solution)/shard_map/ppermute | solution.py:48
  56.1 2.0 %collective-permute-done.13.refs_1_ = bf16[256,256]{1,0:T(8,128)(2,1)S(1)} collective-permute-done((bf16[256,256]{1,0:T(8,128)(2,1)S(1)}, bf16[256,256]{1,0:T(8,128)(2,1)S(1)}, u32[]{:S(2)}, u32[]{:S(2)}) %collective-permute-start.13) | collective-permute-done | bytes 131104 | tf_op jit(solution)/shard_map/ppermute | solution.py:48
  58.0 2.8 %collective-permute-done.17.refs_3_ = bf16[256,256]{1,0:T(8,128)(2,1)S(1)} collective-permute-done((bf16[256,256]{1,0:T(8,128)(2,1)S(1)}, bf16[256,256]{1,0:T(8,128)(2,1)S(1)}, u32[]{:S(2)}, u32[]{:S(2)}) %collective-permute-start.17) | collective-permute-done | bytes 131104 | tf_op jit(solution)/shard_map/ppermute | solution.py:48
  60.8 0.9 %shard_map.65 = bf16[256,512]{1,0:T(8,128)(2,1)} custom-call(f32[256,256]{1,0:T(8,128)S(1)} %get-tuple-element.25.refs_1_.refs_0_, bf16[256,256]{1,0:T(8,128)(2,1)S(1)} %collective-permute-done.13.refs_1_, f32[256,256]{1,0:T(8,128)S(1)} %get-tuple-element.27.refs_2_, bf16[256,256]{1,0:T(8,128)(2,1)S(1)} %collective-permute-done.17.refs_3_, f32[1,512]{1,0:T(1,128)S(1)} %bitcast.11), custom_call_target="tpu_custom_call" | custom-call | flops 10000000 | bytes 2000000 | tf_op jit(solution)/shard_map/pallas_call | solution.py:22
  (25 shorter events, 0.6 us)
Async XLA Ops:
  0.0 1.0 %copy-start = (bf16[16,16,641]{2,1,0:T(8,128)(2,1)S(1)}, bf16[16,16,641]{2,1,0:T(8,128)(2,1)}, u32[]{:S(2)}) copy-start(bf16[16,16,641]{2,1,0:T(8,128)(2,1)} %refs_1_.2) | copy-start | bytes 984580
  1.0 1.0 %copy-start.1 = (bf16[9,16,9,33]{3,1,2,0:T(8,128)(2,1)S(1)}, bf16[9,16,9,33]{3,1,2,0:T(8,128)(2,1)}, u32[]{:S(2)}) copy-start(bf16[9,16,9,33]{3,1,2,0:T(8,128)(2,1)} %param.6) | copy-start | bytes 256612
  2.0 0.9 %copy-start.2 = (bf16[9,641,16]{1,2,0:T(8,128)(2,1)S(1)}, bf16[9,641,16]{1,2,0:T(8,128)(2,1)}, u32[]{:S(2)}) copy-start(bf16[9,641,16]{1,2,0:T(8,128)(2,1)} %param.8) | copy-start | bytes 553828
  3.6 8.6 %collective-permute-start.2 = (bf16[9,16,384]{2,1,0:T(8,128)(2,1)S(1)}, bf16[9,16,384]{2,1,0:T(8,128)(2,1)S(1)}, u32[]{:S(2)}, u32[]{:S(2)}) collective-permute-start(bf16[9,16,384]{2,1,0:T(8,128)(2,1)S(1)} %get-tuple-element.22), channel_id=1, source_target_pairs={{0,1},{1,0},{2,3},{3,2},{4,5},{5,4},{6,7},{7,6},{8,9},{9,8},{10,11... | collective-permute-start | bytes 331784 | tf_op jit(solution)/shard_map/ppermute | solution.py:48
  6.6 5.5 %collective-permute-start = (bf16[4,16,641]{2,1,0:T(8,128)(2,1)S(1)}, bf16[4,16,641]{2,1,0:T(8,128)(2,1)S(1)}, u32[]{:S(2)}, u32[]{:S(2)}) collective-permute-start(bf16[4,16,641]{2,1,0:T(8,128)(2,1)S(1)} %get-tuple-element.19), channel_id=1, source_target_pairs={{0,4},{1,5},{2,6},{3,7},{4,0},{5,1},{6,2},{7,3},{8,16},{9,17},{10,... | collective-permute-start | bytes 246152 | tf_op jit(solution)/shard_map/ppermute | solution.py:248
  9.2 2.9 %collective-permute-start.1 = (bf16[4,16,641]{2,1,0:T(8,128)(2,1)S(1)}, bf16[4,16,641]{2,1,0:T(8,128)(2,1)S(1)}, u32[]{:S(2)}, u32[]{:S(2)}) collective-permute-start(bf16[4,16,641]{2,1,0:T(8,128)(2,1)S(1)} %get-tuple-element.20), channel_id=1, source_target_pairs={{0,8},{1,9},{2,10},{3,11},{4,12},{5,13},{6,14},{7,15},{8,0},{9,1},... | collective-permute-start | bytes 246152 | tf_op jit(solution)/shard_map/ppermute | solution.py:48
  12.2 6.0 %collective-permute-start.3 = (bf16[9,32,384]{2,1,0:T(8,128)(2,1)S(1)}, bf16[9,32,384]{2,1,0:T(8,128)(2,1)S(1)}, u32[]{:S(2)}, u32[]{:S(2)}) collective-permute-start(bf16[9,32,384]{2,1,0:T(8,128)(2,1)S(1)} %shard_map.56.refs_3_.refs_0_), channel_id=1, source_target_pairs={{0,16},{1,17},{2,18},{3,19},{4,20},{5,21},{6,22},{7,23},{8,24},{9,... | collective-permute-start | bytes 663560 | tf_op jit(solution)/shard_map/ppermute | solution.py:48
  12.2 14.1 %collective-permute-start.7 = (bf16[9,32,384]{2,1,0:T(8,128)(2,1)S(1)}, bf16[9,32,384]{2,1,0:T(8,128)(2,1)S(1)}, u32[]{:S(2)}, u32[]{:S(2)}) collective-permute-start(bf16[9,32,384]{2,1,0:T(8,128)(2,1)S(1)} %shard_map.56.refs_3_.refs_0_), channel_id=1, source_target_pairs={{0,4},{1,5},{2,6},{3,7},{4,0},{5,1},{6,2},{7,3},{8,12},{9,13},{10,... | collective-permute-start | bytes 663560 | tf_op jit(solution)/shard_map/ppermute | solution.py:48
  15.0 12.2 %collective-permute-start.9 = (bf16[9,32,384]{2,1,0:T(8,128)(2,1)S(1)}, bf16[9,32,384]{2,1,0:T(8,128)(2,1)S(1)}, u32[]{:S(2)}, u32[]{:S(2)}) collective-permute-start(bf16[9,32,384]{2,1,0:T(8,128)(2,1)S(1)} %shard_map.56.refs_3_.refs_0_), channel_id=1, source_target_pairs={{0,2},{1,3},{2,0},{3,1},{4,6},{5,7},{6,4},{7,5},{8,10},{9,11},{10,... | collective-permute-start | bytes 663560 | tf_op jit(solution)/shard_map/ppermute | solution.py:48
  17.5 15.3 %collective-permute-start.5 = (bf16[24,16,384]{2,1,0:T(8,128)(2,1)S(1)}, bf16[24,16,384]{2,1,0:T(8,128)(2,1)S(1)}, u32[]{:S(2)}, u32[]{:S(2)}) collective-permute-start(bf16[24,16,384]{2,1,0:T(8,128)(2,1)S(1)} %get-tuple-element.23.refs_2_.refs_1_), channel_id=1, source_target_pairs={{0,6},{1,3},{2,0},{3,5},{4,2},{5,7},{6,4},{7,1},{8,14},{9,11},{10,... | collective-permute-start | bytes 884744 | tf_op jit(solution)/shard_map/ppermute | solution.py:267
  17.6 15.6 %collective-permute-start.4 = (bf16[24,16,384]{2,1,0:T(8,128)(2,1)S(1)}, bf16[24,16,384]{2,1,0:T(8,128)(2,1)S(1)}, u32[]{:S(2)}, u32[]{:S(2)}) collective-permute-start(bf16[24,16,384]{2,1,0:T(8,128)(2,1)S(1)} %get-tuple-element.24), channel_id=1, source_target_pairs={{0,1},{1,0},{2,3},{3,2},{4,5},{5,4},{6,7},{7,6},{8,9},{9,8},{10,11... | collective-permute-start | bytes 884744 | tf_op jit(solution)/shard_map/ppermute | solution.py:48
  18.2 22.3 %collective-permute-start.6 = (bf16[24,16,384]{2,1,0:T(8,128)(2,1)S(1)}, bf16[24,16,384]{2,1,0:T(8,128)(2,1)S(1)}, u32[]{:S(2)}, u32[]{:S(2)}) collective-permute-start(bf16[24,16,384]{2,1,0:T(8,128)(2,1)S(1)} %get-tuple-element.24), channel_id=1, source_target_pairs={{0,7},{1,2},{2,1},{3,4},{4,3},{5,6},{6,5},{7,0},{8,15},{9,10},{10,... | collective-permute-start | bytes 884744 | tf_op jit(solution)/shard_map/ppermute | solution.py:268
  26.3 14.2 %collective-permute-start.8 = (bf16[9,32,384]{2,1,0:T(8,128)(2,1)S(1)}, bf16[9,32,384]{2,1,0:T(8,128)(2,1)S(1)}, u32[]{:S(2)}, u32[]{:S(2)}) collective-permute-start(bf16[9,32,384]{2,1,0:T(8,128)(2,1)S(1)} %collective-permute-done.7.refs_1_), channel_id=1, source_target_pairs={{0,16},{1,17},{2,18},{3,19},{4,20},{5,21},{6,22},{7,23},{8,24},{9,... | collective-permute-start | bytes 663560 | tf_op jit(solution)/shard_map/ppermute | solution.py:48
  27.2 13.2 %collective-permute-start.10 = (bf16[9,32,384]{2,1,0:T(8,128)(2,1)S(1)}, bf16[9,32,384]{2,1,0:T(8,128)(2,1)S(1)}, u32[]{:S(2)}, u32[]{:S(2)}) collective-permute-start(bf16[9,32,384]{2,1,0:T(8,128)(2,1)S(1)} %collective-permute-done.9.refs_2_), channel_id=1, source_target_pairs={{0,16},{1,17},{2,18},{3,19},{4,20},{5,21},{6,22},{7,23},{8,24},{9,... | collective-permute-start | bytes 663560 | tf_op jit(solution)/shard_map/ppermute | solution.py:48
  28.3 0.7 %copy-start.4 = (s32[16,9]{1,0:T(8,128)S(1)}, s32[16,9]{1,0:T(8,128)}, u32[]{:S(2)}) copy-start(s32[16,9]{1,0:T(8,128)} %refs_1_.3) | copy-start | bytes 1732
  32.9 10.9 %collective-permute-start.11 = (bf16[9,32,384]{2,1,0:T(8,128)(2,1)S(1)}, bf16[9,32,384]{2,1,0:T(8,128)(2,1)S(1)}, u32[]{:S(2)}, u32[]{:S(2)}) collective-permute-start(bf16[9,32,384]{2,1,0:T(8,128)(2,1)S(1)} %collective-permute-done.7.refs_1_), channel_id=1, source_target_pairs={{0,2},{1,3},{2,0},{3,1},{4,6},{5,7},{6,4},{7,5},{8,10},{9,11},{10,... | collective-permute-start | bytes 663560 | tf_op jit(solution)/shard_map/ppermute | solution.py:48
  43.9 2.5 %collective-permute-start.12 = (bf16[4,9,32,384]{3,2,1,0:T(8,128)(2,1)S(1)}, bf16[4,9,32,384]{3,2,1,0:T(8,128)(2,1)S(1)}, u32[]{:S(2)}, u32[]{:S(2)}) collective-permute-start(bf16[4,9,32,384]{3,2,1,0:T(8,128)(2,1)S(1)} %shard_map.60.refs_1_), channel_id=1, source_target_pairs={{0,8},{1,9},{2,10},{3,11},{4,12},{5,13},{6,14},{7,15},{8,0},{9,1},... | collective-permute-start | bytes 2654216 | tf_op jit(solution)/shard_map/ppermute | solution.py:48
  44.0 9.0 %collective-permute-start.14 = (bf16[3,9,32,384]{3,2,1,0:T(8,128)(2,1)S(1)}, bf16[3,9,32,384]{3,2,1,0:T(8,128)(2,1)S(1)}, u32[]{:S(2)}, u32[]{:S(2)}) collective-permute-start(bf16[3,9,32,384]{3,2,1,0:T(8,128)(2,1)S(1)} %shard_map.62.refs_1_), channel_id=1, source_target_pairs={{0,8},{1,9},{2,10},{3,11},{4,12},{5,13},{6,14},{7,15},{8,0},{9,1},... | collective-permute-start | bytes 1990664 | tf_op jit(solution)/shard_map/ppermute | solution.py:48
  44.6 7.4 %collective-permute-start.15 = (bf16[9,32,384]{2,1,0:T(8,128)(2,1)S(1)}, bf16[9,32,384]{2,1,0:T(8,128)(2,1)S(1)}, u32[]{:S(2)}, u32[]{:S(2)}) collective-permute-start(bf16[9,32,384]{2,1,0:T(8,128)(2,1)S(1)} %collective-permute-done.11.refs_3_), channel_id=1, source_target_pairs={{0,16},{1,17},{2,18},{3,19},{4,20},{5,21},{6,22},{7,23},{8,24},{9,... | collective-permute-start | bytes 663560 | tf_op jit(solution)/shard_map/ppermute | solution.py:48
  52.0 1.5 %collective-permute-start.16 = (bf16[1,9,32,384]{3,2,1,0:T(8,128)(2,1)S(1)}, bf16[1,9,32,384]{3,2,1,0:T(8,128)(2,1)S(1)}, u32[]{:S(2)}, u32[]{:S(2)}) collective-permute-start(bf16[1,9,32,384]{3,2,1,0:T(8,128)(2,1)S(1)} %shard_map.63.refs_3_), channel_id=1, source_target_pairs={{0,8},{1,9},{2,10},{3,11},{4,12},{5,13},{6,14},{7,15},{8,0},{9,1},... | collective-permute-start | bytes 663560 | tf_op jit(solution)/shard_map/ppermute | solution.py:48
  52.1 8.7 %copy-start.3 = (f32[512]{0:T(512)S(1)}, f32[512]{0:T(512)}, u32[]{:S(2)}) copy-start(f32[512]{0:T(512)} %param.9) | copy-start | bytes 6148
  52.1 5.9 %collective-permute-start.13 = (bf16[256,256]{1,0:T(8,128)(2,1)S(1)}, bf16[256,256]{1,0:T(8,128)(2,1)S(1)}, u32[]{:S(2)}, u32[]{:S(2)}) collective-permute-start(bf16[256,256]{1,0:T(8,128)(2,1)S(1)} %get-tuple-element.26), channel_id=1, source_target_pairs={{0,1},{1,0},{2,3},{3,2},{4,5},{5,4},{6,7},{7,6},{8,9},{9,8},{10,11... | collective-permute-start | bytes 393224 | tf_op jit(solution)/shard_map/ppermute | solution.py:48
  55.2 5.7 %collective-permute-start.17 = (bf16[256,256]{1,0:T(8,128)(2,1)S(1)}, bf16[256,256]{1,0:T(8,128)(2,1)S(1)}, u32[]{:S(2)}, u32[]{:S(2)}) collective-permute-start(bf16[256,256]{1,0:T(8,128)(2,1)S(1)} %get-tuple-element.28), channel_id=1, source_target_pairs={{0,1},{1,0},{2,3},{3,2},{4,5},{5,4},{6,7},{7,6},{8,9},{9,8},{10,11... | collective-permute-start | bytes 393224 | tf_op jit(solution)/shard_map/ppermute | solution.py:48

commit v3 on v2

v3 whole, which is shorter than its diff:
```python
import functools

import jax
import jax.numpy as jnp
from jax import lax
from jax.experimental import pallas as pl
from jax.experimental.pallas import tpu as pltpu
from jax.sharding import PartitionSpec as P


AXES = ("lat", "lon")
LANES = 128
HALF = LANES // 2
VMEM_BYTES = 20 * 1024 * 1024


def call(kernel, outs, scratch, *args, after=()):
    held = pl.BlockSpec(memory_space=pltpu.VMEM)
    count = len(args)

    def ordered(*refs):
        kernel(*refs[:count], *refs[count + len(after) :])

    return pl.pallas_call(
        ordered,
        out_shape=outs,
        in_specs=[held] * count + [pl.BlockSpec(memory_space=pl.ANY)] * len(after),
        out_specs=jax.tree.map(lambda _: held, outs),
        scratch_shapes=scratch,
        compiler_params=pltpu.CompilerParams(vmem_limit_bytes=VMEM_BYTES),
    )(*args, *after)


def shape(dims, dtype=jnp.bfloat16):
    return jax.ShapeDtypeStruct(dims, dtype)


def route(move):
    lats, lons = lax.axis_size("lat"), lax.axis_size("lon")
    pairs = []
    for lat in range(lats):
        for lon in range(lons):
            to_lat, to_lon = move(lat, lon, lats, lons)
            pairs.append((lat * lons + lon, to_lat * lons + to_lon))
    return pairs


def swap(block, lat_bits, lon_bits):
    return lax.ppermute(
        block, AXES, route(lambda lat, lon, lats, lons: (lat ^ lat_bits, lon ^ lon_bits))
    )


def outer_move(lat, lon, lats, lons):
    if lat == 0 or lat == lats - 1:
        return lat, (lon + lons // 2) % lons
    return (lat - 1 if lat % 2 == 0 else lat + 1), lon


def along_move(lat, lon, lats, lons):
    return lat, (lon + 2 if lon % 2 else lon - 2) % lons


def across_move(lat, lon, lats, lons):
    return lat, (lon + 1 if lon % 2 else lon - 1) % lons


def lane_of(value):
    return lax.broadcasted_iota(jnp.int32, value.shape, 1)


def turned(value, lanes):
    return pltpu.roll(value, lanes, 1)


def put(refs, odd, at, low, high):
    wide = low.shape[1]
    low, high = low.astype(jnp.bfloat16), high.astype(jnp.bfloat16)
    refs[0][:, at : at + wide] = jnp.where(odd == 1, high, low)
    refs[1][:, at : at + wide] = jnp.where(odd == 1, low, high)


def put_main(refs, odd, at, value, main):
    put(refs, odd, at, value[:, :main], value[:, main : 2 * main])


def split_of(value, main):
    return value[:, 2 * main : 2 * main + LANES].astype(jnp.float32)


def put_pair(refs, odd, at, first, second, main):
    put_main(refs, odd, at, first, main)
    put_main(refs, odd, at + main, second, main)
    first, second = split_of(first, main), split_of(second, main)
    front = lane_of(first) < HALF
    low = jnp.where(front, first, turned(second, HALF))
    high = jnp.where(front, turned(first, HALF), second)
    put(refs, odd, at + 2 * main, low, high)


def spare_of(tile, values, main, start):
    lane = lane_of(tile)
    for at, value in enumerate(values):
        last = value[:, 2 * main + LANES :].astype(jnp.float32)
        tile = jnp.where(lane == start + at, jnp.broadcast_to(last, tile.shape), tile)
    return tile


def start_kernel(main, w_ref, x_ref, own_ref, pair_ref, outer_ref, inner_ref):
    odd = lax.axis_index("lon") % 2
    refs = own_ref, pair_ref
    bases = w_ref.shape[0]
    values = [w_ref[k] for k in range(bases)]
    for k in range(0, bases - 1, 2):
        put_pair(refs, odd, k // 2 * (2 * main + LANES), values[k], values[k + 1], main)
    at = bases // 2 * (2 * main + LANES)
    put_main(refs, odd, at, values[-1], main)
    tile = split_of(values[-1], main)
    front = lane_of(tile) < HALF
    low, high = jnp.where(front, tile, 0.0), jnp.where(front, turned(tile, HALF), 0.0)
    put(refs, odd, at + main, low, spare_of(high, values, main, HALF))
    radius = outer_ref.shape[0]
    lower = lax.axis_index("lat") % 2
    low, high = x_ref[:radius], x_ref[-radius:]
    outer_ref[...] = jnp.where(lower == 1, high, low)
    inner_ref[...] = jnp.where(lower == 1, low, high)


def strip_kernel(main, x_ref, outer_ref, inner_ref, mine_ref, other_ref, rows_ref):
    lat, odd = lax.axis_index("lat"), lax.axis_index("lon") % 2
    pole = (lat == 0) | (lat == lax.axis_size("lat") - 1)
    radius, rows = outer_ref.shape[0], x_ref.shape[0]
    rows_ref[radius : radius + rows] = x_ref[...]
    far = radius + rows
    for r in range(radius):
        rows_ref[lat % 2 * far + r] = outer_ref[jnp.where(pole, radius - 1 - r, r)]
        rows_ref[(1 - lat % 2) * far + r] = inner_ref[r]
    refs = mine_ref, other_ref
    count = rows_ref.shape[0]
    values = [rows_ref[r] for r in range(count)]
    for r in range(count // 2):
        at = r * (2 * main + LANES)
        put_pair(refs, odd, at, values[r], values[r + count // 2], main)
    none = jnp.zeros((x_ref.shape[1], LANES), jnp.float32)
    put(refs, odd, count // 2 * (2 * main + LANES), none, spare_of(none, values, main, 0))


def join_kernel(mine_ref, other_ref, out_ref):
    odd = lax.axis_index("lon") % 2
    share = mine_ref.shape[0]
    low, high = mine_ref[...], other_ref[...]
    out_ref[:share] = jnp.where(odd == 1, high, low)
    out_ref[share:] = jnp.where(odd == 1, low, high)


def copy_kernel(source_ref, out_ref):
    out_ref[...] = source_ref[...]


def stack_kernel(*refs):
    for at, ref in enumerate(refs[:-1]):
        refs[-1][at] = ref[...]


def band_kernel(reach, f_ref, w_ref, band_ref, row_ref):
    bases, span, rows, taps = f_ref.shape
    columns = band_ref.shape[1] // (2 * bases)
    pitch = columns + taps - 1
    wide = band_ref.shape[2]
    offset = jnp.abs(lax.broadcasted_iota(jnp.int32, (rows, taps), 1) - reach)
    row_ref[...] = jnp.zeros_like(row_ref)
    for d in range(span):
        inside = offset <= w_ref[:, d : d + 1]
        for k in range(bases):
            tap = jnp.where(inside, f_ref[k, d].astype(jnp.float32), 0.0)
            row_ref[k, :, d * pitch : d * pitch + taps] = tap

    def one_pair(pair, _):
        for e in range(2):
            for k in range(bases):
                same = jnp.broadcast_to(row_ref[k, pl.ds(2 * pair + e, 1), :], (columns, wide))
                band = pltpu.roll(same, e * pitch, 1, stride=1, stride_axis=0)
                at = (e * bases + k) * columns
                band_ref[pair, at : at + columns, :] = band.astype(jnp.bfloat16)
        return 0

    lax.fori_loop(0, rows // 2, one_pair, 0)


def unpack(source_ref, slab_ref, slot, main):
    count = slab_ref.shape[0]
    wide = 2 * main + LANES
    spare = source_ref[:, count // 2 * wide :].astype(jnp.float32)
    lane = lane_of(spare)
    for r in range(count // 2):
        tile = source_ref[:, r * wide + 2 * main : (r + 1) * wide].astype(jnp.float32)
        for row, third in ((r, tile), (r + count // 2, turned(tile, HALF))):
            at = r * wide + (main if row > r else 0)
            slab_ref[row, slot, :, :main] = source_ref[:, at : at + main]
            last = turned(spare, (HALF - row) % LANES)
            third = jnp.where(lane == HALF, last, third)
            slab_ref[row, slot, :, main:] = third.astype(jnp.bfloat16)


def feature_kernel(span, band_ref, mine_ref, pair_ref, along_ref, across_ref, out_ref, slab_ref):
    odd = lax.axis_index("lon") % 2
    strips, rows, columns, _ = out_ref.shape
    half = slab_ref.shape[3]
    main = half - LANES
    unpack(mine_ref, slab_ref, 1 + odd, main)
    unpack(pair_ref, slab_ref, 2 - odd, main)
    unpack(along_ref, slab_ref, 3 * (1 - odd), main)
    unpack(across_ref, slab_ref, 3 * odd, main)
    bases = band_ref.shape[1] // (2 * columns)
    depth = (span + 1) * 3 * columns
    wide = 2 * main + LANES

    def one_pair(pair, _):
        band = band_ref[pair][:, :depth]
        source = [
            slab_ref[pl.ds(2 * pair, span + 1), strip : strip + 3].reshape(depth, half)
            for strip in range(strips)
        ]
        summed = jnp.dot(
            band, jnp.concatenate(source, axis=1), preferred_element_type=jnp.float32
        )
        for e in range(2):
            for strip in range(strips):

                def save(at, value):
                    out_ref[strip, 2 * pair + e, :, at : at + value.shape[1]] = value.astype(
                        jnp.bfloat16
                    )

                parts = []
                for k in range(bases):
                    at = (e * bases + k) * columns
                    parts.append(summed[at : at + columns, strip * half : (strip + 1) * half])
                lane = lane_of(parts[0][:, main:])
                for k, part in enumerate(parts):
                    save(k // 2 * wide + k % 2 * main, part[:, :main])
                for k in range(0, bases - 1, 2):
                    second = turned(parts[k + 1][:, main:], HALF)
                    save(k // 2 * wide + 2 * main, jnp.where(lane < HALF, parts[k][:, main:], second))
                tile = parts[-1][:, main:]
                for k in range(bases):
                    tile = jnp.where(lane == HALF + k, turned(parts[k][:, main:], k), tile)
                save(bases // 2 * wide + main, tile)
        return 0

    lax.fori_loop(0, rows // 2, one_pair, 0)


def strip_sum(feature_ref, strip, weight):
    return lax.dot_general(
        feature_ref[strip], weight, (((1,), (1,)), ((), ())), preferred_element_type=jnp.float32
    )


def mix_kernel(sources, feature_ref, *refs):
    piece_refs = refs[: len(sources)]
    keep_ref, send_ref, weight_ref = refs[len(sources) :]
    lat, lon = lax.axis_index("lat"), lax.axis_index("lon")
    odd = lon % 2
    masks = weight_ref.shape[0] // 2
    if sum(len(held) for _, held in sources) < 2 * masks:
        weight_ref[...] = jnp.zeros_like(weight_ref)
    for (core, held), ref in zip(sources, piece_refs):
        for at, mask in enumerate(held):
            place = (lat % 2 ^ core) * masks + ((lon // 2) ^ mask)
            weight_ref[place] = ref[at]
    weight = weight_ref[...].reshape(keep_ref.shape[1], weight_ref.shape[2])
    send_ref[...] = strip_sum(feature_ref, 1 - odd, weight).astype(send_ref.dtype)
    keep_ref[...] = strip_sum(feature_ref, odd, weight)


def rest_kernel(feature_ref, own_ref, crossed_ref, keep_ref, send_ref):
    odd = lax.axis_index("lon") % 2
    weight = jnp.concatenate([own_ref[0], crossed_ref[0]], axis=0)
    count = keep_ref.shape[0]
    for strip, ref in ((1 - odd, send_ref), (odd, keep_ref)):
        total = strip_sum(feature_ref, strip, weight)
        ref[...] = jnp.concatenate([total[:count], total[count:]], axis=1).astype(ref.dtype)


def finish_kernel(last, block, keep_ref, got_ref, keep2_ref, got2_ref, keep3_ref, got3_ref, bias_ref, out_ref):
    lat, lon = lax.axis_index("lat"), lax.axis_index("lon")
    wide = keep_ref.shape[1]

    def save(rows, at, total):
        at = pl.ds(pl.multiple_of(at, LANES), total.shape[1])
        total += bias_ref[:, at]
        grown = 0.5 * total * (1.0 + lax.erf(total * 0.5**0.5))
        out_ref[rows, at] = grown.astype(out_ref.dtype)

    save(slice(None), lat // 2 * wide, keep_ref[...] + got_ref[...].astype(jnp.float32))
    rest = keep3_ref[...] + got3_ref[...].astype(jnp.float32)
    count = rest.shape[0]
    lane = lane_of(rest)
    start = ((lon // 2) ^ last) * block
    inside = (lane >= start) & (lane < start + block)
    for crossed in range(2):
        core = lat % 2 ^ crossed
        at = pl.ds(pl.multiple_of(core * LANES, LANES), LANES)
        for part in range(2):
            rows = slice(part * count, (part + 1) * count)
            held = part * (2 * block) + crossed * block
            moved = pltpu.roll(rest, lax.rem(start - held + LANES, LANES), 1)
            total = keep2_ref[rows, at] + got2_ref[rows, at].astype(jnp.float32)
            total = jnp.where(inside, moved, total)
            save(rows, (1 - lat // 2) * wide + core * LANES, total)


def body(latent, filters, widths, mix_weight, mix_bias):
    lats, lons = lax.axis_size("lat"), lax.axis_size("lon")
    rows, columns, channels = latent.shape
    bases, _, span, taps = filters.shape
    radius, reach = span // 2, taps // 2
    assert reach == columns and rows % 2 == lats % 2 == lons % 2 == 0
    main = channels // (2 * LANES) * LANES
    assert channels == 2 * main + LANES + 1 and bases % 2 == 1
    assert bases <= HALF and rows + 2 * radius <= LANES
    half, packed = main + LANES, 2 * main + LANES
    out_columns, share = mix_bias.shape[0], mix_weight.shape[2]
    depth = bases // 2 * packed + half

    edge, halves = shape((radius, columns, channels)), shape((share, depth))
    weights = jnp.transpose(mix_weight, (0, 2, 1))
    own_weight, pair_weight, outer, inner = call(
        functools.partial(start_kernel, main), (halves, halves, edge, edge), [], weights, latent
    )
    got_weight = swap(pair_weight, 0, 1)
    from_outer = lax.ppermute(outer, AXES, route(outer_move))
    from_inner = swap(inner, 1, 0)
    block = shape((2 * share, depth))
    first = call(
        join_kernel, block, [], own_weight, got_weight, after=(from_outer, from_inner)
    )

    lon_masks, lat_masks = lons // 2, lats // 2
    steps = [1 << at for at in range(lat_masks.bit_length() - 1)]
    blocks = {(0, 0): first}
    bit = lon_masks // 2
    while bit:
        for low, mask in list(blocks):
            blocks[low, mask ^ bit] = swap(blocks[low, mask], 0, 2 * bit)
        bit //= 2
    order = [mask for _, mask in blocks]
    last = order[-1]
    for bit in steps:
        for low in range(bit):
            for mask in order[:-1]:
                blocks[low ^ bit, mask] = swap(blocks[low, mask], 2 * bit, 0)

    count = rows + 2 * radius
    strip = shape((columns, count // 2 * packed + LANES))
    mine, other = call(
        functools.partial(strip_kernel, main),
        (strip, strip),
        [pltpu.VMEM((count, columns, channels), jnp.bfloat16)],
        latent,
        from_outer,
        from_inner,
        after=tuple(blocks[bit, 0] for bit in steps),
    )
    pair_strip = swap(other, 0, 1)
    along = lax.ppermute(mine, AXES, route(along_move))
    across = lax.ppermute(other, AXES, route(across_move))
    deep = -(-(span + 1) * 3 * columns // LANES) * LANES
    band = call(
        functools.partial(band_kernel, reach),
        shape((rows // 2, 2 * bases * columns, deep)),
        [pltpu.VMEM((bases, rows, deep), jnp.float32)],
        jnp.transpose(filters, (0, 2, 1, 3)),
        widths,
        after=(mine,),
    )

    met = [value for key, value in blocks.items() if key != (0, last)]
    blocks[0, last] = call(
        copy_kernel, block, [], blocks[0, last], after=(*met, band, pair_strip, along, across)
    )
    for bit in steps:
        for low in range(bit):
            blocks[low ^ bit, last] = swap(blocks[low, last], 2 * bit, 0)
    features = call(
        functools.partial(feature_kernel, span),
        shape((2, rows, columns, depth)),
        [pltpu.VMEM((count, 4, columns, half), jnp.bfloat16)],
        band,
        mine,
        pair_strip,
        along,
        across,
        after=(blocks[0, last],),
    )
    features = features.reshape(2, rows * columns, depth)

    points, width = rows * columns, out_columns // lat_masks

    def stacked(low, held, after):
        piece = call(
            stack_kernel,
            shape((len(held),) + block.shape),
            [],
            *[blocks[low, mask] for mask in held],
            after=after,
        )
        return [piece, swap(piece, 1, 0)]

    def mixed(groups, pieces):
        sources = [(core, held) for held in groups for core in range(2)]
        keep, send = call(
            functools.partial(mix_kernel, sources),
            (shape((points, width), jnp.float32), shape((points, width))),
            [pltpu.VMEM((2 * lon_masks,) + block.shape, jnp.bfloat16)],
            features,
            *pieces,
        )
        return keep, swap(send, 0, 1)

    gate = (blocks[0, last],)
    if lat_masks == 2 and 8 * share == LANES == lon_masks * 2 * share and points % 2 == 0:
        parts = [*mixed([order], stacked(0, order, gate))]
        parts += mixed([order[:-1]], stacked(1, order[:-1], gate))
        rest = shape((points // 2, LANES), jnp.float32), shape((points // 2, LANES))
        keep, send = call(
            rest_kernel, rest, [], features, *stacked(1, order[-1:], (parts[2],))
        )
        out = call(
            functools.partial(finish_kernel, last, 2 * share),
            shape((points, out_columns)),
            [],
            *parts,
            keep,
            swap(send, 0, 1),
            mix_bias[None],
        )
        return out.reshape(rows, columns, out_columns)
    sums = []
    for low in range(lat_masks):
        keep, got = mixed([order], stacked(low, order, gate))
        sums.append(keep + got.astype(jnp.float32))
    total = jnp.stack(sums, 1)
    total = jnp.take(total, jnp.arange(lat_masks) ^ (lax.axis_index("lat") // 2), axis=1)
    total = total.reshape(rows, columns, out_columns) + mix_bias
    return jax.nn.gelu(total, approximate=False).astype(jnp.bfloat16)


def solution(mesh):
    placed = (
        P("lat", "lon", None),
        P(None, "lat", None, None),
        P("lat", None),
        P(None, None, ("lat", "lon")),
        P(),
    )
    return jax.shard_map(
        body, mesh=mesh, in_specs=placed, out_specs=P("lat", "lon", None), check_vma=False
    )
```

time: 61.9 us -> 57.9 us (0.935)
  waiting for transfers between devices: 25.8 us -> 17.8 us
  starting transfers between devices: 22.5 us -> 25 us
  local copies, waits for them, and re-layouts: 3.61 us -> 4.6 us
    ppermute x1, waiting for transfers between devices: 7.28 us -> 0.01 us  [body(): across = lax.ppermute(other, AXES, route(across_move))]
    ppermute x1, waiting for transfers between devices: 2.42 us -> 0.01 us  [body(): along = lax.ppermute(mine, AXES, route(along_move))]
    ppermute x15 -> x16, waiting for transfers between devices: 13.2 us -> 14.9 us  [swap(): lax.ppermute(block, AXES, route(lambda lat, lon, lats, lons: (lat ^ lat_b...]
    ppermute x15 -> x16, starting transfers between devices: 15.4 us -> 17 us  [swap(): lax.ppermute(block, AXES, route(lambda lat, lon, lats, lons: (lat ^ lat_b...]
    ppermute x1, starting transfers between devices: 0.06 us -> 1.44 us  [body(): along = lax.ppermute(mine, AXES, route(along_move))]
    unnamed x10 -> x12, local copies, waits for them, and re-layouts: 3.61 us -> 4.6 us
    pallas_call x11 -> x13, Pallas kernels: 9.69 us -> 10.1 us  [call(): pl.pallas_call(ordered, out_shape=outs, in_specs=[held] * count + [pl.Blo...]
  transfers between devices with their start and end apart: 18 -> 19, of which waited for: 9 -> 7; matrix products, arithmetic and copies ran while one was open for 0% -> 0% of each run, Pallas kernels for 13% -> 16%
where the time goes in v3:
time: 57.9 us; the launch traced here: 57.6 us
  starting transfers between devices  25 us (43%)
  waiting for transfers between devices  17.8 us (31%)
  Pallas kernels  10.1 us (17%)
  local copies, waits for them, and re-layouts  4.6 us (8%)
    ppermute x16, starting transfers between devices, swap(): lax.ppermute(block, AXES, route(lambda lat, lon, lats, lons: (lat ^ lat_b...  17 us
    ppermute x16, waiting for transfers between devices, swap(): lax.ppermute(block, AXES, route(lambda lat, lon, lats, lons: (lat ^ lat_b...  14.9 us
    pallas_call x13, Pallas kernels, call(): pl.pallas_call(ordered, out_shape=outs, in_specs=[held] * count + [pl.Blo...  10.1 us
    unnamed x12, local copies, waits for them, and re-layouts  4.6 us
    ppermute x1, starting transfers between devices, body(): across = lax.ppermute(other, AXES, route(across_move))  3.91 us
    ppermute x1, waiting for transfers between devices, body(): from_outer = lax.ppermute(outer, AXES, route(outer_move))  2.93 us
    ppermute x1, starting transfers between devices, body(): from_outer = lax.ppermute(outer, AXES, route(outer_move))  2.59 us
    ppermute x1, starting transfers between devices, body(): along = lax.ppermute(mine, AXES, route(along_move))  1.44 us
  transfers between devices with their start and end apart: 19, of which 7 were waited for; matrix products, arithmetic and copies ran while one was open for 0% of the time, Pallas kernels for 16%

profile of v3, /device:TPU:0, one launch (start us, length us, event | category | flops | bytes accessed | tf_op | source)
XLA Modules:
  0.0 57.6 jit_solution(3387086825468482907)
XLA Ops:
  0.0 1.0 %copy-done = bf16[16,16,641]{2,1,0:T(8,128)(2,1)S(1)} copy-done((bf16[16,16,641]{2,1,0:T(8,128)(2,1)S(1)}, bf16[16,16,641]{2,1,0:T(8,128)(2,1)}, u32[]{:S(2)}) %copy-start) | copy-done | bytes 328216
  1.0 0.9 %copy-done.3 = bf16[9,641,16]{1,2,0:T(8,128)(2,1)S(1)} copy-done((bf16[9,641,16]{1,2,0:T(8,128)(2,1)S(1)}, bf16[9,641,16]{1,2,0:T(8,128)(2,1)}, u32[]{:S(2)}) %copy-start.3) | copy-done | bytes 184632
  2.0 3.0 %collective-permute-start.2 = (bf16[16,2944]{1,0:T(8,128)(2,1)S(1)}, bf16[16,2944]{1,0:T(8,128)(2,1)S(1)}, u32[]{:S(2)}, u32[]{:S(2)}) collective-permute-start(bf16[16,2944]{1,0:T(8,128)(2,1)S(1)} %get-tuple-element.20), channel_id=1, source_target_pairs={{0,1},{1,0},{2,3},{3,2},{4,5},{5,4},{6,7},{7,6},{8,9},{9,8},{10,11... | collective-permute-start | bytes 282632 | tf_op jit(solution)/shard_map/ppermute | solution.py:49
  5.1 2.6 %collective-permute-start = (bf16[4,16,641]{2,1,0:T(8,128)(2,1)S(1)}, bf16[4,16,641]{2,1,0:T(8,128)(2,1)S(1)}, u32[]{:S(2)}, u32[]{:S(2)}) collective-permute-start(bf16[4,16,641]{2,1,0:T(8,128)(2,1)S(1)} %get-tuple-element.17), channel_id=1, source_target_pairs={{0,4},{1,5},{2,6},{3,7},{4,0},{5,1},{6,2},{7,3},{8,16},{9,17},{10,... | collective-permute-start | bytes 246152 | tf_op jit(solution)/shard_map/ppermute | solution.py:333
  7.7 2.9 %collective-permute-done.refs_2_.refs_1_ = bf16[4,16,641]{2,1,0:T(8,128)(2,1)S(1)} collective-permute-done((bf16[4,16,641]{2,1,0:T(8,128)(2,1)S(1)}, bf16[4,16,641]{2,1,0:T(8,128)(2,1)S(1)}, u32[]{:S(2)}, u32[]{:S(2)}) %collective-permute-start) | collective-permute-done | bytes 82080 | tf_op jit(solution)/shard_map/ppermute | solution.py:333
  10.6 1.8 %collective-permute-start.9 = (bf16[32,2944]{1,0:T(8,128)(2,1)S(1)}, bf16[32,2944]{1,0:T(8,128)(2,1)S(1)}, u32[]{:S(2)}, u32[]{:S(2)}) collective-permute-start(bf16[32,2944]{1,0:T(8,128)(2,1)S(1)} %shard_map.56.refs_1_.refs_0_), channel_id=1, source_target_pairs={{0,2},{1,3},{2,0},{3,1},{4,6},{5,7},{6,4},{7,5},{8,10},{9,11},{10,... | collective-permute-start | bytes 565256 | tf_op jit(solution)/shard_map/ppermute | solution.py:49
  12.4 3.4 %collective-permute-start.7 = (bf16[32,2944]{1,0:T(8,128)(2,1)S(1)}, bf16[32,2944]{1,0:T(8,128)(2,1)S(1)}, u32[]{:S(2)}, u32[]{:S(2)}) collective-permute-start(bf16[32,2944]{1,0:T(8,128)(2,1)S(1)} %shard_map.56.refs_1_.refs_0_), channel_id=1, source_target_pairs={{0,4},{1,5},{2,6},{3,7},{4,0},{5,1},{6,2},{7,3},{8,12},{9,13},{10,... | collective-permute-start | bytes 565256 | tf_op jit(solution)/shard_map/ppermute | solution.py:49
  15.8 0.5 collective-permute-done.9.refs_3_.refs_2_
  16.3 3.7 %collective-permute-start.11 = (bf16[32,2944]{1,0:T(8,128)(2,1)S(1)}, bf16[32,2944]{1,0:T(8,128)(2,1)S(1)}, u32[]{:S(2)}, u32[]{:S(2)}) collective-permute-start(bf16[32,2944]{1,0:T(8,128)(2,1)S(1)} %collective-permute-done.9.refs_3_.refs_2_), channel_id=1, source_target_pairs={{0,16},{1,17},{2,18},{3,19},{4,20},{5,21},{6,22},{7,23},{8,24},{9,... | collective-permute-start | bytes 565256 | tf_op jit(solution)/shard_map/ppermute | solution.py:49
  20.0 1.0 %copy-done.1 = bf16[16,16,641]{2,1,0:T(8,128)(2,1)S(1)} copy-done((bf16[16,16,641]{2,1,0:T(8,128)(2,1)S(1)}, bf16[16,16,641]{2,1,0:T(8,128)(2,1)}, u32[]{:S(2)}) %copy-start.1) | copy-done | bytes 328216
  21.0 0.2 shard_map.57
  21.2 3.9 %collective-permute-start.6 = (bf16[16,7808]{1,0:T(8,128)(2,1)S(1)}, bf16[16,7808]{1,0:T(8,128)(2,1)S(1)}, u32[]{:S(2)}, u32[]{:S(2)}) collective-permute-start(bf16[16,7808]{1,0:T(8,128)(2,1)S(1)} %get-tuple-element.22), channel_id=1, source_target_pairs={{0,7},{1,2},{2,1},{3,4},{4,3},{5,6},{6,5},{7,0},{8,15},{9,10},{10,... | collective-permute-start | bytes 749576 | tf_op jit(solution)/shard_map/ppermute | solution.py:368
  25.1 1.4 %collective-permute-start.5 = (bf16[16,7808]{1,0:T(8,128)(2,1)S(1)}, bf16[16,7808]{1,0:T(8,128)(2,1)S(1)}, u32[]{:S(2)}, u32[]{:S(2)}) collective-permute-start(bf16[16,7808]{1,0:T(8,128)(2,1)S(1)} %get-tuple-element.21.refs_2_.refs_1_), channel_id=1, source_target_pairs={{0,6},{1,3},{2,0},{3,5},{4,2},{5,7},{6,4},{7,1},{8,14},{9,11},{10,... | collective-permute-start | bytes 749576 | tf_op jit(solution)/shard_map/ppermute | solution.py:367
  26.6 0.6 %collective-permute-start.8 = (bf16[32,2944]{1,0:T(8,128)(2,1)S(1)}, bf16[32,2944]{1,0:T(8,128)(2,1)S(1)}, u32[]{:S(2)}, u32[]{:S(2)}) collective-permute-start(bf16[32,2944]{1,0:T(8,128)(2,1)S(1)} %collective-permute-done.7.refs_2_.refs_1_), channel_id=1, source_target_pairs={{0,2},{1,3},{2,0},{3,1},{4,6},{5,7},{6,4},{7,5},{8,10},{9,11},{10,... | collective-permute-start | bytes 565256 | tf_op jit(solution)/shard_map/ppermute | solution.py:49
  27.2 1.0 %copy-done.2 = bf16[9,16,9,33]{3,1,2,0:T(8,128)(2,1)S(1)} copy-done((bf16[9,16,9,33]{3,1,2,0:T(8,128)(2,1)S(1)}, bf16[9,16,9,33]{3,1,2,0:T(8,128)(2,1)}, u32[]{:S(2)}) %copy-start.2) | copy-done | bytes 85560
  28.2 0.7 %copy-done.4 = s32[16,9]{1,0:T(8,128)S(1)} copy-done((s32[16,9]{1,0:T(8,128)S(1)}, s32[16,9]{1,0:T(8,128)}, u32[]{:S(2)}) %copy-start.4) | copy-done | bytes 600
  28.9 1.4 %shard_map.58.refs_7_.refs_0_ = bf16[8,288,512]{2,1,0:T(8,128)(2,1)S(1)} custom-call(bf16[9,9,16,33]{3,2,1,0:T(8,128)(2,1)S(1)} %bitcast.8, s32[16,9]{1,0:T(8,128)S(1)} %copy-done.4, bf16[16,7808]{1,0:T(8,128)(2,1)S(1)} %get-tuple-element.21.refs_2_.refs_1_), custom_call_target="tpu_custom_call" | custom-call | tf_op jit(solution)/shard_map/pallas_call | solution.py:24
  30.3 1.9 %collective-permute-done.10.refs_5_.refs_1_ = bf16[32,2944]{1,0:T(8,128)(2,1)S(1)} collective-permute-done((bf16[32,2944]{1,0:T(8,128)(2,1)S(1)}, bf16[32,2944]{1,0:T(8,128)(2,1)S(1)}, u32[]{:S(2)}, u32[]{:S(2)}) %collective-permute-start.10) | collective-permute-done | bytes 188448 | tf_op jit(solution)/shard_map/ppermute | solution.py:49
  32.1 7.5 %collective-permute-done.8.refs_0_ = bf16[32,2944]{1,0:T(8,128)(2,1)S(1)} collective-permute-done((bf16[32,2944]{1,0:T(8,128)(2,1)S(1)}, bf16[32,2944]{1,0:T(8,128)(2,1)S(1)}, u32[]{:S(2)}, u32[]{:S(2)}) %collective-permute-start.8) | collective-permute-done | bytes 188448 | tf_op jit(solution)/shard_map/ppermute | solution.py:49
  39.9 0.6 collective-permute-start.14
  40.4 0.3 collective-permute-start.16
  40.7 4.0 %shard_map.60 = bf16[2,16,16,2944]{3,2,1,0:T(8,128)(2,1)S(1)} custom-call(bf16[8,288,512]{2,1,0:T(8,128)(2,1)S(1)} %shard_map.58.refs_7_.refs_0_, bf16[16,7808]{1,0:T(8,128)(2,1)S(1)} %get-tuple-element.21.refs_2_.refs_1_, bf16[16,7808]{1,0:T(8,128)(2,1)S(1)} %collective-permute-done.4.refs_8_.refs_2_, ...), custom_call_target="tpu_custom_call" | custom-call | tf_op jit(solution)/shard_map/pallas_call | solution.py:24
  44.8 1.2 %shard_map.64 = (f32[256,256]{1,0:T(8,128)S(1)}, bf16[256,256]{1,0:T(8,128)(2,1)S(1)}) custom-call(bf16[2,256,2944]{2,1,0:T(8,128)(2,1)S(1)} %bitcast.5, bf16[3,32,2944]{2,1,0:T(8,128)(2,1)S(1)} %shard_map.63.refs_1_, bf16[3,32,2944]{2,1,0:T(8,128)(2,1)S(1)} %collective-permute-done.14.refs_2_), custom_call_target="tpu_custom_call" | custom-call | tf_op jit(solution)/shard_map/pallas_call | solution.py:24
  46.0 1.2 %collective-permute-done.16.refs_0_ = bf16[32,2944]{1,0:T(8,128)(2,1)S(1)} collective-permute-done((bf16[32,2944]{1,0:T(8,128)(2,1)S(1)}, bf16[32,2944]{1,0:T(8,128)(2,1)S(1)}, u32[]{:S(2)}, u32[]{:S(2)}) %collective-permute-start.16) | collective-permute-done | bytes 188448 | tf_op jit(solution)/shard_map/ppermute | solution.py:49
  47.3 1.3 %collective-permute-start.15 = (bf16[256,256]{1,0:T(8,128)(2,1)S(1)}, bf16[256,256]{1,0:T(8,128)(2,1)S(1)}, u32[]{:S(2)}, u32[]{:S(2)}) collective-permute-start(bf16[256,256]{1,0:T(8,128)(2,1)S(1)} %get-tuple-element.26), channel_id=1, source_target_pairs={{0,1},{1,0},{2,3},{3,2},{4,5},{5,4},{6,7},{7,6},{8,9},{9,8},{10,11... | collective-permute-start | bytes 393224 | tf_op jit(solution)/shard_map/ppermute | solution.py:49
  48.6 1.1 %shard_map.62 = (f32[256,256]{1,0:T(8,128)S(1)}, bf16[256,256]{1,0:T(8,128)(2,1)S(1)}) custom-call(bf16[2,256,2944]{2,1,0:T(8,128)(2,1)S(1)} %bitcast.6, bf16[4,32,2944]{2,1,0:T(8,128)(2,1)S(1)} %shard_map.61.refs_1_, bf16[4,32,2944]{2,1,0:T(8,128)(2,1)S(1)} %collective-permute-done.12.refs_2_), custom_call_target="tpu_custom_call" | custom-call | tf_op jit(solution)/shard_map/pallas_call | solution.py:24
  49.7 0.8 %collective-permute-start.13 = (bf16[256,256]{1,0:T(8,128)(2,1)S(1)}, bf16[256,256]{1,0:T(8,128)(2,1)S(1)}, u32[]{:S(2)}, u32[]{:S(2)}) collective-permute-start(bf16[256,256]{1,0:T(8,128)(2,1)S(1)} %get-tuple-element.24), channel_id=1, source_target_pairs={{0,1},{1,0},{2,3},{3,2},{4,5},{5,4},{6,7},{7,6},{8,9},{9,8},{10,11... | collective-permute-start | bytes 393224 | tf_op jit(solution)/shard_map/ppermute | solution.py:49
  50.6 1.0 %shard_map.66 = (f32[128,128]{1,0:T(8,128)S(1)}, bf16[128,128]{1,0:T(8,128)(2,1)S(1)}) custom-call(bf16[2,256,2944]{2,1,0:T(8,128)(2,1)S(1)} %bitcast.7, bf16[1,32,2944]{2,1,0:T(8,128)(2,1)S(1)} %shard_map.65.refs_1_, bf16[1,32,2944]{2,1,0:T(8,128)(2,1)S(1)} %collective-permute-done.17.refs_2_), custom_call_target="tpu_custom_call" | custom-call | tf_op jit(solution)/shard_map/pallas_call | solution.py:24
  51.6 1.3 %collective-permute-start.18 = (bf16[128,128]{1,0:T(8,128)(2,1)S(1)}, bf16[128,128]{1,0:T(8,128)(2,1)S(1)}, u32[]{:S(2)}, u32[]{:S(2)}) collective-permute-start(bf16[128,128]{1,0:T(8,128)(2,1)S(1)} %get-tuple-element.28), channel_id=1, source_target_pairs={{0,1},{1,0},{2,3},{3,2},{4,5},{5,4},{6,7},{7,6},{8,9},{9,8},{10,11... | collective-permute-start | bytes 98312 | tf_op jit(solution)/shard_map/ppermute | solution.py:49
  52.9 0.7 %collective-permute-done.15.refs_3_ = bf16[256,256]{1,0:T(8,128)(2,1)S(1)} collective-permute-done((bf16[256,256]{1,0:T(8,128)(2,1)S(1)}, bf16[256,256]{1,0:T(8,128)(2,1)S(1)}, u32[]{:S(2)}, u32[]{:S(2)}) %collective-permute-start.15) | collective-permute-done | bytes 131104 | tf_op jit(solution)/shard_map/ppermute | solution.py:49
  53.6 3.0 %collective-permute-done.18.refs_5_ = bf16[128,128]{1,0:T(8,128)(2,1)S(1)} collective-permute-done((bf16[128,128]{1,0:T(8,128)(2,1)S(1)}, bf16[128,128]{1,0:T(8,128)(2,1)S(1)}, u32[]{:S(2)}, u32[]{:S(2)}) %collective-permute-start.18) | collective-permute-done | bytes 32800 | tf_op jit(solution)/shard_map/ppermute | solution.py:49
  56.7 0.9 %shard_map.67 = bf16[256,512]{1,0:T(8,128)(2,1)} custom-call(f32[256,256]{1,0:T(8,128)S(1)} %get-tuple-element.23.refs_0_, bf16[256,256]{1,0:T(8,128)(2,1)S(1)} %collective-permute-done.13.refs_1_, f32[256,256]{1,0:T(8,128)S(1)} %get-tuple-element.25.refs_1_.refs_2_, bf16[256,256]{1,0:T(8,128)(2,1)S(1)} %collective-permute-done.15.refs_3_, ...), custom_call_target="tpu_custom_call" | custom-call | tf_op jit(solution)/shard_map/pallas_call | solution.py:24
  (31 shorter events, 0.5 us)
Async XLA Ops:
  0.0 1.0 %copy-start = (bf16[16,16,641]{2,1,0:T(8,128)(2,1)S(1)}, bf16[16,16,641]{2,1,0:T(8,128)(2,1)}, u32[]{:S(2)}) copy-start(bf16[16,16,641]{2,1,0:T(8,128)(2,1)} %refs_0_.1) | copy-start | bytes 984580
  1.0 0.9 %copy-start.3 = (bf16[9,641,16]{1,2,0:T(8,128)(2,1)S(1)}, bf16[9,641,16]{1,2,0:T(8,128)(2,1)}, u32[]{:S(2)}) copy-start(bf16[9,641,16]{1,2,0:T(8,128)(2,1)} %param.8) | copy-start | bytes 553828
  2.0 8.6 %collective-permute-start.2 = (bf16[16,2944]{1,0:T(8,128)(2,1)S(1)}, bf16[16,2944]{1,0:T(8,128)(2,1)S(1)}, u32[]{:S(2)}, u32[]{:S(2)}) collective-permute-start(bf16[16,2944]{1,0:T(8,128)(2,1)S(1)} %get-tuple-element.20), channel_id=1, source_target_pairs={{0,1},{1,0},{2,3},{3,2},{4,5},{5,4},{6,7},{7,6},{8,9},{9,8},{10,11... | collective-permute-start | bytes 282632 | tf_op jit(solution)/shard_map/ppermute | solution.py:49
  5.1 5.5 %collective-permute-start = (bf16[4,16,641]{2,1,0:T(8,128)(2,1)S(1)}, bf16[4,16,641]{2,1,0:T(8,128)(2,1)S(1)}, u32[]{:S(2)}, u32[]{:S(2)}) collective-permute-start(bf16[4,16,641]{2,1,0:T(8,128)(2,1)S(1)} %get-tuple-element.17), channel_id=1, source_target_pairs={{0,4},{1,5},{2,6},{3,7},{4,0},{5,1},{6,2},{7,3},{8,16},{9,17},{10,... | collective-permute-start | bytes 246152 | tf_op jit(solution)/shard_map/ppermute | solution.py:333
  7.7 2.9 %collective-permute-start.1 = (bf16[4,16,641]{2,1,0:T(8,128)(2,1)S(1)}, bf16[4,16,641]{2,1,0:T(8,128)(2,1)S(1)}, u32[]{:S(2)}, u32[]{:S(2)}) collective-permute-start(bf16[4,16,641]{2,1,0:T(8,128)(2,1)S(1)} %get-tuple-element.18), channel_id=1, source_target_pairs={{0,8},{1,9},{2,10},{3,11},{4,12},{5,13},{6,14},{7,15},{8,0},{9,1},... | collective-permute-start | bytes 246152 | tf_op jit(solution)/shard_map/ppermute | solution.py:49
  10.6 5.7 %collective-permute-start.9 = (bf16[32,2944]{1,0:T(8,128)(2,1)S(1)}, bf16[32,2944]{1,0:T(8,128)(2,1)S(1)}, u32[]{:S(2)}, u32[]{:S(2)}) collective-permute-start(bf16[32,2944]{1,0:T(8,128)(2,1)S(1)} %shard_map.56.refs_1_.refs_0_), channel_id=1, source_target_pairs={{0,2},{1,3},{2,0},{3,1},{4,6},{5,7},{6,4},{7,5},{8,10},{9,11},{10,... | collective-permute-start | bytes 565256 | tf_op jit(solution)/shard_map/ppermute | solution.py:49
  12.4 7.6 %collective-permute-start.3 = (bf16[32,2944]{1,0:T(8,128)(2,1)S(1)}, bf16[32,2944]{1,0:T(8,128)(2,1)S(1)}, u32[]{:S(2)}, u32[]{:S(2)}) collective-permute-start(bf16[32,2944]{1,0:T(8,128)(2,1)S(1)} %shard_map.56.refs_1_.refs_0_), channel_id=1, source_target_pairs={{0,16},{1,17},{2,18},{3,19},{4,20},{5,21},{6,22},{7,23},{8,24},{9,... | collective-permute-start | bytes 565256 | tf_op jit(solution)/shard_map/ppermute | solution.py:49
  12.4 14.1 %collective-permute-start.7 = (bf16[32,2944]{1,0:T(8,128)(2,1)S(1)}, bf16[32,2944]{1,0:T(8,128)(2,1)S(1)}, u32[]{:S(2)}, u32[]{:S(2)}) collective-permute-start(bf16[32,2944]{1,0:T(8,128)(2,1)S(1)} %shard_map.56.refs_1_.refs_0_), channel_id=1, source_target_pairs={{0,4},{1,5},{2,6},{3,7},{4,0},{5,1},{6,2},{7,3},{8,12},{9,13},{10,... | collective-permute-start | bytes 565256 | tf_op jit(solution)/shard_map/ppermute | solution.py:49
  16.3 10.3 %collective-permute-start.11 = (bf16[32,2944]{1,0:T(8,128)(2,1)S(1)}, bf16[32,2944]{1,0:T(8,128)(2,1)S(1)}, u32[]{:S(2)}, u32[]{:S(2)}) collective-permute-start(bf16[32,2944]{1,0:T(8,128)(2,1)S(1)} %collective-permute-done.9.refs_3_.refs_2_), channel_id=1, source_target_pairs={{0,16},{1,17},{2,18},{3,19},{4,20},{5,21},{6,22},{7,23},{8,24},{9,... | collective-permute-start | bytes 565256 | tf_op jit(solution)/shard_map/ppermute | solution.py:49
  20.0 1.0 %copy-start.1 = (bf16[16,16,641]{2,1,0:T(8,128)(2,1)S(1)}, bf16[16,16,641]{2,1,0:T(8,128)(2,1)}, u32[]{:S(2)}) copy-start(bf16[16,16,641]{2,1,0:T(8,128)(2,1)} %refs_0_.1) | copy-start | bytes 984580
  21.2 18.5 %collective-permute-start.6 = (bf16[16,7808]{1,0:T(8,128)(2,1)S(1)}, bf16[16,7808]{1,0:T(8,128)(2,1)S(1)}, u32[]{:S(2)}, u32[]{:S(2)}) collective-permute-start(bf16[16,7808]{1,0:T(8,128)(2,1)S(1)} %get-tuple-element.22), channel_id=1, source_target_pairs={{0,7},{1,2},{2,1},{3,4},{4,3},{5,6},{6,5},{7,0},{8,15},{9,10},{10,... | collective-permute-start | bytes 749576 | tf_op jit(solution)/shard_map/ppermute | solution.py:368
  25.1 14.6 %collective-permute-start.4 = (bf16[16,7808]{1,0:T(8,128)(2,1)S(1)}, bf16[16,7808]{1,0:T(8,128)(2,1)S(1)}, u32[]{:S(2)}, u32[]{:S(2)}) collective-permute-start(bf16[16,7808]{1,0:T(8,128)(2,1)S(1)} %get-tuple-element.22), channel_id=1, source_target_pairs={{0,1},{1,0},{2,3},{3,2},{4,5},{5,4},{6,7},{7,6},{8,9},{9,8},{10,11... | collective-permute-start | bytes 749576 | tf_op jit(solution)/shard_map/ppermute | solution.py:49
  25.1 14.6 %collective-permute-start.5 = (bf16[16,7808]{1,0:T(8,128)(2,1)S(1)}, bf16[16,7808]{1,0:T(8,128)(2,1)S(1)}, u32[]{:S(2)}, u32[]{:S(2)}) collective-permute-start(bf16[16,7808]{1,0:T(8,128)(2,1)S(1)} %get-tuple-element.21.refs_2_.refs_1_), channel_id=1, source_target_pairs={{0,6},{1,3},{2,0},{3,5},{4,2},{5,7},{6,4},{7,1},{8,14},{9,11},{10,... | collective-permute-start | bytes 749576 | tf_op jit(solution)/shard_map/ppermute | solution.py:367
  26.6 5.6 %collective-permute-start.10 = (bf16[32,2944]{1,0:T(8,128)(2,1)S(1)}, bf16[32,2944]{1,0:T(8,128)(2,1)S(1)}, u32[]{:S(2)}, u32[]{:S(2)}) collective-permute-start(bf16[32,2944]{1,0:T(8,128)(2,1)S(1)} %collective-permute-done.7.refs_2_.refs_1_), channel_id=1, source_target_pairs={{0,16},{1,17},{2,18},{3,19},{4,20},{5,21},{6,22},{7,23},{8,24},{9,... | collective-permute-start | bytes 565256 | tf_op jit(solution)/shard_map/ppermute | solution.py:49
  26.6 13.0 %collective-permute-start.8 = (bf16[32,2944]{1,0:T(8,128)(2,1)S(1)}, bf16[32,2944]{1,0:T(8,128)(2,1)S(1)}, u32[]{:S(2)}, u32[]{:S(2)}) collective-permute-start(bf16[32,2944]{1,0:T(8,128)(2,1)S(1)} %collective-permute-done.7.refs_2_.refs_1_), channel_id=1, source_target_pairs={{0,2},{1,3},{2,0},{3,1},{4,6},{5,7},{6,4},{7,5},{8,10},{9,11},{10,... | collective-permute-start | bytes 565256 | tf_op jit(solution)/shard_map/ppermute | solution.py:49
  27.2 1.0 %copy-start.2 = (bf16[9,16,9,33]{3,1,2,0:T(8,128)(2,1)S(1)}, bf16[9,16,9,33]{3,1,2,0:T(8,128)(2,1)}, u32[]{:S(2)}) copy-start(bf16[9,16,9,33]{3,1,2,0:T(8,128)(2,1)} %param.6) | copy-start | bytes 256612
  28.2 0.7 %copy-start.4 = (s32[16,9]{1,0:T(8,128)S(1)}, s32[16,9]{1,0:T(8,128)}, u32[]{:S(2)}) copy-start(s32[16,9]{1,0:T(8,128)} %refs_1_.3) | copy-start | bytes 1732
  39.8 8.8 %collective-permute-start.12 = (bf16[4,32,2944]{2,1,0:T(8,128)(2,1)S(1)}, bf16[4,32,2944]{2,1,0:T(8,128)(2,1)S(1)}, u32[]{:S(2)}, u32[]{:S(2)}) collective-permute-start(bf16[4,32,2944]{2,1,0:T(8,128)(2,1)S(1)} %shard_map.61.refs_1_), channel_id=1, source_target_pairs={{0,8},{1,9},{2,10},{3,11},{4,12},{5,13},{6,14},{7,15},{8,0},{9,1},... | collective-permute-start | bytes 2261000 | tf_op jit(solution)/shard_map/ppermute | solution.py:49
  39.9 4.9 %collective-permute-start.14 = (bf16[3,32,2944]{2,1,0:T(8,128)(2,1)S(1)}, bf16[3,32,2944]{2,1,0:T(8,128)(2,1)S(1)}, u32[]{:S(2)}, u32[]{:S(2)}) collective-permute-start(bf16[3,32,2944]{2,1,0:T(8,128)(2,1)S(1)} %shard_map.63.refs_1_), channel_id=1, source_target_pairs={{0,8},{1,9},{2,10},{3,11},{4,12},{5,13},{6,14},{7,15},{8,0},{9,1},... | collective-permute-start | bytes 1695752 | tf_op jit(solution)/shard_map/ppermute | solution.py:49
  40.4 6.7 %collective-permute-start.16 = (bf16[32,2944]{1,0:T(8,128)(2,1)S(1)}, bf16[32,2944]{1,0:T(8,128)(2,1)S(1)}, u32[]{:S(2)}, u32[]{:S(2)}) collective-permute-start(bf16[32,2944]{1,0:T(8,128)(2,1)S(1)} %shard_map.59.refs_5_.refs_3_.refs_4_), channel_id=1, source_target_pairs={{0,16},{1,17},{2,18},{3,19},{4,20},{5,21},{6,22},{7,23},{8,24},{9,... | collective-permute-start | bytes 565256 | tf_op jit(solution)/shard_map/ppermute | solution.py:49
  47.2 3.4 %collective-permute-start.17 = (bf16[1,32,2944]{2,1,0:T(8,128)(2,1)S(1)}, bf16[1,32,2944]{2,1,0:T(8,128)(2,1)S(1)}, u32[]{:S(2)}, u32[]{:S(2)}) collective-permute-start(bf16[1,32,2944]{2,1,0:T(8,128)(2,1)S(1)} %shard_map.65.refs_1_), channel_id=1, source_target_pairs={{0,8},{1,9},{2,10},{3,11},{4,12},{5,13},{6,14},{7,15},{8,0},{9,1},... | collective-permute-start | bytes 565256 | tf_op jit(solution)/shard_map/ppermute | solution.py:49
  47.2 9.4 %copy-start.5 = (f32[512]{0:T(512)S(1)}, f32[512]{0:T(512)}, u32[]{:S(2)}) copy-start(f32[512]{0:T(512)} %param.9) | copy-start | bytes 6148
  47.3 6.4 %collective-permute-start.15 = (bf16[256,256]{1,0:T(8,128)(2,1)S(1)}, bf16[256,256]{1,0:T(8,128)(2,1)S(1)}, u32[]{:S(2)}, u32[]{:S(2)}) collective-permute-start(bf16[256,256]{1,0:T(8,128)(2,1)S(1)} %get-tuple-element.26), channel_id=1, source_target_pairs={{0,1},{1,0},{2,3},{3,2},{4,5},{5,4},{6,7},{7,6},{8,9},{9,8},{10,11... | collective-permute-start | bytes 393224 | tf_op jit(solution)/shard_map/ppermute | solution.py:49
  49.7 6.9 %collective-permute-start.13 = (bf16[256,256]{1,0:T(8,128)(2,1)S(1)}, bf16[256,256]{1,0:T(8,128)(2,1)S(1)}, u32[]{:S(2)}, u32[]{:S(2)}) collective-permute-start(bf16[256,256]{1,0:T(8,128)(2,1)S(1)} %get-tuple-element.24), channel_id=1, source_target_pairs={{0,1},{1,0},{2,3},{3,2},{4,5},{5,4},{6,7},{7,6},{8,9},{9,8},{10,11... | collective-permute-start | bytes 393224 | tf_op jit(solution)/shard_map/ppermute | solution.py:49
  51.6 5.1 %collective-permute-start.18 = (bf16[128,128]{1,0:T(8,128)(2,1)S(1)}, bf16[128,128]{1,0:T(8,128)(2,1)S(1)}, u32[]{:S(2)}, u32[]{:S(2)}) collective-permute-start(bf16[128,128]{1,0:T(8,128)(2,1)S(1)} %get-tuple-element.28), channel_id=1, source_target_pairs={{0,1},{1,0},{2,3},{3,2},{4,5},{5,4},{6,7},{7,6},{8,9},{9,8},{10,11... | collective-permute-start | bytes 98312 | tf_op jit(solution)/shard_map/ppermute | solution.py:49

commit v4 on v3

--- a/solution.py
+++ b/solution.py
@@ -106,7 +106,7 @@
     return tile
 
 
-def start_kernel(main, w_ref, x_ref, own_ref, pair_ref, outer_ref, inner_ref):
+def weight_kernel(main, w_ref, own_ref, pair_ref):
     odd = lax.axis_index("lon") % 2
     refs = own_ref, pair_ref
     bases = w_ref.shape[0]
@@ -119,22 +119,27 @@
     front = lane_of(tile) < HALF
     low, high = jnp.where(front, tile, 0.0), jnp.where(front, turned(tile, HALF), 0.0)
     put(refs, odd, at + main, low, spare_of(high, values, main, HALF))
+
+
+def edge_kernel(x_ref, outer_ref, held_ref):
     radius = outer_ref.shape[0]
     lower = lax.axis_index("lat") % 2
-    low, high = x_ref[:radius], x_ref[-radius:]
-    outer_ref[...] = jnp.where(lower == 1, high, low)
-    inner_ref[...] = jnp.where(lower == 1, low, high)
-
-
-def strip_kernel(main, x_ref, outer_ref, inner_ref, mine_ref, other_ref, rows_ref):
+    outer_ref[...] = jnp.where(lower == 1, x_ref[-radius:], x_ref[:radius])
+    held_ref[...] = x_ref[...]
+
+
+def start_kernel(main, w_ref, x_ref, own_ref, pair_ref, outer_ref, held_ref):
+    weight_kernel(main, w_ref, own_ref, pair_ref)
+    edge_kernel(x_ref, outer_ref, held_ref)
+
+
+def strip_kernel(main, x_ref, outer_ref, mine_ref, other_ref, rows_ref):
     lat, odd = lax.axis_index("lat"), lax.axis_index("lon") % 2
     pole = (lat == 0) | (lat == lax.axis_size("lat") - 1)
     radius, rows = outer_ref.shape[0], x_ref.shape[0]
-    rows_ref[radius : radius + rows] = x_ref[...]
-    far = radius + rows
+    rows_ref[pl.ds((1 - lat % 2) * radius, rows)] = x_ref[...]
     for r in range(radius):
-        rows_ref[lat % 2 * far + r] = outer_ref[jnp.where(pole, radius - 1 - r, r)]
-        rows_ref[(1 - lat % 2) * far + r] = inner_ref[r]
+        rows_ref[lat % 2 * rows + r] = outer_ref[jnp.where(pole, radius - 1 - r, r)]
     refs = mine_ref, other_ref
     count = rows_ref.shape[0]
     values = [rows_ref[r] for r in range(count)]
@@ -202,15 +207,26 @@
             slab_ref[row, slot, :, main:] = third.astype(jnp.bfloat16)
 
 
-def feature_kernel(span, band_ref, mine_ref, pair_ref, along_ref, across_ref, out_ref, slab_ref):
+def slab_kernel(mine_ref, pair_ref, along_ref, across_ref, slab_ref, inner_ref):
     odd = lax.axis_index("lon") % 2
-    strips, rows, columns, _ = out_ref.shape
-    half = slab_ref.shape[3]
-    main = half - LANES
+    main = slab_ref.shape[3] - LANES
     unpack(mine_ref, slab_ref, 1 + odd, main)
     unpack(pair_ref, slab_ref, 2 - odd, main)
     unpack(along_ref, slab_ref, 3 * (1 - odd), main)
     unpack(across_ref, slab_ref, 3 * odd, main)
+    radius = inner_ref.shape[0]
+    start = (1 - lax.axis_index("lat") % 2) * (slab_ref.shape[0] - radius)
+    inner_ref[...] = slab_ref[pl.ds(start, radius)]
+
+
+def feature_kernel(span, band_ref, rows_ref, inner_ref, out_ref, slab_ref):
+    lower = lax.axis_index("lat") % 2
+    held, radius = rows_ref.shape[0], inner_ref.shape[0]
+    slab_ref[pl.ds(lower * radius, held)] = rows_ref[...]
+    slab_ref[pl.ds((1 - lower) * held, radius)] = inner_ref[...]
+    strips, rows, columns, _ = out_ref.shape
+    half = slab_ref.shape[3]
+    main = half - LANES
     bases = band_ref.shape[1] // (2 * columns)
     depth = (span + 1) * 3 * columns
     wide = 2 * main + LANES
@@ -251,27 +267,30 @@
     lax.fori_loop(0, rows // 2, one_pair, 0)
 
 
-def strip_sum(feature_ref, strip, weight):
+def product(feature_ref, strip, weight):
     return lax.dot_general(
         feature_ref[strip], weight, (((1,), (1,)), ((), ())), preferred_element_type=jnp.float32
     )
 
 
-def mix_kernel(sources, feature_ref, *refs):
+def partner_mix_kernel(sources, feature_ref, *refs):
     piece_refs = refs[: len(sources)]
-    keep_ref, send_ref, weight_ref = refs[len(sources) :]
+    send_ref, weight_ref = refs[len(sources) :]
     lat, lon = lax.axis_index("lat"), lax.axis_index("lon")
-    odd = lon % 2
-    masks = weight_ref.shape[0] // 2
-    if sum(len(held) for _, held in sources) < 2 * masks:
+    masks = lax.axis_size("lon") // 2
+    if sum(len(held) for _, _, held in sources) < weight_ref.shape[0]:
         weight_ref[...] = jnp.zeros_like(weight_ref)
-    for (core, held), ref in zip(sources, piece_refs):
+    for (core, low, held), ref in zip(sources, piece_refs):
+        row = 2 * ((lat // 2) ^ low) + (lat % 2 ^ core)
         for at, mask in enumerate(held):
-            place = (lat % 2 ^ core) * masks + ((lon // 2) ^ mask)
-            weight_ref[place] = ref[at]
+            weight_ref[row * masks + ((lon // 2) ^ mask)] = ref[at]
+    weight = weight_ref[...].reshape(send_ref.shape[1], weight_ref.shape[2])
+    send_ref[...] = product(feature_ref, 1 - lon % 2, weight).astype(send_ref.dtype)
+
+
+def own_mix_kernel(feature_ref, weight_ref, keep_ref):
     weight = weight_ref[...].reshape(keep_ref.shape[1], weight_ref.shape[2])
-    send_ref[...] = strip_sum(feature_ref, 1 - odd, weight).astype(send_ref.dtype)
-    keep_ref[...] = strip_sum(feature_ref, odd, weight)
+    keep_ref[...] = product(feature_ref, lax.axis_index("lon") % 2, weight)
 
 
 def rest_kernel(feature_ref, own_ref, crossed_ref, keep_ref, send_ref):
@@ -279,36 +298,35 @@
     weight = jnp.concatenate([own_ref[0], crossed_ref[0]], axis=0)
     count = keep_ref.shape[0]
     for strip, ref in ((1 - odd, send_ref), (odd, keep_ref)):
-        total = strip_sum(feature_ref, strip, weight)
+        total = product(feature_ref, strip, weight)
         ref[...] = jnp.concatenate([total[:count], total[count:]], axis=1).astype(ref.dtype)
 
 
-def finish_kernel(last, block, keep_ref, got_ref, keep2_ref, got2_ref, keep3_ref, got3_ref, bias_ref, out_ref):
+def finish_kernel(last, block, keep_ref, got_ref, keep2_ref, got2_ref, bias_ref, out_ref):
     lat, lon = lax.axis_index("lat"), lax.axis_index("lon")
-    wide = keep_ref.shape[1]
+    wide = out_ref.shape[1] // 2
 
     def save(rows, at, total):
-        at = pl.ds(pl.multiple_of(at, LANES), total.shape[1])
         total += bias_ref[:, at]
         grown = 0.5 * total * (1.0 + lax.erf(total * 0.5**0.5))
         out_ref[rows, at] = grown.astype(out_ref.dtype)
 
-    save(slice(None), lat // 2 * wide, keep_ref[...] + got_ref[...].astype(jnp.float32))
-    rest = keep3_ref[...] + got3_ref[...].astype(jnp.float32)
+    at = pl.ds(pl.multiple_of(lat // 2 * wide, LANES), wide)
+    save(slice(None), at, keep_ref[:, at] + got_ref[:, at].astype(jnp.float32))
+    rest = keep2_ref[...] + got2_ref[...].astype(jnp.float32)
     count = rest.shape[0]
     lane = lane_of(rest)
     start = ((lon // 2) ^ last) * block
     inside = (lane >= start) & (lane < start + block)
     for crossed in range(2):
-        core = lat % 2 ^ crossed
-        at = pl.ds(pl.multiple_of(core * LANES, LANES), LANES)
+        tile = (1 - lat // 2) * 2 + (lat % 2 ^ crossed)
+        at = pl.ds(pl.multiple_of(tile * LANES, LANES), LANES)
         for part in range(2):
             rows = slice(part * count, (part + 1) * count)
             held = part * (2 * block) + crossed * block
             moved = pltpu.roll(rest, lax.rem(start - held + LANES, LANES), 1)
-            total = keep2_ref[rows, at] + got2_ref[rows, at].astype(jnp.float32)
-            total = jnp.where(inside, moved, total)
-            save(rows, (1 - lat // 2) * wide + core * LANES, total)
+            total = keep_ref[rows, at] + got_ref[rows, at].astype(jnp.float32)
+            save(rows, at, jnp.where(inside, moved, total))
 
 
 def body(latent, filters, widths, mix_weight, mix_bias):
@@ -326,16 +344,14 @@
 
     edge, halves = shape((radius, columns, channels)), shape((share, depth))
     weights = jnp.transpose(mix_weight, (0, 2, 1))
-    own_weight, pair_weight, outer, inner = call(
-        functools.partial(start_kernel, main), (halves, halves, edge, edge), [], weights, latent
-    )
+    own_weight, pair_weight = call(
+        functools.partial(weight_kernel, main), (halves, halves), [], weights
+    )
+    outer, held_latent = call(edge_kernel, (edge, shape(latent.shape)), [], latent)
     got_weight = swap(pair_weight, 0, 1)
     from_outer = lax.ppermute(outer, AXES, route(outer_move))
-    from_inner = swap(inner, 1, 0)
     block = shape((2 * share, depth))
-    first = call(
-        join_kernel, block, [], own_weight, got_weight, after=(from_outer, from_inner)
-    )
+    first = call(join_kernel, block, [], own_weight, got_weight)
 
     lon_masks, lat_masks = lons // 2, lats // 2
     steps = [1 << at for at in range(lat_masks.bit_length() - 1)]
@@ -347,22 +363,27 @@
         bit //= 2
     order = [mask for _, mask in blocks]
     last = order[-1]
-    for bit in steps:
-        for low in range(bit):
-            for mask in order[:-1]:
-                blocks[low ^ bit, mask] = swap(blocks[low, mask], 2 * bit, 0)
-
-    count = rows + 2 * radius
+    count = rows + radius
     strip = shape((columns, count // 2 * packed + LANES))
+
+    def cross(masks):
+        for bit in steps:
+            for low in range(bit):
+                for mask in masks:
+                    blocks[low ^ bit, mask] = swap(blocks[low, mask], 2 * bit, 0)
+
+    cross(order[:1])
+    crossed_first = tuple(blocks[bit, 0] for bit in steps)
     mine, other = call(
         functools.partial(strip_kernel, main),
         (strip, strip),
         [pltpu.VMEM((count, columns, channels), jnp.bfloat16)],
-        latent,
+        held_latent,
         from_outer,
-        from_inner,
-        after=tuple(blocks[bit, 0] for bit in steps),
-    )
+    )
+    for mask in order[1:-1]:
+        blocks[0, mask] = call(copy_kernel, block, [], blocks[0, mask], after=(mine,))
+    cross(order[1:-1])
     pair_strip = swap(other, 0, 1)
     along = lax.ppermute(mine, AXES, route(along_move))
     across = lax.ppermute(other, AXES, route(across_move))
@@ -373,30 +394,34 @@
         [pltpu.VMEM((bases, rows, deep), jnp.float32)],
         jnp.transpose(filters, (0, 2, 1, 3)),
         widths,
-        after=(mine,),
-    )
-
-    met = [value for key, value in blocks.items() if key != (0, last)]
-    blocks[0, last] = call(
-        copy_kernel, block, [], blocks[0, last], after=(*met, band, pair_strip, along, across)
-    )
-    for bit in steps:
-        for low in range(bit):
-            blocks[low ^ bit, last] = swap(blocks[low, last], 2 * bit, 0)
-    features = call(
-        functools.partial(feature_kernel, span),
-        shape((2, rows, columns, depth)),
-        [pltpu.VMEM((count, 4, columns, half), jnp.bfloat16)],
-        band,
+        after=(pair_strip,),
+    )
+    slab, inner = call(
+        slab_kernel,
+        (shape((count, 4, columns, half)), shape((radius, 4, columns, half))),
+        [],
         mine,
         pair_strip,
         along,
         across,
-        after=(blocks[0, last],),
+    )
+    from_inner = swap(inner, 1, 0)
+
+    features = call(
+        functools.partial(feature_kernel, span),
+        shape((2, rows, columns, depth)),
+        [pltpu.VMEM((rows + 2 * radius, 4, columns, half), jnp.bfloat16)],
+        band,
+        slab,
+        from_inner,
     )
     features = features.reshape(2, rows * columns, depth)
-
-    points, width = rows * columns, out_columns // lat_masks
+    met = [value for key, value in blocks.items() if key != (0, last)]
+    blocks[0, last] = call(
+        copy_kernel, block, [], blocks[0, last], after=(*met, band, *(features,))
+    )
+    cross(order[-1:])
+    points = rows * columns
 
     def stacked(low, held, after):
         piece = call(
@@ -408,43 +433,42 @@
         )
         return [piece, swap(piece, 1, 0)]
 
-    def mixed(groups, pieces):
-        sources = [(core, held) for held in groups for core in range(2)]
-        keep, send = call(
-            functools.partial(mix_kernel, sources),
-            (shape((points, width), jnp.float32), shape((points, width))),
-            [pltpu.VMEM((2 * lon_masks,) + block.shape, jnp.bfloat16)],
-            features,
-            *pieces,
-        )
-        return keep, swap(send, 0, 1)
-
-    gate = (blocks[0, last],)
-    if lat_masks == 2 and 8 * share == LANES == lon_masks * 2 * share and points % 2 == 0:
-        parts = [*mixed([order], stacked(0, order, gate))]
-        parts += mixed([order[:-1]], stacked(1, order[:-1], gate))
-        rest = shape((points // 2, LANES), jnp.float32), shape((points // 2, LANES))
-        keep, send = call(
-            rest_kernel, rest, [], features, *stacked(1, order[-1:], (parts[2],))
-        )
-        out = call(
-            functools.partial(finish_kernel, last, 2 * share),
-            shape((points, out_columns)),
-            [],
-            *parts,
-            keep,
-            swap(send, 0, 1),
-            mix_bias[None],
-        )
-        return out.reshape(rows, columns, out_columns)
-    sums = []
+    apart = lat_masks == 2 and 8 * share == LANES == lon_masks * 2 * share and points % 2 == 0
+    sources, pieces = [], []
     for low in range(lat_masks):
-        keep, got = mixed([order], stacked(low, order, gate))
-        sums.append(keep + got.astype(jnp.float32))
-    total = jnp.stack(sums, 1)
-    total = jnp.take(total, jnp.arange(lat_masks) ^ (lax.axis_index("lat") // 2), axis=1)
-    total = total.reshape(rows, columns, out_columns) + mix_bias
-    return jax.nn.gelu(total, approximate=False).astype(jnp.bfloat16)
+        held = order[:-1] if low and apart else order
+        sources += [(core, low, held) for core in range(2)]
+        pieces += stacked(low, held, (blocks[0, last],) if low == 0 else (blocks[0, last],))
+    send, weight = call(
+        functools.partial(partner_mix_kernel, sources),
+        (shape((points, out_columns)), shape((lats * lon_masks,) + block.shape)),
+        [],
+        features,
+        *pieces,
+    )
+    got = swap(send, 0, 1)
+    sums = shape((points, out_columns), jnp.float32)
+    if not apart:
+        keep = call(own_mix_kernel, sums, [], features, weight)
+        total = (keep + got.astype(jnp.float32)).reshape(rows, columns, out_columns) + mix_bias
+        return jax.nn.gelu(total, approximate=False).astype(jnp.bfloat16)
+    rest = shape((points // 2, LANES), jnp.float32), shape((points // 2, LANES))
+    rest_keep, rest_send = call(
+        rest_kernel, rest, [], features, *stacked(1, order[-1:], (send,))
+    )
+    rest_got = swap(rest_send, 0, 1)
+    keep = call(own_mix_kernel, sums, [], features, weight)
+    out = call(
+        functools.partial(finish_kernel, last, 2 * share),
+        shape((points, out_columns)),
+        [],
+        keep,
+        got,
+        rest_keep,
+        rest_got,
+        mix_bias[None],
+    )
+    return out.reshape(rows, columns, out_columns)
 
 
 def solution(mesh):

time: 57.9 us -> 54.7 us (0.945)
  local copies, waits for them, and re-layouts: 4.6 us -> 1.94 us
  waiting for transfers between devices: 17.8 us -> 16.1 us
  starting transfers between devices: 25 us -> 25.9 us
    ppermute x16 -> x15, waiting for transfers between devices: 14.9 us -> 10.8 us  [swap(): lax.ppermute(block, AXES, route(lambda lat, lon, lats, lons: (lat ^ lat_b...]
    ppermute x1, waiting for transfers between devices: 2.93 us -> 0.01 us  [body(): from_outer = lax.ppermute(outer, AXES, route(outer_move))]
    ppermute x1, waiting for transfers between devices: 0.01 us -> 2.88 us  [body(): along = lax.ppermute(mine, AXES, route(along_move))]
    unnamed x12 -> x10, local copies, waits for them, and re-layouts: 4.6 us -> 1.94 us
    ppermute x1, waiting for transfers between devices: 0.01 us -> 2.47 us  [body(): across = lax.ppermute(other, AXES, route(across_move))]
    ppermute x1, starting transfers between devices: 3.91 us -> 5.87 us  [body(): across = lax.ppermute(other, AXES, route(across_move))]
    ppermute x16 -> x15, starting transfers between devices: 17 us -> 15.3 us  [swap(): lax.ppermute(block, AXES, route(lambda lat, lon, lats, lons: (lat ^ lat_b...]
    ppermute x1, starting transfers between devices: 2.59 us -> 4.1 us  [body(): from_outer = lax.ppermute(outer, AXES, route(outer_move))]
  transfers between devices with their start and end apart: 19 -> 18, of which waited for: 7 -> 9; matrix products, arithmetic and copies ran while one was open for 0% -> 0% of each run, Pallas kernels for 16% -> 17%
where the time goes in v4:
time: 54.7 us; the launch traced here: 54.5 us
  starting transfers between devices  25.9 us (47%)
  waiting for transfers between devices  16.1 us (29%)
  Pallas kernels  10.3 us (19%)
  local copies, waits for them, and re-layouts  1.94 us (4%)
    ppermute x15, starting transfers between devices, swap(): lax.ppermute(block, AXES, route(lambda lat, lon, lats, lons: (lat ^ lat_b...  15.3 us
    ppermute x15, waiting for transfers between devices, swap(): lax.ppermute(block, AXES, route(lambda lat, lon, lats, lons: (lat ^ lat_b...  10.8 us
    pallas_call x17, Pallas kernels, call(): pl.pallas_call(ordered, out_shape=outs, in_specs=[held] * count + [pl.Blo...  10.3 us
    ppermute x1, starting transfers between devices, body(): across = lax.ppermute(other, AXES, route(across_move))  5.87 us
    ppermute x1, starting transfers between devices, body(): from_outer = lax.ppermute(outer, AXES, route(outer_move))  4.1 us
    ppermute x1, waiting for transfers between devices, body(): along = lax.ppermute(mine, AXES, route(along_move))  2.88 us
    ppermute x1, waiting for transfers between devices, body(): across = lax.ppermute(other, AXES, route(across_move))  2.47 us
    unnamed x10, local copies, waits for them, and re-layouts  1.94 us
  transfers between devices with their start and end apart: 18, of which 9 were waited for; matrix products, arithmetic and copies ran while one was open for 0% of the time, Pallas kernels for 17%

profile of v4, /device:TPU:0, one launch (start us, length us, event | category | flops | bytes accessed | tf_op | source)
XLA Modules:
  0.0 54.5 jit_solution(6572044993826092124)
XLA Ops:
  0.0 1.0 %copy-done = bf16[16,16,641]{2,1,0:T(8,128)(2,1)S(1)} copy-done((bf16[16,16,641]{2,1,0:T(8,128)(2,1)S(1)}, bf16[16,16,641]{2,1,0:T(8,128)(2,1)}, u32[]{:S(2)}) %copy-start) | copy-done | bytes 328216
  1.0 4.1 %collective-permute-start = (bf16[4,16,641]{2,1,0:T(8,128)(2,1)S(1)}, bf16[4,16,641]{2,1,0:T(8,128)(2,1)S(1)}, u32[]{:S(2)}, u32[]{:S(2)}) collective-permute-start(bf16[4,16,641]{2,1,0:T(8,128)(2,1)S(1)} %get-tuple-element.18), channel_id=1, source_target_pairs={{0,4},{1,5},{2,6},{3,7},{4,0},{5,1},{6,2},{7,3},{8,16},{9,17},{10,... | collective-permute-start | bytes 246152 | tf_op jit(solution)/shard_map/ppermute | solution.py:352
  5.1 0.9 %copy-done.2 = bf16[9,641,16]{1,2,0:T(8,128)(2,1)S(1)} copy-done((bf16[9,641,16]{1,2,0:T(8,128)(2,1)S(1)}, bf16[9,641,16]{1,2,0:T(8,128)(2,1)}, u32[]{:S(2)}) %copy-start.2) | copy-done | bytes 184632
  6.2 1.6 %collective-permute-start.5 = (bf16[16,2944]{1,0:T(8,128)(2,1)S(1)}, bf16[16,2944]{1,0:T(8,128)(2,1)S(1)}, u32[]{:S(2)}, u32[]{:S(2)}) collective-permute-start(bf16[16,2944]{1,0:T(8,128)(2,1)S(1)} %get-tuple-element.24), channel_id=1, source_target_pairs={{0,1},{1,0},{2,3},{3,2},{4,5},{5,4},{6,7},{7,6},{8,9},{9,8},{10,11... | collective-permute-start | bytes 282632 | tf_op jit(solution)/shard_map/ppermute | solution.py:49
  7.8 0.2 shard_map.56
  7.9 5.9 %collective-permute-start.3 = (bf16[16,6528]{1,0:T(8,128)(2,1)S(1)}, bf16[16,6528]{1,0:T(8,128)(2,1)S(1)}, u32[]{:S(2)}, u32[]{:S(2)}) collective-permute-start(bf16[16,6528]{1,0:T(8,128)(2,1)S(1)} %get-tuple-element.19), channel_id=1, source_target_pairs={{0,7},{1,2},{2,1},{3,4},{4,3},{5,6},{6,5},{7,0},{8,15},{9,10},{10,... | collective-permute-start | bytes 626696 | tf_op jit(solution)/shard_map/ppermute | solution.py:389
  13.8 0.6 %collective-permute-start.2 = (bf16[16,6528]{1,0:T(8,128)(2,1)S(1)}, bf16[16,6528]{1,0:T(8,128)(2,1)S(1)}, u32[]{:S(2)}, u32[]{:S(2)}) collective-permute-start(bf16[16,6528]{1,0:T(8,128)(2,1)S(1)} %get-tuple-element.20.refs_0_.refs_1_), channel_id=1, source_target_pairs={{0,6},{1,3},{2,0},{3,5},{4,2},{5,7},{6,4},{7,1},{8,14},{9,11},{10,... | collective-permute-start | bytes 626696 | tf_op jit(solution)/shard_map/ppermute | solution.py:388
  14.5 0.5 collective-permute-start.6
  15.0 2.0 %collective-permute-start.7 = (bf16[32,2944]{1,0:T(8,128)(2,1)S(1)}, bf16[32,2944]{1,0:T(8,128)(2,1)S(1)}, u32[]{:S(2)}, u32[]{:S(2)}) collective-permute-start(bf16[32,2944]{1,0:T(8,128)(2,1)S(1)} %shard_map.61.refs_1_.refs_0_), channel_id=1, source_target_pairs={{0,2},{1,3},{2,0},{3,1},{4,6},{5,7},{6,4},{7,5},{8,10},{9,11},{10,... | collective-permute-start | bytes 565256 | tf_op jit(solution)/shard_map/ppermute | solution.py:49
  17.0 2.5 %collective-permute-done.3.refs_3_ = bf16[16,6528]{1,0:T(8,128)(2,1)S(1)} collective-permute-done((bf16[16,6528]{1,0:T(8,128)(2,1)S(1)}, bf16[16,6528]{1,0:T(8,128)(2,1)S(1)}, u32[]{:S(2)}, u32[]{:S(2)}) %collective-permute-start.3) | collective-permute-done | bytes 208928 | tf_op jit(solution)/shard_map/ppermute | solution.py:389
  19.5 1.6 %collective-permute-done.1.refs_2_.refs_1_ = bf16[16,6528]{1,0:T(8,128)(2,1)S(1)} collective-permute-done((bf16[16,6528]{1,0:T(8,128)(2,1)S(1)}, bf16[16,6528]{1,0:T(8,128)(2,1)S(1)}, u32[]{:S(2)}, u32[]{:S(2)}) %collective-permute-start.1) | collective-permute-done | bytes 208928 | tf_op jit(solution)/shard_map/ppermute | solution.py:49
  21.1 2.9 %collective-permute-done.2.refs_2_ = bf16[16,6528]{1,0:T(8,128)(2,1)S(1)} collective-permute-done((bf16[16,6528]{1,0:T(8,128)(2,1)S(1)}, bf16[16,6528]{1,0:T(8,128)(2,1)S(1)}, u32[]{:S(2)}, u32[]{:S(2)}) %collective-permute-start.2) | collective-permute-done | bytes 208928 | tf_op jit(solution)/shard_map/ppermute | solution.py:388
  24.0 0.2 shard_map.58
  24.4 4.0 %collective-permute-done.6.refs_0_ = bf16[32,2944]{1,0:T(8,128)(2,1)S(1)} collective-permute-done((bf16[32,2944]{1,0:T(8,128)(2,1)S(1)}, bf16[32,2944]{1,0:T(8,128)(2,1)S(1)}, u32[]{:S(2)}, u32[]{:S(2)}) %collective-permute-start.6) | collective-permute-done | bytes 188448 | tf_op jit(solution)/shard_map/ppermute | solution.py:49
  28.4 2.3 %collective-permute-start.10 = (bf16[32,2944]{1,0:T(8,128)(2,1)S(1)}, bf16[32,2944]{1,0:T(8,128)(2,1)S(1)}, u32[]{:S(2)}, u32[]{:S(2)}) collective-permute-start(bf16[32,2944]{1,0:T(8,128)(2,1)S(1)} %shard_map.62.refs_2_.refs_1_), channel_id=1, source_target_pairs={{0,16},{1,17},{2,18},{3,19},{4,20},{5,21},{6,22},{7,23},{8,24},{9,... | collective-permute-start | bytes 565256 | tf_op jit(solution)/shard_map/ppermute | solution.py:49
  30.7 2.0 %collective-permute-start.8 = (bf16[32,2944]{1,0:T(8,128)(2,1)S(1)}, bf16[32,2944]{1,0:T(8,128)(2,1)S(1)}, u32[]{:S(2)}, u32[]{:S(2)}) collective-permute-start(bf16[32,2944]{1,0:T(8,128)(2,1)S(1)} %collective-permute-done.6.refs_0_), channel_id=1, source_target_pairs={{0,2},{1,3},{2,0},{3,1},{4,6},{5,7},{6,4},{7,5},{8,10},{9,11},{10,... | collective-permute-start | bytes 565256 | tf_op jit(solution)/shard_map/ppermute | solution.py:49
  32.7 0.1 collective-permute-start.11
  32.8 1.4 %shard_map.57.refs_0_.refs_7_ = bf16[8,288,512]{2,1,0:T(8,128)(2,1)S(1)} custom-call(bf16[9,9,16,33]{3,2,1,0:T(8,128)(2,1)S(1)} %bitcast.9, s32[16,9]{1,0:T(8,128)S(1)} %copy-done.3, bf16[16,6528]{1,0:T(8,128)(2,1)S(1)} %collective-permute-done.1.refs_2_.refs_1_), custom_call_target="tpu_custom_call" | custom-call | tf_op jit(solution)/shard_map/pallas_call | solution.py:24
  34.2 3.9 %shard_map.59 = bf16[2,16,16,2944]{3,2,1,0:T(8,128)(2,1)S(1)} custom-call(bf16[8,288,512]{2,1,0:T(8,128)(2,1)S(1)} %shard_map.57.refs_0_.refs_7_, bf16[20,4,16,384]{3,2,1,0:T(8,128)(2,1)S(1)} %get-tuple-element.21.refs_1_, bf16[4,4,16,384]{3,2,1,0:T(8,128)(2,1)S(1)} %collective-permute-done.4.refs_2_), custom_call_target="tpu_custom_call" | custom-call | tf_op jit(solution)/shard_map/pallas_call | solution.py:24
  38.1 1.4 %collective-permute-done.11.refs_6_.refs_2_ = bf16[32,2944]{1,0:T(8,128)(2,1)S(1)} collective-permute-done((bf16[32,2944]{1,0:T(8,128)(2,1)S(1)}, bf16[32,2944]{1,0:T(8,128)(2,1)S(1)}, u32[]{:S(2)}, u32[]{:S(2)}) %collective-permute-start.11) | collective-permute-done | bytes 188448 | tf_op jit(solution)/shard_map/ppermute | solution.py:49
  39.7 0.6 %collective-permute-start.13 = (bf16[3,32,2944]{2,1,0:T(8,128)(2,1)S(1)}, bf16[3,32,2944]{2,1,0:T(8,128)(2,1)S(1)}, u32[]{:S(2)}, u32[]{:S(2)}) collective-permute-start(bf16[3,32,2944]{2,1,0:T(8,128)(2,1)S(1)} %shard_map.66.refs_3_), channel_id=1, source_target_pairs={{0,8},{1,9},{2,10},{3,11},{4,12},{5,13},{6,14},{7,15},{8,0},{9,1},... | collective-permute-start | bytes 1695752 | tf_op jit(solution)/shard_map/ppermute | solution.py:49
  40.3 1.7 %collective-permute-start.15 = (bf16[32,2944]{1,0:T(8,128)(2,1)S(1)}, bf16[32,2944]{1,0:T(8,128)(2,1)S(1)}, u32[]{:S(2)}, u32[]{:S(2)}) collective-permute-start(bf16[32,2944]{1,0:T(8,128)(2,1)S(1)} %shard_map.64.refs_3_.refs_4_), channel_id=1, source_target_pairs={{0,16},{1,17},{2,18},{3,19},{4,20},{5,21},{6,22},{7,23},{8,24},{9,... | collective-permute-start | bytes 565256 | tf_op jit(solution)/shard_map/ppermute | solution.py:49
  41.9 0.8 %collective-permute-done.13.refs_4_ = bf16[3,32,2944]{2,1,0:T(8,128)(2,1)S(1)} collective-permute-done((bf16[3,32,2944]{2,1,0:T(8,128)(2,1)S(1)}, bf16[3,32,2944]{2,1,0:T(8,128)(2,1)S(1)}, u32[]{:S(2)}, u32[]{:S(2)}) %collective-permute-start.13) | collective-permute-done | bytes 565280 | tf_op jit(solution)/shard_map/ppermute | solution.py:49
  42.7 1.4 %shard_map.67 = (bf16[256,512]{1,0:T(8,128)(2,1)S(1)}, bf16[16,32,2944]{2,1,0:T(8,128)(2,1)S(1)}) custom-call(bf16[2,256,2944]{2,1,0:T(8,128)(2,1)S(1)} %bitcast.6, bf16[4,32,2944]{2,1,0:T(8,128)(2,1)S(1)} %shard_map.65.refs_1_, bf16[4,32,2944]{2,1,0:T(8,128)(2,1)S(1)} %collective-permute-done.12.refs_2_, bf16[3,32,2944]{2,1,0:T(8,128)(2,1)S(1)} %shard_map.66.refs_3_, ...), custom_call_target="tpu_custom_call" | custom-call | tf_op jit(solution)/shard_map/pallas_call | solution.py:24
  44.1 2.1 %collective-permute-start.14 = (bf16[256,512]{1,0:T(8,128)(2,1)S(1)}, bf16[256,512]{1,0:T(8,128)(2,1)S(1)}, u32[]{:S(2)}, u32[]{:S(2)}) collective-permute-start(bf16[256,512]{1,0:T(8,128)(2,1)S(1)} %get-tuple-element.26.refs_1_), channel_id=1, source_target_pairs={{0,1},{1,0},{2,3},{3,2},{4,5},{5,4},{6,7},{7,6},{8,9},{9,8},{10,11... | collective-permute-start | bytes 786440 | tf_op jit(solution)/shard_map/ppermute | solution.py:49
  46.2 0.7 %collective-permute-done.15.refs_0_ = bf16[32,2944]{1,0:T(8,128)(2,1)S(1)} collective-permute-done((bf16[32,2944]{1,0:T(8,128)(2,1)S(1)}, bf16[32,2944]{1,0:T(8,128)(2,1)S(1)}, u32[]{:S(2)}, u32[]{:S(2)}) %collective-permute-start.15) | collective-permute-done | bytes 188448 | tf_op jit(solution)/shard_map/ppermute | solution.py:49
  47.1 1.4 %collective-permute-done.16.refs_2_ = bf16[1,32,2944]{2,1,0:T(8,128)(2,1)S(1)} collective-permute-done((bf16[1,32,2944]{2,1,0:T(8,128)(2,1)S(1)}, bf16[1,32,2944]{2,1,0:T(8,128)(2,1)S(1)}, u32[]{:S(2)}, u32[]{:S(2)}) %collective-permute-start.16) | collective-permute-done | bytes 188448 | tf_op jit(solution)/shard_map/ppermute | solution.py:49
  48.5 1.0 %shard_map.70 = (f32[128,128]{1,0:T(8,128)S(1)}, bf16[128,128]{1,0:T(8,128)(2,1)S(1)}) custom-call(bf16[2,256,2944]{2,1,0:T(8,128)(2,1)S(1)} %bitcast.7, bf16[1,32,2944]{2,1,0:T(8,128)(2,1)S(1)} %shard_map.69.refs_1_, bf16[1,32,2944]{2,1,0:T(8,128)(2,1)S(1)} %collective-permute-done.16.refs_2_), custom_call_target="tpu_custom_call" | custom-call | tf_op jit(solution)/shard_map/pallas_call | solution.py:24
  49.5 2.1 %collective-permute-start.17 = (bf16[128,128]{1,0:T(8,128)(2,1)S(1)}, bf16[128,128]{1,0:T(8,128)(2,1)S(1)}, u32[]{:S(2)}, u32[]{:S(2)}) collective-permute-start(bf16[128,128]{1,0:T(8,128)(2,1)S(1)} %get-tuple-element.28), channel_id=1, source_target_pairs={{0,1},{1,0},{2,3},{3,2},{4,5},{5,4},{6,7},{7,6},{8,9},{9,8},{10,11... | collective-permute-start | bytes 98312 | tf_op jit(solution)/shard_map/ppermute | solution.py:49
  51.6 1.0 %shard_map.68.refs_0_ = f32[256,512]{1,0:T(8,128)S(1)} custom-call(bf16[2,256,2944]{2,1,0:T(8,128)(2,1)S(1)} %bitcast.8, bf16[16,32,2944]{2,1,0:T(8,128)(2,1)S(1)} %get-tuple-element.25.refs_1_), custom_call_target="tpu_custom_call" | custom-call | tf_op jit(solution)/shard_map/pallas_call | solution.py:24
  52.6 0.9 %collective-permute-done.17.refs_3_ = bf16[128,128]{1,0:T(8,128)(2,1)S(1)} collective-permute-done((bf16[128,128]{1,0:T(8,128)(2,1)S(1)}, bf16[128,128]{1,0:T(8,128)(2,1)S(1)}, u32[]{:S(2)}, u32[]{:S(2)}) %collective-permute-start.17) | collective-permute-done | bytes 32800 | tf_op jit(solution)/shard_map/ppermute | solution.py:49
  53.6 0.9 %shard_map.71 = bf16[256,512]{1,0:T(8,128)(2,1)} custom-call(f32[256,512]{1,0:T(8,128)S(1)} %shard_map.68.refs_0_, bf16[256,512]{1,0:T(8,128)(2,1)S(1)} %collective-permute-done.14.refs_1_, f32[128,128]{1,0:T(8,128)S(1)} %get-tuple-element.27.refs_2_, bf16[128,128]{1,0:T(8,128)(2,1)S(1)} %collective-permute-done.17.refs_3_, f32[1,512]{1,0:T(1,128)S(1)} %bitcast.11), custom_call_target="tpu_custom_call" | custom-call | tf_op jit(solution)/shard_map/pallas_call | solution.py:24
  (31 shorter events, 0.6 us)
Async XLA Ops:
  0.0 1.0 %copy-start = (bf16[16,16,641]{2,1,0:T(8,128)(2,1)S(1)}, bf16[16,16,641]{2,1,0:T(8,128)(2,1)}, u32[]{:S(2)}) copy-start(bf16[16,16,641]{2,1,0:T(8,128)(2,1)} %refs_0_.1) | copy-start | bytes 984580
  1.0 31.8 %copy-start.1 = (bf16[9,16,9,33]{3,1,2,0:T(8,128)(2,1)S(1)}, bf16[9,16,9,33]{3,1,2,0:T(8,128)(2,1)}, u32[]{:S(2)}) copy-start(bf16[9,16,9,33]{3,1,2,0:T(8,128)(2,1)} %param.6) | copy-start | bytes 256612
  1.0 31.8 %copy-start.3 = (s32[16,9]{1,0:T(8,128)S(1)}, s32[16,9]{1,0:T(8,128)}, u32[]{:S(2)}) copy-start(s32[16,9]{1,0:T(8,128)} %refs_1_.1) | copy-start | bytes 1732
  1.0 6.7 %collective-permute-start = (bf16[4,16,641]{2,1,0:T(8,128)(2,1)S(1)}, bf16[4,16,641]{2,1,0:T(8,128)(2,1)S(1)}, u32[]{:S(2)}, u32[]{:S(2)}) collective-permute-start(bf16[4,16,641]{2,1,0:T(8,128)(2,1)S(1)} %get-tuple-element.18), channel_id=1, source_target_pairs={{0,4},{1,5},{2,6},{3,7},{4,0},{5,1},{6,2},{7,3},{8,16},{9,17},{10,... | collective-permute-start | bytes 246152 | tf_op jit(solution)/shard_map/ppermute | solution.py:352
  5.1 0.9 %copy-start.2 = (bf16[9,641,16]{1,2,0:T(8,128)(2,1)S(1)}, bf16[9,641,16]{1,2,0:T(8,128)(2,1)}, u32[]{:S(2)}) copy-start(bf16[9,641,16]{1,2,0:T(8,128)(2,1)} %param.8) | copy-start | bytes 553828
  6.2 8.3 %collective-permute-start.5 = (bf16[16,2944]{1,0:T(8,128)(2,1)S(1)}, bf16[16,2944]{1,0:T(8,128)(2,1)S(1)}, u32[]{:S(2)}, u32[]{:S(2)}) collective-permute-start(bf16[16,2944]{1,0:T(8,128)(2,1)S(1)} %get-tuple-element.24), channel_id=1, source_target_pairs={{0,1},{1,0},{2,3},{3,2},{4,5},{5,4},{6,7},{7,6},{8,9},{9,8},{10,11... | collective-permute-start | bytes 282632 | tf_op jit(solution)/shard_map/ppermute | solution.py:49
  7.9 11.5 %collective-permute-start.3 = (bf16[16,6528]{1,0:T(8,128)(2,1)S(1)}, bf16[16,6528]{1,0:T(8,128)(2,1)S(1)}, u32[]{:S(2)}, u32[]{:S(2)}) collective-permute-start(bf16[16,6528]{1,0:T(8,128)(2,1)S(1)} %get-tuple-element.19), channel_id=1, source_target_pairs={{0,7},{1,2},{2,1},{3,4},{4,3},{5,6},{6,5},{7,0},{8,15},{9,10},{10,... | collective-permute-start | bytes 626696 | tf_op jit(solution)/shard_map/ppermute | solution.py:389
  13.8 7.3 %collective-permute-start.1 = (bf16[16,6528]{1,0:T(8,128)(2,1)S(1)}, bf16[16,6528]{1,0:T(8,128)(2,1)S(1)}, u32[]{:S(2)}, u32[]{:S(2)}) collective-permute-start(bf16[16,6528]{1,0:T(8,128)(2,1)S(1)} %get-tuple-element.19), channel_id=1, source_target_pairs={{0,1},{1,0},{2,3},{3,2},{4,5},{5,4},{6,7},{7,6},{8,9},{9,8},{10,11... | collective-permute-start | bytes 626696 | tf_op jit(solution)/shard_map/ppermute | solution.py:49
  13.8 10.1 %collective-permute-start.2 = (bf16[16,6528]{1,0:T(8,128)(2,1)S(1)}, bf16[16,6528]{1,0:T(8,128)(2,1)S(1)}, u32[]{:S(2)}, u32[]{:S(2)}) collective-permute-start(bf16[16,6528]{1,0:T(8,128)(2,1)S(1)} %get-tuple-element.20.refs_0_.refs_1_), channel_id=1, source_target_pairs={{0,6},{1,3},{2,0},{3,5},{4,2},{5,7},{6,4},{7,1},{8,14},{9,11},{10,... | collective-permute-start | bytes 626696 | tf_op jit(solution)/shard_map/ppermute | solution.py:388
  14.5 13.9 %collective-permute-start.6 = (bf16[32,2944]{1,0:T(8,128)(2,1)S(1)}, bf16[32,2944]{1,0:T(8,128)(2,1)S(1)}, u32[]{:S(2)}, u32[]{:S(2)}) collective-permute-start(bf16[32,2944]{1,0:T(8,128)(2,1)S(1)} %shard_map.61.refs_1_.refs_0_), channel_id=1, source_target_pairs={{0,4},{1,5},{2,6},{3,7},{4,0},{5,1},{6,2},{7,3},{8,12},{9,13},{10,... | collective-permute-start | bytes 565256 | tf_op jit(solution)/shard_map/ppermute | solution.py:49
  15.0 17.7 %collective-permute-start.7 = (bf16[32,2944]{1,0:T(8,128)(2,1)S(1)}, bf16[32,2944]{1,0:T(8,128)(2,1)S(1)}, u32[]{:S(2)}, u32[]{:S(2)}) collective-permute-start(bf16[32,2944]{1,0:T(8,128)(2,1)S(1)} %shard_map.61.refs_1_.refs_0_), channel_id=1, source_target_pairs={{0,2},{1,3},{2,0},{3,1},{4,6},{5,7},{6,4},{7,5},{8,10},{9,11},{10,... | collective-permute-start | bytes 565256 | tf_op jit(solution)/shard_map/ppermute | solution.py:49
  24.2 10.0 %collective-permute-start.4 = (bf16[4,4,16,384]{3,2,1,0:T(8,128)(2,1)S(1)}, bf16[4,4,16,384]{3,2,1,0:T(8,128)(2,1)S(1)}, u32[]{:S(2)}, u32[]{:S(2)}) collective-permute-start(bf16[4,4,16,384]{3,2,1,0:T(8,128)(2,1)S(1)} %get-tuple-element.22), channel_id=1, source_target_pairs={{0,8},{1,9},{2,10},{3,11},{4,12},{5,13},{6,14},{7,15},{8,0},{9,1},... | collective-permute-start | bytes 589832 | tf_op jit(solution)/shard_map/ppermute | solution.py:49
  24.3 13.8 %collective-permute-start.9 = (bf16[32,2944]{1,0:T(8,128)(2,1)S(1)}, bf16[32,2944]{1,0:T(8,128)(2,1)S(1)}, u32[]{:S(2)}, u32[]{:S(2)}) collective-permute-start(bf16[32,2944]{1,0:T(8,128)(2,1)S(1)} %shard_map.61.refs_1_.refs_0_), channel_id=1, source_target_pairs={{0,16},{1,17},{2,18},{3,19},{4,20},{5,21},{6,22},{7,23},{8,24},{9,... | collective-permute-start | bytes 565256 | tf_op jit(solution)/shard_map/ppermute | solution.py:49
  28.4 9.8 %collective-permute-start.10 = (bf16[32,2944]{1,0:T(8,128)(2,1)S(1)}, bf16[32,2944]{1,0:T(8,128)(2,1)S(1)}, u32[]{:S(2)}, u32[]{:S(2)}) collective-permute-start(bf16[32,2944]{1,0:T(8,128)(2,1)S(1)} %shard_map.62.refs_2_.refs_1_), channel_id=1, source_target_pairs={{0,16},{1,17},{2,18},{3,19},{4,20},{5,21},{6,22},{7,23},{8,24},{9,... | collective-permute-start | bytes 565256 | tf_op jit(solution)/shard_map/ppermute | solution.py:49
  30.7 7.5 %collective-permute-start.8 = (bf16[32,2944]{1,0:T(8,128)(2,1)S(1)}, bf16[32,2944]{1,0:T(8,128)(2,1)S(1)}, u32[]{:S(2)}, u32[]{:S(2)}) collective-permute-start(bf16[32,2944]{1,0:T(8,128)(2,1)S(1)} %collective-permute-done.6.refs_0_), channel_id=1, source_target_pairs={{0,2},{1,3},{2,0},{3,1},{4,6},{5,7},{6,4},{7,5},{8,10},{9,11},{10,... | collective-permute-start | bytes 565256 | tf_op jit(solution)/shard_map/ppermute | solution.py:49
  32.7 6.8 %collective-permute-start.11 = (bf16[32,2944]{1,0:T(8,128)(2,1)S(1)}, bf16[32,2944]{1,0:T(8,128)(2,1)S(1)}, u32[]{:S(2)}, u32[]{:S(2)}) collective-permute-start(bf16[32,2944]{1,0:T(8,128)(2,1)S(1)} %shard_map.63.refs_3_.refs_2_), channel_id=1, source_target_pairs={{0,16},{1,17},{2,18},{3,19},{4,20},{5,21},{6,22},{7,23},{8,24},{9,... | collective-permute-start | bytes 565256 | tf_op jit(solution)/shard_map/ppermute | solution.py:49
  39.6 3.1 %collective-permute-start.12 = (bf16[4,32,2944]{2,1,0:T(8,128)(2,1)S(1)}, bf16[4,32,2944]{2,1,0:T(8,128)(2,1)S(1)}, u32[]{:S(2)}, u32[]{:S(2)}) collective-permute-start(bf16[4,32,2944]{2,1,0:T(8,128)(2,1)S(1)} %shard_map.65.refs_1_), channel_id=1, source_target_pairs={{0,8},{1,9},{2,10},{3,11},{4,12},{5,13},{6,14},{7,15},{8,0},{9,1},... | collective-permute-start | bytes 2261000 | tf_op jit(solution)/shard_map/ppermute | solution.py:49
  39.7 3.0 %collective-permute-start.13 = (bf16[3,32,2944]{2,1,0:T(8,128)(2,1)S(1)}, bf16[3,32,2944]{2,1,0:T(8,128)(2,1)S(1)}, u32[]{:S(2)}, u32[]{:S(2)}) collective-permute-start(bf16[3,32,2944]{2,1,0:T(8,128)(2,1)S(1)} %shard_map.66.refs_3_), channel_id=1, source_target_pairs={{0,8},{1,9},{2,10},{3,11},{4,12},{5,13},{6,14},{7,15},{8,0},{9,1},... | collective-permute-start | bytes 1695752 | tf_op jit(solution)/shard_map/ppermute | solution.py:49
  40.3 6.7 %collective-permute-start.15 = (bf16[32,2944]{1,0:T(8,128)(2,1)S(1)}, bf16[32,2944]{1,0:T(8,128)(2,1)S(1)}, u32[]{:S(2)}, u32[]{:S(2)}) collective-permute-start(bf16[32,2944]{1,0:T(8,128)(2,1)S(1)} %shard_map.64.refs_3_.refs_4_), channel_id=1, source_target_pairs={{0,16},{1,17},{2,18},{3,19},{4,20},{5,21},{6,22},{7,23},{8,24},{9,... | collective-permute-start | bytes 565256 | tf_op jit(solution)/shard_map/ppermute | solution.py:49
  44.1 9.5 %collective-permute-start.14 = (bf16[256,512]{1,0:T(8,128)(2,1)S(1)}, bf16[256,512]{1,0:T(8,128)(2,1)S(1)}, u32[]{:S(2)}, u32[]{:S(2)}) collective-permute-start(bf16[256,512]{1,0:T(8,128)(2,1)S(1)} %get-tuple-element.26.refs_1_), channel_id=1, source_target_pairs={{0,1},{1,0},{2,3},{3,2},{4,5},{5,4},{6,7},{7,6},{8,9},{9,8},{10,11... | collective-permute-start | bytes 786440 | tf_op jit(solution)/shard_map/ppermute | solution.py:49
  47.0 1.5 %collective-permute-start.16 = (bf16[1,32,2944]{2,1,0:T(8,128)(2,1)S(1)}, bf16[1,32,2944]{2,1,0:T(8,128)(2,1)S(1)}, u32[]{:S(2)}, u32[]{:S(2)}) collective-permute-start(bf16[1,32,2944]{2,1,0:T(8,128)(2,1)S(1)} %shard_map.69.refs_1_), channel_id=1, source_target_pairs={{0,8},{1,9},{2,10},{3,11},{4,12},{5,13},{6,14},{7,15},{8,0},{9,1},... | collective-permute-start | bytes 565256 | tf_op jit(solution)/shard_map/ppermute | solution.py:49
  49.5 4.1 %collective-permute-start.17 = (bf16[128,128]{1,0:T(8,128)(2,1)S(1)}, bf16[128,128]{1,0:T(8,128)(2,1)S(1)}, u32[]{:S(2)}, u32[]{:S(2)}) collective-permute-start(bf16[128,128]{1,0:T(8,128)(2,1)S(1)} %get-tuple-element.28), channel_id=1, source_target_pairs={{0,1},{1,0},{2,3},{3,2},{4,5},{5,4},{6,7},{7,6},{8,9},{9,8},{10,11... | collective-permute-start | bytes 98312 | tf_op jit(solution)/shard_map/ppermute | solution.py:49
  51.6 1.9 %copy-start.4 = (f32[512]{0:T(512)S(1)}, f32[512]{0:T(512)}, u32[]{:S(2)}) copy-start(f32[512]{0:T(512)} %param.9) | copy-start | bytes 6148

commit v5 on v4

--- a/solution.py
+++ b/solution.py
@@ -293,13 +293,12 @@
     keep_ref[...] = product(feature_ref, lax.axis_index("lon") % 2, weight)
 
 
-def rest_kernel(feature_ref, own_ref, crossed_ref, keep_ref, send_ref):
+def rest_kernel(own, feature_ref, own_ref, crossed_ref, sum_ref):
     odd = lax.axis_index("lon") % 2
     weight = jnp.concatenate([own_ref[0], crossed_ref[0]], axis=0)
-    count = keep_ref.shape[0]
-    for strip, ref in ((1 - odd, send_ref), (odd, keep_ref)):
-        total = product(feature_ref, strip, weight)
-        ref[...] = jnp.concatenate([total[:count], total[count:]], axis=1).astype(ref.dtype)
+    count = sum_ref.shape[0]
+    total = product(feature_ref, odd if own else 1 - odd, weight)
+    sum_ref[...] = jnp.concatenate([total[:count], total[count:]], axis=1).astype(sum_ref.dtype)
 
 
 def finish_kernel(last, block, keep_ref, got_ref, keep2_ref, got2_ref, bias_ref, out_ref):
@@ -373,7 +372,6 @@
                     blocks[low ^ bit, mask] = swap(blocks[low, mask], 2 * bit, 0)
 
     cross(order[:1])
-    crossed_first = tuple(blocks[bit, 0] for bit in steps)
     mine, other = call(
         functools.partial(strip_kernel, main),
         (strip, strip),
@@ -418,7 +416,7 @@
     features = features.reshape(2, rows * columns, depth)
     met = [value for key, value in blocks.items() if key != (0, last)]
     blocks[0, last] = call(
-        copy_kernel, block, [], blocks[0, last], after=(*met, band, *(features,))
+        copy_kernel, block, [], blocks[0, last], after=(*met, features)
     )
     cross(order[-1:])
     points = rows * columns
@@ -452,12 +450,20 @@
         keep = call(own_mix_kernel, sums, [], features, weight)
         total = (keep + got.astype(jnp.float32)).reshape(rows, columns, out_columns) + mix_bias
         return jax.nn.gelu(total, approximate=False).astype(jnp.bfloat16)
-    rest = shape((points // 2, LANES), jnp.float32), shape((points // 2, LANES))
-    rest_keep, rest_send = call(
-        rest_kernel, rest, [], features, *stacked(1, order[-1:], (send,))
+    rest, pieces = (points // 2, LANES), stacked(1, order[-1:], (send,))
+    rest_send = call(
+        functools.partial(rest_kernel, False), shape(rest), [], features, *pieces
     )
     rest_got = swap(rest_send, 0, 1)
-    keep = call(own_mix_kernel, sums, [], features, weight)
+    keep = call(own_mix_kernel, sums, [], features, weight, after=(rest_send,))
+    rest_keep = call(
+        functools.partial(rest_kernel, True),
+        shape(rest, jnp.float32),
+        [],
+        features,
+        *pieces,
+        after=(rest_send,),
+    )
     out = call(
         functools.partial(finish_kernel, last, 2 * share),
         shape((points, out_columns)),

time: 54.7 us -> 54.7 us (level)
    pallas_call x17 -> x18, Pallas kernels: 10.3 us -> 10.5 us  [call(): pl.pallas_call(ordered, out_shape=outs, in_specs=[held] * count + [pl.Blo...]
where the time goes in v5:
time: 54.7 us; the launch traced here: 54.5 us
  starting transfers between devices  25.9 us (47%)
  waiting for transfers between devices  15.9 us (29%)
  Pallas kernels  10.5 us (19%)
  local copies, waits for them, and re-layouts  1.94 us (4%)
    ppermute x15, starting transfers between devices, swap(): lax.ppermute(block, AXES, route(lambda lat, lon, lats, lons: (lat ^ lat_b...  15.3 us
    ppermute x15, waiting for transfers between devices, swap(): lax.ppermute(block, AXES, route(lambda lat, lon, lats, lons: (lat ^ lat_b...  10.5 us
    pallas_call x18, Pallas kernels, call(): pl.pallas_call(ordered, out_shape=outs, in_specs=[held] * count + [pl.Blo...  10.5 us
    ppermute x1, starting transfers between devices, body(): across = lax.ppermute(other, AXES, route(across_move))  5.87 us
    ppermute x1, starting transfers between devices, body(): from_outer = lax.ppermute(outer, AXES, route(outer_move))  4.1 us
    ppermute x1, waiting for transfers between devices, body(): along = lax.ppermute(mine, AXES, route(along_move))  2.88 us
    ppermute x1, waiting for transfers between devices, body(): across = lax.ppermute(other, AXES, route(across_move))  2.47 us
    unnamed x10, local copies, waits for them, and re-layouts  1.94 us
  transfers between devices with their start and end apart: 18, of which 9 were waited for; matrix products, arithmetic and copies ran while one was open for 0% of the time, Pallas kernels for 17%

profile of v5, /device:TPU:0, one launch (start us, length us, event | category | flops | bytes accessed | tf_op | source)
XLA Modules:
  0.0 54.5 jit_solution(5743666598504116389)
XLA Ops:
  0.0 1.0 %copy-done = bf16[16,16,641]{2,1,0:T(8,128)(2,1)S(1)} copy-done((bf16[16,16,641]{2,1,0:T(8,128)(2,1)S(1)}, bf16[16,16,641]{2,1,0:T(8,128)(2,1)}, u32[]{:S(2)}) %copy-start) | copy-done | bytes 328216
  1.0 4.1 %collective-permute-start = (bf16[4,16,641]{2,1,0:T(8,128)(2,1)S(1)}, bf16[4,16,641]{2,1,0:T(8,128)(2,1)S(1)}, u32[]{:S(2)}, u32[]{:S(2)}) collective-permute-start(bf16[4,16,641]{2,1,0:T(8,128)(2,1)S(1)} %get-tuple-element.16), channel_id=1, source_target_pairs={{0,4},{1,5},{2,6},{3,7},{4,0},{5,1},{6,2},{7,3},{8,16},{9,17},{10,... | collective-permute-start | bytes 246152 | tf_op jit(solution)/shard_map/ppermute | solution.py:351
  5.1 0.9 %copy-done.2 = bf16[9,641,16]{1,2,0:T(8,128)(2,1)S(1)} copy-done((bf16[9,641,16]{1,2,0:T(8,128)(2,1)S(1)}, bf16[9,641,16]{1,2,0:T(8,128)(2,1)}, u32[]{:S(2)}) %copy-start.2) | copy-done | bytes 184632
  6.2 1.6 %collective-permute-start.5 = (bf16[16,2944]{1,0:T(8,128)(2,1)S(1)}, bf16[16,2944]{1,0:T(8,128)(2,1)S(1)}, u32[]{:S(2)}, u32[]{:S(2)}) collective-permute-start(bf16[16,2944]{1,0:T(8,128)(2,1)S(1)} %get-tuple-element.22), channel_id=1, source_target_pairs={{0,1},{1,0},{2,3},{3,2},{4,5},{5,4},{6,7},{7,6},{8,9},{9,8},{10,11... | collective-permute-start | bytes 282632 | tf_op jit(solution)/shard_map/ppermute | solution.py:49
  7.8 0.2 shard_map.56
  7.9 5.9 %collective-permute-start.3 = (bf16[16,6528]{1,0:T(8,128)(2,1)S(1)}, bf16[16,6528]{1,0:T(8,128)(2,1)S(1)}, u32[]{:S(2)}, u32[]{:S(2)}) collective-permute-start(bf16[16,6528]{1,0:T(8,128)(2,1)S(1)} %get-tuple-element.17), channel_id=1, source_target_pairs={{0,7},{1,2},{2,1},{3,4},{4,3},{5,6},{6,5},{7,0},{8,15},{9,10},{10,... | collective-permute-start | bytes 626696 | tf_op jit(solution)/shard_map/ppermute | solution.py:387
  13.8 0.6 %collective-permute-start.2 = (bf16[16,6528]{1,0:T(8,128)(2,1)S(1)}, bf16[16,6528]{1,0:T(8,128)(2,1)S(1)}, u32[]{:S(2)}, u32[]{:S(2)}) collective-permute-start(bf16[16,6528]{1,0:T(8,128)(2,1)S(1)} %get-tuple-element.18.refs_0_.refs_1_), channel_id=1, source_target_pairs={{0,6},{1,3},{2,0},{3,5},{4,2},{5,7},{6,4},{7,1},{8,14},{9,11},{10,... | collective-permute-start | bytes 626696 | tf_op jit(solution)/shard_map/ppermute | solution.py:386
  14.5 0.5 collective-permute-start.6
  15.0 2.0 %collective-permute-start.7 = (bf16[32,2944]{1,0:T(8,128)(2,1)S(1)}, bf16[32,2944]{1,0:T(8,128)(2,1)S(1)}, u32[]{:S(2)}, u32[]{:S(2)}) collective-permute-start(bf16[32,2944]{1,0:T(8,128)(2,1)S(1)} %shard_map.61.refs_1_.refs_0_), channel_id=1, source_target_pairs={{0,2},{1,3},{2,0},{3,1},{4,6},{5,7},{6,4},{7,5},{8,10},{9,11},{10,... | collective-permute-start | bytes 565256 | tf_op jit(solution)/shard_map/ppermute | solution.py:49
  17.0 2.5 %collective-permute-done.3.refs_3_ = bf16[16,6528]{1,0:T(8,128)(2,1)S(1)} collective-permute-done((bf16[16,6528]{1,0:T(8,128)(2,1)S(1)}, bf16[16,6528]{1,0:T(8,128)(2,1)S(1)}, u32[]{:S(2)}, u32[]{:S(2)}) %collective-permute-start.3) | collective-permute-done | bytes 208928 | tf_op jit(solution)/shard_map/ppermute | solution.py:387
  19.5 1.6 %collective-permute-done.1.refs_2_.refs_1_ = bf16[16,6528]{1,0:T(8,128)(2,1)S(1)} collective-permute-done((bf16[16,6528]{1,0:T(8,128)(2,1)S(1)}, bf16[16,6528]{1,0:T(8,128)(2,1)S(1)}, u32[]{:S(2)}, u32[]{:S(2)}) %collective-permute-start.1) | collective-permute-done | bytes 208928 | tf_op jit(solution)/shard_map/ppermute | solution.py:49
  21.1 2.9 %collective-permute-done.2.refs_2_ = bf16[16,6528]{1,0:T(8,128)(2,1)S(1)} collective-permute-done((bf16[16,6528]{1,0:T(8,128)(2,1)S(1)}, bf16[16,6528]{1,0:T(8,128)(2,1)S(1)}, u32[]{:S(2)}, u32[]{:S(2)}) %collective-permute-start.2) | collective-permute-done | bytes 208928 | tf_op jit(solution)/shard_map/ppermute | solution.py:386
  24.0 0.2 shard_map.58
  24.4 4.0 %collective-permute-done.6.refs_0_ = bf16[32,2944]{1,0:T(8,128)(2,1)S(1)} collective-permute-done((bf16[32,2944]{1,0:T(8,128)(2,1)S(1)}, bf16[32,2944]{1,0:T(8,128)(2,1)S(1)}, u32[]{:S(2)}, u32[]{:S(2)}) %collective-permute-start.6) | collective-permute-done | bytes 188448 | tf_op jit(solution)/shard_map/ppermute | solution.py:49
  28.4 2.3 %collective-permute-start.10 = (bf16[32,2944]{1,0:T(8,128)(2,1)S(1)}, bf16[32,2944]{1,0:T(8,128)(2,1)S(1)}, u32[]{:S(2)}, u32[]{:S(2)}) collective-permute-start(bf16[32,2944]{1,0:T(8,128)(2,1)S(1)} %shard_map.62.refs_2_.refs_1_), channel_id=1, source_target_pairs={{0,16},{1,17},{2,18},{3,19},{4,20},{5,21},{6,22},{7,23},{8,24},{9,... | collective-permute-start | bytes 565256 | tf_op jit(solution)/shard_map/ppermute | solution.py:49
  30.7 2.0 %collective-permute-start.8 = (bf16[32,2944]{1,0:T(8,128)(2,1)S(1)}, bf16[32,2944]{1,0:T(8,128)(2,1)S(1)}, u32[]{:S(2)}, u32[]{:S(2)}) collective-permute-start(bf16[32,2944]{1,0:T(8,128)(2,1)S(1)} %collective-permute-done.6.refs_0_), channel_id=1, source_target_pairs={{0,2},{1,3},{2,0},{3,1},{4,6},{5,7},{6,4},{7,5},{8,10},{9,11},{10,... | collective-permute-start | bytes 565256 | tf_op jit(solution)/shard_map/ppermute | solution.py:49
  32.8 1.4 %shard_map.57.refs_0_ = bf16[8,288,512]{2,1,0:T(8,128)(2,1)S(1)} custom-call(bf16[9,9,16,33]{3,2,1,0:T(8,128)(2,1)S(1)} %bitcast.10, s32[16,9]{1,0:T(8,128)S(1)} %copy-done.3, bf16[16,6528]{1,0:T(8,128)(2,1)S(1)} %collective-permute-done.1.refs_2_.refs_1_), custom_call_target="tpu_custom_call" | custom-call | tf_op jit(solution)/shard_map/pallas_call | solution.py:24
  34.2 3.9 %shard_map.59 = bf16[2,16,16,2944]{3,2,1,0:T(8,128)(2,1)S(1)} custom-call(bf16[8,288,512]{2,1,0:T(8,128)(2,1)S(1)} %shard_map.57.refs_0_, bf16[20,4,16,384]{3,2,1,0:T(8,128)(2,1)S(1)} %get-tuple-element.19.refs_1_, bf16[4,4,16,384]{3,2,1,0:T(8,128)(2,1)S(1)} %collective-permute-done.4.refs_2_), custom_call_target="tpu_custom_call" | custom-call | tf_op jit(solution)/shard_map/pallas_call | solution.py:24
  38.1 1.4 %collective-permute-done.11.refs_6_.refs_2_ = bf16[32,2944]{1,0:T(8,128)(2,1)S(1)} collective-permute-done((bf16[32,2944]{1,0:T(8,128)(2,1)S(1)}, bf16[32,2944]{1,0:T(8,128)(2,1)S(1)}, u32[]{:S(2)}, u32[]{:S(2)}) %collective-permute-start.11) | collective-permute-done | bytes 188448 | tf_op jit(solution)/shard_map/ppermute | solution.py:49
  39.7 0.6 %collective-permute-start.13 = (bf16[3,32,2944]{2,1,0:T(8,128)(2,1)S(1)}, bf16[3,32,2944]{2,1,0:T(8,128)(2,1)S(1)}, u32[]{:S(2)}, u32[]{:S(2)}) collective-permute-start(bf16[3,32,2944]{2,1,0:T(8,128)(2,1)S(1)} %shard_map.66.refs_3_), channel_id=1, source_target_pairs={{0,8},{1,9},{2,10},{3,11},{4,12},{5,13},{6,14},{7,15},{8,0},{9,1},... | collective-permute-start | bytes 1695752 | tf_op jit(solution)/shard_map/ppermute | solution.py:49
  40.3 1.7 %collective-permute-start.14 = (bf16[32,2944]{1,0:T(8,128)(2,1)S(1)}, bf16[32,2944]{1,0:T(8,128)(2,1)S(1)}, u32[]{:S(2)}, u32[]{:S(2)}) collective-permute-start(bf16[32,2944]{1,0:T(8,128)(2,1)S(1)} %shard_map.64.refs_3_.refs_4_), channel_id=1, source_target_pairs={{0,16},{1,17},{2,18},{3,19},{4,20},{5,21},{6,22},{7,23},{8,24},{9,... | collective-permute-start | bytes 565256 | tf_op jit(solution)/shard_map/ppermute | solution.py:49
  41.9 0.8 %collective-permute-done.13.refs_4_ = bf16[3,32,2944]{2,1,0:T(8,128)(2,1)S(1)} collective-permute-done((bf16[3,32,2944]{2,1,0:T(8,128)(2,1)S(1)}, bf16[3,32,2944]{2,1,0:T(8,128)(2,1)S(1)}, u32[]{:S(2)}, u32[]{:S(2)}) %collective-permute-start.13) | collective-permute-done | bytes 565280 | tf_op jit(solution)/shard_map/ppermute | solution.py:49
  42.7 1.4 %shard_map.67 = (bf16[256,512]{1,0:T(8,128)(2,1)S(1)}, bf16[16,32,2944]{2,1,0:T(8,128)(2,1)S(1)}) custom-call(bf16[2,256,2944]{2,1,0:T(8,128)(2,1)S(1)} %bitcast.6, bf16[4,32,2944]{2,1,0:T(8,128)(2,1)S(1)} %shard_map.65.refs_1_, bf16[4,32,2944]{2,1,0:T(8,128)(2,1)S(1)} %collective-permute-done.12.refs_2_, bf16[3,32,2944]{2,1,0:T(8,128)(2,1)S(1)} %shard_map.66.refs_3_, ...), custom_call_target="tpu_custom_call" | custom-call | tf_op jit(solution)/shard_map/pallas_call | solution.py:24
  44.1 2.1 %collective-permute-start.16 = (bf16[256,512]{1,0:T(8,128)(2,1)S(1)}, bf16[256,512]{1,0:T(8,128)(2,1)S(1)}, u32[]{:S(2)}, u32[]{:S(2)}) collective-permute-start(bf16[256,512]{1,0:T(8,128)(2,1)S(1)} %get-tuple-element.24.refs_1_), channel_id=1, source_target_pairs={{0,1},{1,0},{2,3},{3,2},{4,5},{5,4},{6,7},{7,6},{8,9},{9,8},{10,11... | collective-permute-start | bytes 786440 | tf_op jit(solution)/shard_map/ppermute | solution.py:49
  46.2 0.7 %collective-permute-done.14.refs_0_ = bf16[32,2944]{1,0:T(8,128)(2,1)S(1)} collective-permute-done((bf16[32,2944]{1,0:T(8,128)(2,1)S(1)}, bf16[32,2944]{1,0:T(8,128)(2,1)S(1)}, u32[]{:S(2)}, u32[]{:S(2)}) %collective-permute-start.14) | collective-permute-done | bytes 188448 | tf_op jit(solution)/shard_map/ppermute | solution.py:49
  47.1 1.4 %collective-permute-done.15.refs_2_ = bf16[1,32,2944]{2,1,0:T(8,128)(2,1)S(1)} collective-permute-done((bf16[1,32,2944]{2,1,0:T(8,128)(2,1)S(1)}, bf16[1,32,2944]{2,1,0:T(8,128)(2,1)S(1)}, u32[]{:S(2)}, u32[]{:S(2)}) %collective-permute-start.15) | collective-permute-done | bytes 188448 | tf_op jit(solution)/shard_map/ppermute | solution.py:49
  48.5 0.6 %shard_map.69.refs_2_.refs_3_ = bf16[128,128]{1,0:T(8,128)(2,1)S(1)} custom-call(bf16[2,256,2944]{2,1,0:T(8,128)(2,1)S(1)} %bitcast.7, bf16[1,32,2944]{2,1,0:T(8,128)(2,1)S(1)} %shard_map.68.refs_1_, bf16[1,32,2944]{2,1,0:T(8,128)(2,1)S(1)} %collective-permute-done.15.refs_2_), custom_call_target="tpu_custom_call" | custom-call | tf_op jit(solution)/shard_map/pallas_call | solution.py:24
  49.1 2.1 %collective-permute-start.17 = (bf16[128,128]{1,0:T(8,128)(2,1)S(1)}, bf16[128,128]{1,0:T(8,128)(2,1)S(1)}, u32[]{:S(2)}, u32[]{:S(2)}) collective-permute-start(bf16[128,128]{1,0:T(8,128)(2,1)S(1)} %shard_map.69.refs_2_.refs_3_), channel_id=1, source_target_pairs={{0,1},{1,0},{2,3},{3,2},{4,5},{5,4},{6,7},{7,6},{8,9},{9,8},{10,11... | collective-permute-start | bytes 98312 | tf_op jit(solution)/shard_map/ppermute | solution.py:49
  51.2 1.0 %shard_map.70.refs_0_ = f32[256,512]{1,0:T(8,128)S(1)} custom-call(bf16[2,256,2944]{2,1,0:T(8,128)(2,1)S(1)} %bitcast.8, bf16[16,32,2944]{2,1,0:T(8,128)(2,1)S(1)} %get-tuple-element.23.refs_1_, bf16[128,128]{1,0:T(8,128)(2,1)S(1)} %shard_map.69.refs_2_.refs_3_), custom_call_target="tpu_custom_call" | custom-call | tf_op jit(solution)/shard_map/pallas_call | solution.py:24
  52.2 0.6 %shard_map.71.refs_2_ = f32[128,128]{1,0:T(8,128)S(1)} custom-call(bf16[2,256,2944]{2,1,0:T(8,128)(2,1)S(1)} %bitcast.9, bf16[1,32,2944]{2,1,0:T(8,128)(2,1)S(1)} %shard_map.68.refs_1_, bf16[1,32,2944]{2,1,0:T(8,128)(2,1)S(1)} %collective-permute-done.15.refs_2_, bf16[128,128]{1,0:T(8,128)(2,1)S(1)} %shard_map.69.refs_2_.refs_3_), custom_call_target="tpu_custom_call" | custom-call | tf_op jit(solution)/shard_map/pallas_call | solution.py:24
  52.9 0.7 %collective-permute-done.17.refs_3_ = bf16[128,128]{1,0:T(8,128)(2,1)S(1)} collective-permute-done((bf16[128,128]{1,0:T(8,128)(2,1)S(1)}, bf16[128,128]{1,0:T(8,128)(2,1)S(1)}, u32[]{:S(2)}, u32[]{:S(2)}) %collective-permute-start.17) | collective-permute-done | bytes 32800 | tf_op jit(solution)/shard_map/ppermute | solution.py:49
  53.6 0.9 %shard_map.72 = bf16[256,512]{1,0:T(8,128)(2,1)} custom-call(f32[256,512]{1,0:T(8,128)S(1)} %shard_map.70.refs_0_, bf16[256,512]{1,0:T(8,128)(2,1)S(1)} %collective-permute-done.16.refs_1_, f32[128,128]{1,0:T(8,128)S(1)} %shard_map.71.refs_2_, bf16[128,128]{1,0:T(8,128)(2,1)S(1)} %collective-permute-done.17.refs_3_, f32[1,512]{1,0:T(1,128)S(1)} %bitcast.12), custom_call_target="tpu_custom_call" | custom-call | tf_op jit(solution)/shard_map/pallas_call | solution.py:24
  (32 shorter events, 0.8 us)
Async XLA Ops:
  0.0 1.0 %copy-start = (bf16[16,16,641]{2,1,0:T(8,128)(2,1)S(1)}, bf16[16,16,641]{2,1,0:T(8,128)(2,1)}, u32[]{:S(2)}) copy-start(bf16[16,16,641]{2,1,0:T(8,128)(2,1)} %refs_0_.1) | copy-start | bytes 984580
  1.0 31.8 %copy-start.1 = (bf16[9,16,9,33]{3,1,2,0:T(8,128)(2,1)S(1)}, bf16[9,16,9,33]{3,1,2,0:T(8,128)(2,1)}, u32[]{:S(2)}) copy-start(bf16[9,16,9,33]{3,1,2,0:T(8,128)(2,1)} %param.6) | copy-start | bytes 256612
  1.0 31.8 %copy-start.3 = (s32[16,9]{1,0:T(8,128)S(1)}, s32[16,9]{1,0:T(8,128)}, u32[]{:S(2)}) copy-start(s32[16,9]{1,0:T(8,128)} %refs_1_.1) | copy-start | bytes 1732
  1.0 6.7 %collective-permute-start = (bf16[4,16,641]{2,1,0:T(8,128)(2,1)S(1)}, bf16[4,16,641]{2,1,0:T(8,128)(2,1)S(1)}, u32[]{:S(2)}, u32[]{:S(2)}) collective-permute-start(bf16[4,16,641]{2,1,0:T(8,128)(2,1)S(1)} %get-tuple-element.16), channel_id=1, source_target_pairs={{0,4},{1,5},{2,6},{3,7},{4,0},{5,1},{6,2},{7,3},{8,16},{9,17},{10,... | collective-permute-start | bytes 246152 | tf_op jit(solution)/shard_map/ppermute | solution.py:351
  5.1 0.9 %copy-start.2 = (bf16[9,641,16]{1,2,0:T(8,128)(2,1)S(1)}, bf16[9,641,16]{1,2,0:T(8,128)(2,1)}, u32[]{:S(2)}) copy-start(bf16[9,641,16]{1,2,0:T(8,128)(2,1)} %param.8) | copy-start | bytes 553828
  6.2 8.3 %collective-permute-start.5 = (bf16[16,2944]{1,0:T(8,128)(2,1)S(1)}, bf16[16,2944]{1,0:T(8,128)(2,1)S(1)}, u32[]{:S(2)}, u32[]{:S(2)}) collective-permute-start(bf16[16,2944]{1,0:T(8,128)(2,1)S(1)} %get-tuple-element.22), channel_id=1, source_target_pairs={{0,1},{1,0},{2,3},{3,2},{4,5},{5,4},{6,7},{7,6},{8,9},{9,8},{10,11... | collective-permute-start | bytes 282632 | tf_op jit(solution)/shard_map/ppermute | solution.py:49
  7.9 11.5 %collective-permute-start.3 = (bf16[16,6528]{1,0:T(8,128)(2,1)S(1)}, bf16[16,6528]{1,0:T(8,128)(2,1)S(1)}, u32[]{:S(2)}, u32[]{:S(2)}) collective-permute-start(bf16[16,6528]{1,0:T(8,128)(2,1)S(1)} %get-tuple-element.17), channel_id=1, source_target_pairs={{0,7},{1,2},{2,1},{3,4},{4,3},{5,6},{6,5},{7,0},{8,15},{9,10},{10,... | collective-permute-start | bytes 626696 | tf_op jit(solution)/shard_map/ppermute | solution.py:387
  13.8 7.3 %collective-permute-start.1 = (bf16[16,6528]{1,0:T(8,128)(2,1)S(1)}, bf16[16,6528]{1,0:T(8,128)(2,1)S(1)}, u32[]{:S(2)}, u32[]{:S(2)}) collective-permute-start(bf16[16,6528]{1,0:T(8,128)(2,1)S(1)} %get-tuple-element.17), channel_id=1, source_target_pairs={{0,1},{1,0},{2,3},{3,2},{4,5},{5,4},{6,7},{7,6},{8,9},{9,8},{10,11... | collective-permute-start | bytes 626696 | tf_op jit(solution)/shard_map/ppermute | solution.py:49
  13.8 10.1 %collective-permute-start.2 = (bf16[16,6528]{1,0:T(8,128)(2,1)S(1)}, bf16[16,6528]{1,0:T(8,128)(2,1)S(1)}, u32[]{:S(2)}, u32[]{:S(2)}) collective-permute-start(bf16[16,6528]{1,0:T(8,128)(2,1)S(1)} %get-tuple-element.18.refs_0_.refs_1_), channel_id=1, source_target_pairs={{0,6},{1,3},{2,0},{3,5},{4,2},{5,7},{6,4},{7,1},{8,14},{9,11},{10,... | collective-permute-start | bytes 626696 | tf_op jit(solution)/shard_map/ppermute | solution.py:386
  14.5 13.9 %collective-permute-start.6 = (bf16[32,2944]{1,0:T(8,128)(2,1)S(1)}, bf16[32,2944]{1,0:T(8,128)(2,1)S(1)}, u32[]{:S(2)}, u32[]{:S(2)}) collective-permute-start(bf16[32,2944]{1,0:T(8,128)(2,1)S(1)} %shard_map.61.refs_1_.refs_0_), channel_id=1, source_target_pairs={{0,4},{1,5},{2,6},{3,7},{4,0},{5,1},{6,2},{7,3},{8,12},{9,13},{10,... | collective-permute-start | bytes 565256 | tf_op jit(solution)/shard_map/ppermute | solution.py:49
  15.0 17.7 %collective-permute-start.7 = (bf16[32,2944]{1,0:T(8,128)(2,1)S(1)}, bf16[32,2944]{1,0:T(8,128)(2,1)S(1)}, u32[]{:S(2)}, u32[]{:S(2)}) collective-permute-start(bf16[32,2944]{1,0:T(8,128)(2,1)S(1)} %shard_map.61.refs_1_.refs_0_), channel_id=1, source_target_pairs={{0,2},{1,3},{2,0},{3,1},{4,6},{5,7},{6,4},{7,5},{8,10},{9,11},{10,... | collective-permute-start | bytes 565256 | tf_op jit(solution)/shard_map/ppermute | solution.py:49
  24.2 10.0 %collective-permute-start.4 = (bf16[4,4,16,384]{3,2,1,0:T(8,128)(2,1)S(1)}, bf16[4,4,16,384]{3,2,1,0:T(8,128)(2,1)S(1)}, u32[]{:S(2)}, u32[]{:S(2)}) collective-permute-start(bf16[4,4,16,384]{3,2,1,0:T(8,128)(2,1)S(1)} %get-tuple-element.20), channel_id=1, source_target_pairs={{0,8},{1,9},{2,10},{3,11},{4,12},{5,13},{6,14},{7,15},{8,0},{9,1},... | collective-permute-start | bytes 589832 | tf_op jit(solution)/shard_map/ppermute | solution.py:49
  24.3 13.8 %collective-permute-start.9 = (bf16[32,2944]{1,0:T(8,128)(2,1)S(1)}, bf16[32,2944]{1,0:T(8,128)(2,1)S(1)}, u32[]{:S(2)}, u32[]{:S(2)}) collective-permute-start(bf16[32,2944]{1,0:T(8,128)(2,1)S(1)} %shard_map.61.refs_1_.refs_0_), channel_id=1, source_target_pairs={{0,16},{1,17},{2,18},{3,19},{4,20},{5,21},{6,22},{7,23},{8,24},{9,... | collective-permute-start | bytes 565256 | tf_op jit(solution)/shard_map/ppermute | solution.py:49
  28.4 9.8 %collective-permute-start.10 = (bf16[32,2944]{1,0:T(8,128)(2,1)S(1)}, bf16[32,2944]{1,0:T(8,128)(2,1)S(1)}, u32[]{:S(2)}, u32[]{:S(2)}) collective-permute-start(bf16[32,2944]{1,0:T(8,128)(2,1)S(1)} %shard_map.62.refs_2_.refs_1_), channel_id=1, source_target_pairs={{0,16},{1,17},{2,18},{3,19},{4,20},{5,21},{6,22},{7,23},{8,24},{9,... | collective-permute-start | bytes 565256 | tf_op jit(solution)/shard_map/ppermute | solution.py:49
  30.7 7.5 %collective-permute-start.8 = (bf16[32,2944]{1,0:T(8,128)(2,1)S(1)}, bf16[32,2944]{1,0:T(8,128)(2,1)S(1)}, u32[]{:S(2)}, u32[]{:S(2)}) collective-permute-start(bf16[32,2944]{1,0:T(8,128)(2,1)S(1)} %collective-permute-done.6.refs_0_), channel_id=1, source_target_pairs={{0,2},{1,3},{2,0},{3,1},{4,6},{5,7},{6,4},{7,5},{8,10},{9,11},{10,... | collective-permute-start | bytes 565256 | tf_op jit(solution)/shard_map/ppermute | solution.py:49
  32.7 6.8 %collective-permute-start.11 = (bf16[32,2944]{1,0:T(8,128)(2,1)S(1)}, bf16[32,2944]{1,0:T(8,128)(2,1)S(1)}, u32[]{:S(2)}, u32[]{:S(2)}) collective-permute-start(bf16[32,2944]{1,0:T(8,128)(2,1)S(1)} %shard_map.63.refs_3_.refs_2_), channel_id=1, source_target_pairs={{0,16},{1,17},{2,18},{3,19},{4,20},{5,21},{6,22},{7,23},{8,24},{9,... | collective-permute-start | bytes 565256 | tf_op jit(solution)/shard_map/ppermute | solution.py:49
  39.6 3.1 %collective-permute-start.12 = (bf16[4,32,2944]{2,1,0:T(8,128)(2,1)S(1)}, bf16[4,32,2944]{2,1,0:T(8,128)(2,1)S(1)}, u32[]{:S(2)}, u32[]{:S(2)}) collective-permute-start(bf16[4,32,2944]{2,1,0:T(8,128)(2,1)S(1)} %shard_map.65.refs_1_), channel_id=1, source_target_pairs={{0,8},{1,9},{2,10},{3,11},{4,12},{5,13},{6,14},{7,15},{8,0},{9,1},... | collective-permute-start | bytes 2261000 | tf_op jit(solution)/shard_map/ppermute | solution.py:49
  39.7 3.0 %collective-permute-start.13 = (bf16[3,32,2944]{2,1,0:T(8,128)(2,1)S(1)}, bf16[3,32,2944]{2,1,0:T(8,128)(2,1)S(1)}, u32[]{:S(2)}, u32[]{:S(2)}) collective-permute-start(bf16[3,32,2944]{2,1,0:T(8,128)(2,1)S(1)} %shard_map.66.refs_3_), channel_id=1, source_target_pairs={{0,8},{1,9},{2,10},{3,11},{4,12},{5,13},{6,14},{7,15},{8,0},{9,1},... | collective-permute-start | bytes 1695752 | tf_op jit(solution)/shard_map/ppermute | solution.py:49
  40.3 6.7 %collective-permute-start.14 = (bf16[32,2944]{1,0:T(8,128)(2,1)S(1)}, bf16[32,2944]{1,0:T(8,128)(2,1)S(1)}, u32[]{:S(2)}, u32[]{:S(2)}) collective-permute-start(bf16[32,2944]{1,0:T(8,128)(2,1)S(1)} %shard_map.64.refs_3_.refs_4_), channel_id=1, source_target_pairs={{0,16},{1,17},{2,18},{3,19},{4,20},{5,21},{6,22},{7,23},{8,24},{9,... | collective-permute-start | bytes 565256 | tf_op jit(solution)/shard_map/ppermute | solution.py:49
  44.1 9.4 %collective-permute-start.16 = (bf16[256,512]{1,0:T(8,128)(2,1)S(1)}, bf16[256,512]{1,0:T(8,128)(2,1)S(1)}, u32[]{:S(2)}, u32[]{:S(2)}) collective-permute-start(bf16[256,512]{1,0:T(8,128)(2,1)S(1)} %get-tuple-element.24.refs_1_), channel_id=1, source_target_pairs={{0,1},{1,0},{2,3},{3,2},{4,5},{5,4},{6,7},{7,6},{8,9},{9,8},{10,11... | collective-permute-start | bytes 786440 | tf_op jit(solution)/shard_map/ppermute | solution.py:49
  47.0 1.5 %collective-permute-start.15 = (bf16[1,32,2944]{2,1,0:T(8,128)(2,1)S(1)}, bf16[1,32,2944]{2,1,0:T(8,128)(2,1)S(1)}, u32[]{:S(2)}, u32[]{:S(2)}) collective-permute-start(bf16[1,32,2944]{2,1,0:T(8,128)(2,1)S(1)} %shard_map.68.refs_1_), channel_id=1, source_target_pairs={{0,8},{1,9},{2,10},{3,11},{4,12},{5,13},{6,14},{7,15},{8,0},{9,1},... | collective-permute-start | bytes 565256 | tf_op jit(solution)/shard_map/ppermute | solution.py:49
  49.1 4.5 %collective-permute-start.17 = (bf16[128,128]{1,0:T(8,128)(2,1)S(1)}, bf16[128,128]{1,0:T(8,128)(2,1)S(1)}, u32[]{:S(2)}, u32[]{:S(2)}) collective-permute-start(bf16[128,128]{1,0:T(8,128)(2,1)S(1)} %shard_map.69.refs_2_.refs_3_), channel_id=1, source_target_pairs={{0,1},{1,0},{2,3},{3,2},{4,5},{5,4},{6,7},{7,6},{8,9},{9,8},{10,11... | collective-permute-start | bytes 98312 | tf_op jit(solution)/shard_map/ppermute | solution.py:49
  52.2 1.3 %copy-start.4 = (f32[512]{0:T(512)S(1)}, f32[512]{0:T(512)}, u32[]{:S(2)}) copy-start(f32[512]{0:T(512)} %param.9) | copy-start | bytes 6148

commit v6 on v5

--- a/solution.py
+++ b/solution.py
@@ -278,11 +278,11 @@
     send_ref, weight_ref = refs[len(sources) :]
     lat, lon = lax.axis_index("lat"), lax.axis_index("lon")
     masks = lax.axis_size("lon") // 2
-    if sum(len(held) for _, _, held in sources) < weight_ref.shape[0]:
+    if sum(len(keys) for _, keys in sources) < weight_ref.shape[0]:
         weight_ref[...] = jnp.zeros_like(weight_ref)
-    for (core, low, held), ref in zip(sources, piece_refs):
-        row = 2 * ((lat // 2) ^ low) + (lat % 2 ^ core)
-        for at, mask in enumerate(held):
+    for (core, keys), ref in zip(sources, piece_refs):
+        for at, (low, mask) in enumerate(keys):
+            row = 2 * ((lat // 2) ^ low) + (lat % 2 ^ core)
             weight_ref[row * masks + ((lon // 2) ^ mask)] = ref[at]
     weight = weight_ref[...].reshape(send_ref.shape[1], weight_ref.shape[2])
     send_ref[...] = product(feature_ref, 1 - lon % 2, weight).astype(send_ref.dtype)
@@ -421,22 +421,21 @@
     cross(order[-1:])
     points = rows * columns
 
-    def stacked(low, held, after):
+    def stacked(keys, after):
+        values = [blocks[key] for key in keys]
         piece = call(
-            stack_kernel,
-            shape((len(held),) + block.shape),
-            [],
-            *[blocks[low, mask] for mask in held],
-            after=after,
+            stack_kernel, shape((len(keys),) + block.shape), [], *values, after=after
         )
         return [piece, swap(piece, 1, 0)]
 
     apart = lat_masks == 2 and 8 * share == LANES == lon_masks * 2 * share and points % 2 == 0
+    early = [key for key in blocks if key[1] == 0 or (key[0] == 0 and key[1] != last)]
+    late = [key for key in blocks if key not in early and not (apart and key == (1, last))]
     sources, pieces = [], []
-    for low in range(lat_masks):
-        held = order[:-1] if low and apart else order
-        sources += [(core, low, held) for core in range(2)]
-        pieces += stacked(low, held, (blocks[0, last],) if low == 0 else (blocks[0, last],))
+    for keys, after in ((early, (slab,)), (late, (features,))):
+        if keys:
+            sources += [(core, keys) for core in range(2)]
+            pieces += stacked(keys, after)
     send, weight = call(
         functools.partial(partner_mix_kernel, sources),
         (shape((points, out_columns)), shape((lats * lon_masks,) + block.shape)),
@@ -450,7 +449,7 @@
         keep = call(own_mix_kernel, sums, [], features, weight)
         total = (keep + got.astype(jnp.float32)).reshape(rows, columns, out_columns) + mix_bias
         return jax.nn.gelu(total, approximate=False).astype(jnp.bfloat16)
-    rest, pieces = (points // 2, LANES), stacked(1, order[-1:], (send,))
+    rest, pieces = (points // 2, LANES), stacked([(1, last)], (send,))
     rest_send = call(
         functools.partial(rest_kernel, False), shape(rest), [], features, *pieces
     )

time: 54.7 us -> 55.3 us (1.011)
  starting transfers between devices: 25.9 us -> 26.7 us
    ppermute x1, starting transfers between devices: 5.87 us -> 0.97 us  [body(): across = lax.ppermute(other, AXES, route(across_move))]
    ppermute x1, starting transfers between devices: 0.64 us -> 4.92 us  [body(): along = lax.ppermute(mine, AXES, route(along_move))]
    ppermute x1, waiting for transfers between devices: 2.88 us -> 0.01 us  [body(): along = lax.ppermute(mine, AXES, route(along_move))]
    ppermute x1, waiting for transfers between devices: 0.01 us -> 2.6 us  [body(): from_outer = lax.ppermute(outer, AXES, route(outer_move))]
    ppermute x15, starting transfers between devices: 15.3 us -> 16.7 us  [swap(): lax.ppermute(block, AXES, route(lambda lat, lon, lats, lons: (lat ^ lat_b...]
where the time goes in v6:
time: 55.3 us; the launch traced here: 55.2 us
  starting transfers between devices  26.7 us (48%)
  waiting for transfers between devices  15.8 us (29%)
  Pallas kernels  10.5 us (19%)
  local copies, waits for them, and re-layouts  1.94 us (4%)
    ppermute x15, starting transfers between devices, swap(): lax.ppermute(block, AXES, route(lambda lat, lon, lats, lons: (lat ^ lat_b...  16.7 us
    pallas_call x18, Pallas kernels, call(): pl.pallas_call(ordered, out_shape=outs, in_specs=[held] * count + [pl.Blo...  10.5 us
    ppermute x15, waiting for transfers between devices, swap(): lax.ppermute(block, AXES, route(lambda lat, lon, lats, lons: (lat ^ lat_b...  10.4 us
    ppermute x1, starting transfers between devices, body(): along = lax.ppermute(mine, AXES, route(along_move))  4.92 us
    ppermute x1, starting transfers between devices, body(): from_outer = lax.ppermute(outer, AXES, route(outer_move))  4.1 us
    ppermute x1, waiting for transfers between devices, body(): across = lax.ppermute(other, AXES, route(across_move))  2.86 us
    ppermute x1, waiting for transfers between devices, body(): from_outer = lax.ppermute(outer, AXES, route(outer_move))  2.6 us
    unnamed x10, local copies, waits for them, and re-layouts  1.94 us
  transfers between devices with their start and end apart: 18, of which 9 were waited for; matrix products, arithmetic and copies ran while one was open for 0% of the time, Pallas kernels for 17%

profile of v6, /device:TPU:0, one launch (start us, length us, event | category | flops | bytes accessed | tf_op | source)
XLA Modules:
  0.0 55.2 jit_solution(7110850837839531575)
XLA Ops:
  0.0 1.0 %copy-done = bf16[16,16,641]{2,1,0:T(8,128)(2,1)S(1)} copy-done((bf16[16,16,641]{2,1,0:T(8,128)(2,1)S(1)}, bf16[16,16,641]{2,1,0:T(8,128)(2,1)}, u32[]{:S(2)}) %copy-start) | copy-done | bytes 328216
  1.0 4.1 %collective-permute-start = (bf16[4,16,641]{2,1,0:T(8,128)(2,1)S(1)}, bf16[4,16,641]{2,1,0:T(8,128)(2,1)S(1)}, u32[]{:S(2)}, u32[]{:S(2)}) collective-permute-start(bf16[4,16,641]{2,1,0:T(8,128)(2,1)S(1)} %get-tuple-element.16), channel_id=1, source_target_pairs={{0,4},{1,5},{2,6},{3,7},{4,0},{5,1},{6,2},{7,3},{8,16},{9,17},{10,... | collective-permute-start | bytes 246152 | tf_op jit(solution)/shard_map/ppermute | solution.py:351
  5.1 2.6 %collective-permute-done.refs_1_ = bf16[4,16,641]{2,1,0:T(8,128)(2,1)S(1)} collective-permute-done((bf16[4,16,641]{2,1,0:T(8,128)(2,1)S(1)}, bf16[4,16,641]{2,1,0:T(8,128)(2,1)S(1)}, u32[]{:S(2)}, u32[]{:S(2)}) %collective-permute-start) | collective-permute-done | bytes 82080 | tf_op jit(solution)/shard_map/ppermute | solution.py:351
  7.9 4.9 %collective-permute-start.2 = (bf16[16,6528]{1,0:T(8,128)(2,1)S(1)}, bf16[16,6528]{1,0:T(8,128)(2,1)S(1)}, u32[]{:S(2)}, u32[]{:S(2)}) collective-permute-start(bf16[16,6528]{1,0:T(8,128)(2,1)S(1)} %get-tuple-element.18.refs_0_.refs_1_), channel_id=1, source_target_pairs={{0,6},{1,3},{2,0},{3,5},{4,2},{5,7},{6,4},{7,1},{8,14},{9,11},{10,... | collective-permute-start | bytes 626696 | tf_op jit(solution)/shard_map/ppermute | solution.py:386
  12.8 0.9 %copy-done.2 = bf16[9,641,16]{1,2,0:T(8,128)(2,1)S(1)} copy-done((bf16[9,641,16]{1,2,0:T(8,128)(2,1)S(1)}, bf16[9,641,16]{1,2,0:T(8,128)(2,1)}, u32[]{:S(2)}) %copy-start.2) | copy-done | bytes 184632
  14.0 2.0 %collective-permute-start.1 = (bf16[16,6528]{1,0:T(8,128)(2,1)S(1)}, bf16[16,6528]{1,0:T(8,128)(2,1)S(1)}, u32[]{:S(2)}, u32[]{:S(2)}) collective-permute-start(bf16[16,6528]{1,0:T(8,128)(2,1)S(1)} %get-tuple-element.17), channel_id=1, source_target_pairs={{0,1},{1,0},{2,3},{3,2},{4,5},{5,4},{6,7},{7,6},{8,9},{9,8},{10,11... | collective-permute-start | bytes 626696 | tf_op jit(solution)/shard_map/ppermute | solution.py:49
  16.0 1.0 %collective-permute-start.3 = (bf16[16,6528]{1,0:T(8,128)(2,1)S(1)}, bf16[16,6528]{1,0:T(8,128)(2,1)S(1)}, u32[]{:S(2)}, u32[]{:S(2)}) collective-permute-start(bf16[16,6528]{1,0:T(8,128)(2,1)S(1)} %get-tuple-element.17), channel_id=1, source_target_pairs={{0,7},{1,2},{2,1},{3,4},{4,3},{5,6},{6,5},{7,0},{8,15},{9,10},{10,... | collective-permute-start | bytes 626696 | tf_op jit(solution)/shard_map/ppermute | solution.py:387
  16.9 3.8 %collective-permute-done.5.refs_1_ = bf16[16,2944]{1,0:T(8,128)(2,1)S(1)} collective-permute-done((bf16[16,2944]{1,0:T(8,128)(2,1)S(1)}, bf16[16,2944]{1,0:T(8,128)(2,1)S(1)}, u32[]{:S(2)}, u32[]{:S(2)}) %collective-permute-start.5) | collective-permute-done | bytes 94240 | tf_op jit(solution)/shard_map/ppermute | solution.py:49
  20.8 0.4 collective-permute-start.6
  21.2 0.2 collective-permute-start.7
  21.4 0.3 collective-permute-start.8
  21.7 2.0 %collective-permute-done.1.refs_2_.refs_1_ = bf16[16,6528]{1,0:T(8,128)(2,1)S(1)} collective-permute-done((bf16[16,6528]{1,0:T(8,128)(2,1)S(1)}, bf16[16,6528]{1,0:T(8,128)(2,1)S(1)}, u32[]{:S(2)}, u32[]{:S(2)}) %collective-permute-start.1) | collective-permute-done | bytes 208928 | tf_op jit(solution)/shard_map/ppermute | solution.py:49
  23.7 2.9 %collective-permute-done.3.refs_3_ = bf16[16,6528]{1,0:T(8,128)(2,1)S(1)} collective-permute-done((bf16[16,6528]{1,0:T(8,128)(2,1)S(1)}, bf16[16,6528]{1,0:T(8,128)(2,1)S(1)}, u32[]{:S(2)}, u32[]{:S(2)}) %collective-permute-start.3) | collective-permute-done | bytes 208928 | tf_op jit(solution)/shard_map/ppermute | solution.py:387
  26.5 0.2 shard_map.58
  26.9 2.4 %collective-permute-done.6.refs_0_ = bf16[32,2944]{1,0:T(8,128)(2,1)S(1)} collective-permute-done((bf16[32,2944]{1,0:T(8,128)(2,1)S(1)}, bf16[32,2944]{1,0:T(8,128)(2,1)S(1)}, u32[]{:S(2)}, u32[]{:S(2)}) %collective-permute-start.6) | collective-permute-done | bytes 188448 | tf_op jit(solution)/shard_map/ppermute | solution.py:49
  29.2 1.0 %collective-permute-start.11 = (bf16[32,2944]{1,0:T(8,128)(2,1)S(1)}, bf16[32,2944]{1,0:T(8,128)(2,1)S(1)}, u32[]{:S(2)}, u32[]{:S(2)}) collective-permute-start(bf16[32,2944]{1,0:T(8,128)(2,1)S(1)} %shard_map.62.refs_1_.refs_2_), channel_id=1, source_target_pairs={{0,16},{1,17},{2,18},{3,19},{4,20},{5,21},{6,22},{7,23},{8,24},{9,... | collective-permute-start | bytes 565256 | tf_op jit(solution)/shard_map/ppermute | solution.py:49
  30.2 1.2 %collective-permute-start.12 = (bf16[32,2944]{1,0:T(8,128)(2,1)S(1)}, bf16[32,2944]{1,0:T(8,128)(2,1)S(1)}, u32[]{:S(2)}, u32[]{:S(2)}) collective-permute-start(bf16[32,2944]{1,0:T(8,128)(2,1)S(1)} %shard_map.63.refs_2_.refs_3_), channel_id=1, source_target_pairs={{0,16},{1,17},{2,18},{3,19},{4,20},{5,21},{6,22},{7,23},{8,24},{9,... | collective-permute-start | bytes 565256 | tf_op jit(solution)/shard_map/ppermute | solution.py:49
  31.4 1.1 %collective-permute-start.10 = (bf16[32,2944]{1,0:T(8,128)(2,1)S(1)}, bf16[32,2944]{1,0:T(8,128)(2,1)S(1)}, u32[]{:S(2)}, u32[]{:S(2)}) collective-permute-start(bf16[32,2944]{1,0:T(8,128)(2,1)S(1)} %collective-permute-done.6.refs_0_), channel_id=1, source_target_pairs={{0,2},{1,3},{2,0},{3,1},{4,6},{5,7},{6,4},{7,5},{8,10},{9,11},{10,... | collective-permute-start | bytes 565256 | tf_op jit(solution)/shard_map/ppermute | solution.py:49
  32.7 1.4 %shard_map.57.refs_0_ = bf16[8,288,512]{2,1,0:T(8,128)(2,1)S(1)} custom-call(bf16[9,9,16,33]{3,2,1,0:T(8,128)(2,1)S(1)} %bitcast.11, s32[16,9]{1,0:T(8,128)S(1)} %copy-done.3, bf16[16,6528]{1,0:T(8,128)(2,1)S(1)} %collective-permute-done.1.refs_2_.refs_1_), custom_call_target="tpu_custom_call" | custom-call | tf_op jit(solution)/shard_map/pallas_call | solution.py:24
  34.1 3.9 %shard_map.59 = bf16[2,16,16,2944]{3,2,1,0:T(8,128)(2,1)S(1)} custom-call(bf16[8,288,512]{2,1,0:T(8,128)(2,1)S(1)} %shard_map.57.refs_0_, bf16[20,4,16,384]{3,2,1,0:T(8,128)(2,1)S(1)} %get-tuple-element.19.refs_1_.refs_4_, bf16[4,4,16,384]{3,2,1,0:T(8,128)(2,1)S(1)} %collective-permute-done.4.refs_2_), custom_call_target="tpu_custom_call" | custom-call | tf_op jit(solution)/shard_map/pallas_call | solution.py:24
  38.2 0.5 collective-permute-start.13
  38.7 1.2 %collective-permute-start.14 = (bf16[32,2944]{1,0:T(8,128)(2,1)S(1)}, bf16[32,2944]{1,0:T(8,128)(2,1)S(1)}, u32[]{:S(2)}, u32[]{:S(2)}) collective-permute-start(bf16[32,2944]{1,0:T(8,128)(2,1)S(1)} %shard_map.65.refs_0_), channel_id=1, source_target_pairs={{0,16},{1,17},{2,18},{3,19},{4,20},{5,21},{6,22},{7,23},{8,24},{9,... | collective-permute-start | bytes 565256 | tf_op jit(solution)/shard_map/ppermute | solution.py:49
  39.8 0.4 collective-permute-done.13.refs_4_
  40.2 1.4 %shard_map.67 = (bf16[256,512]{1,0:T(8,128)(2,1)S(1)}, bf16[16,32,2944]{2,1,0:T(8,128)(2,1)S(1)}) custom-call(bf16[2,256,2944]{2,1,0:T(8,128)(2,1)S(1)} %bitcast.7, bf16[4,32,2944]{2,1,0:T(8,128)(2,1)S(1)} %shard_map.64.refs_1_, bf16[4,32,2944]{2,1,0:T(8,128)(2,1)S(1)} %collective-permute-done.9.refs_2_, bf16[3,32,2944]{2,1,0:T(8,128)(2,1)S(1)} %shard_map.66.refs_3_, ...), custom_call_target="tpu_custom_call" | custom-call | tf_op jit(solution)/shard_map/pallas_call | solution.py:24
  41.7 4.8 %collective-permute-start.16 = (bf16[256,512]{1,0:T(8,128)(2,1)S(1)}, bf16[256,512]{1,0:T(8,128)(2,1)S(1)}, u32[]{:S(2)}, u32[]{:S(2)}) collective-permute-start(bf16[256,512]{1,0:T(8,128)(2,1)S(1)} %get-tuple-element.24.refs_1_), channel_id=1, source_target_pairs={{0,1},{1,0},{2,3},{3,2},{4,5},{5,4},{6,7},{7,6},{8,9},{9,8},{10,11... | collective-permute-start | bytes 786440 | tf_op jit(solution)/shard_map/ppermute | solution.py:49
  46.5 1.4 %collective-permute-done.15.refs_2_ = bf16[1,32,2944]{2,1,0:T(8,128)(2,1)S(1)} collective-permute-done((bf16[1,32,2944]{2,1,0:T(8,128)(2,1)S(1)}, bf16[1,32,2944]{2,1,0:T(8,128)(2,1)S(1)}, u32[]{:S(2)}, u32[]{:S(2)}) %collective-permute-start.15) | collective-permute-done | bytes 188448 | tf_op jit(solution)/shard_map/ppermute | solution.py:49
  48.0 0.6 %shard_map.69.refs_2_.refs_3_ = bf16[128,128]{1,0:T(8,128)(2,1)S(1)} custom-call(bf16[2,256,2944]{2,1,0:T(8,128)(2,1)S(1)} %bitcast.8, bf16[1,32,2944]{2,1,0:T(8,128)(2,1)S(1)} %shard_map.68.refs_1_, bf16[1,32,2944]{2,1,0:T(8,128)(2,1)S(1)} %collective-permute-done.15.refs_2_), custom_call_target="tpu_custom_call" | custom-call | tf_op jit(solution)/shard_map/pallas_call | solution.py:24
  48.6 3.8 %collective-permute-start.17 = (bf16[128,128]{1,0:T(8,128)(2,1)S(1)}, bf16[128,128]{1,0:T(8,128)(2,1)S(1)}, u32[]{:S(2)}, u32[]{:S(2)}) collective-permute-start(bf16[128,128]{1,0:T(8,128)(2,1)S(1)} %shard_map.69.refs_2_.refs_3_), channel_id=1, source_target_pairs={{0,1},{1,0},{2,3},{3,2},{4,5},{5,4},{6,7},{7,6},{8,9},{9,8},{10,11... | collective-permute-start | bytes 98312 | tf_op jit(solution)/shard_map/ppermute | solution.py:49
  52.3 1.0 %shard_map.70.refs_0_ = f32[256,512]{1,0:T(8,128)S(1)} custom-call(bf16[2,256,2944]{2,1,0:T(8,128)(2,1)S(1)} %bitcast.9, bf16[16,32,2944]{2,1,0:T(8,128)(2,1)S(1)} %get-tuple-element.23.refs_1_, bf16[128,128]{1,0:T(8,128)(2,1)S(1)} %shard_map.69.refs_2_.refs_3_), custom_call_target="tpu_custom_call" | custom-call | tf_op jit(solution)/shard_map/pallas_call | solution.py:24
  53.4 0.6 %shard_map.71.refs_2_ = f32[128,128]{1,0:T(8,128)S(1)} custom-call(bf16[2,256,2944]{2,1,0:T(8,128)(2,1)S(1)} %bitcast.10, bf16[1,32,2944]{2,1,0:T(8,128)(2,1)S(1)} %shard_map.68.refs_1_, bf16[1,32,2944]{2,1,0:T(8,128)(2,1)S(1)} %collective-permute-done.15.refs_2_, bf16[128,128]{1,0:T(8,128)(2,1)S(1)} %shard_map.69.refs_2_.refs_3_), custom_call_target="tpu_custom_call" | custom-call | tf_op jit(solution)/shard_map/pallas_call | solution.py:24
  54.0 0.3 collective-permute-done.17.refs_3_
  54.2 0.9 %shard_map.72 = bf16[256,512]{1,0:T(8,128)(2,1)} custom-call(f32[256,512]{1,0:T(8,128)S(1)} %shard_map.70.refs_0_, bf16[256,512]{1,0:T(8,128)(2,1)S(1)} %collective-permute-done.16.refs_1_, f32[128,128]{1,0:T(8,128)S(1)} %shard_map.71.refs_2_, bf16[128,128]{1,0:T(8,128)(2,1)S(1)} %collective-permute-done.17.refs_3_, f32[1,512]{1,0:T(1,128)S(1)} %bitcast.13), custom_call_target="tpu_custom_call" | custom-call | tf_op jit(solution)/shard_map/pallas_call | solution.py:24
  (32 shorter events, 0.9 us)
Async XLA Ops:
  0.0 1.0 %copy-start = (bf16[16,16,641]{2,1,0:T(8,128)(2,1)S(1)}, bf16[16,16,641]{2,1,0:T(8,128)(2,1)}, u32[]{:S(2)}) copy-start(bf16[16,16,641]{2,1,0:T(8,128)(2,1)} %refs_0_.1) | copy-start | bytes 984580
  1.0 31.7 %copy-start.1 = (bf16[9,16,9,33]{3,1,2,0:T(8,128)(2,1)S(1)}, bf16[9,16,9,33]{3,1,2,0:T(8,128)(2,1)}, u32[]{:S(2)}) copy-start(bf16[9,16,9,33]{3,1,2,0:T(8,128)(2,1)} %param.6) | copy-start | bytes 256612
  1.0 31.7 %copy-start.3 = (s32[16,9]{1,0:T(8,128)S(1)}, s32[16,9]{1,0:T(8,128)}, u32[]{:S(2)}) copy-start(s32[16,9]{1,0:T(8,128)} %refs_1_.1) | copy-start | bytes 1732
  1.0 6.7 %collective-permute-start = (bf16[4,16,641]{2,1,0:T(8,128)(2,1)S(1)}, bf16[4,16,641]{2,1,0:T(8,128)(2,1)S(1)}, u32[]{:S(2)}, u32[]{:S(2)}) collective-permute-start(bf16[4,16,641]{2,1,0:T(8,128)(2,1)S(1)} %get-tuple-element.16), channel_id=1, source_target_pairs={{0,4},{1,5},{2,6},{3,7},{4,0},{5,1},{6,2},{7,3},{8,16},{9,17},{10,... | collective-permute-start | bytes 246152 | tf_op jit(solution)/shard_map/ppermute | solution.py:351
  7.9 13.5 %collective-permute-start.2 = (bf16[16,6528]{1,0:T(8,128)(2,1)S(1)}, bf16[16,6528]{1,0:T(8,128)(2,1)S(1)}, u32[]{:S(2)}, u32[]{:S(2)}) collective-permute-start(bf16[16,6528]{1,0:T(8,128)(2,1)S(1)} %get-tuple-element.18.refs_0_.refs_1_), channel_id=1, source_target_pairs={{0,6},{1,3},{2,0},{3,5},{4,2},{5,7},{6,4},{7,1},{8,14},{9,11},{10,... | collective-permute-start | bytes 626696 | tf_op jit(solution)/shard_map/ppermute | solution.py:386
  12.8 0.9 %copy-start.2 = (bf16[9,641,16]{1,2,0:T(8,128)(2,1)S(1)}, bf16[9,641,16]{1,2,0:T(8,128)(2,1)}, u32[]{:S(2)}) copy-start(bf16[9,641,16]{1,2,0:T(8,128)(2,1)} %param.8) | copy-start | bytes 553828
  13.9 6.9 %collective-permute-start.5 = (bf16[16,2944]{1,0:T(8,128)(2,1)S(1)}, bf16[16,2944]{1,0:T(8,128)(2,1)S(1)}, u32[]{:S(2)}, u32[]{:S(2)}) collective-permute-start(bf16[16,2944]{1,0:T(8,128)(2,1)S(1)} %get-tuple-element.22), channel_id=1, source_target_pairs={{0,1},{1,0},{2,3},{3,2},{4,5},{5,4},{6,7},{7,6},{8,9},{9,8},{10,11... | collective-permute-start | bytes 282632 | tf_op jit(solution)/shard_map/ppermute | solution.py:49
  14.0 9.7 %collective-permute-start.1 = (bf16[16,6528]{1,0:T(8,128)(2,1)S(1)}, bf16[16,6528]{1,0:T(8,128)(2,1)S(1)}, u32[]{:S(2)}, u32[]{:S(2)}) collective-permute-start(bf16[16,6528]{1,0:T(8,128)(2,1)S(1)} %get-tuple-element.17), channel_id=1, source_target_pairs={{0,1},{1,0},{2,3},{3,2},{4,5},{5,4},{6,7},{7,6},{8,9},{9,8},{10,11... | collective-permute-start | bytes 626696 | tf_op jit(solution)/shard_map/ppermute | solution.py:49
  16.0 10.6 %collective-permute-start.3 = (bf16[16,6528]{1,0:T(8,128)(2,1)S(1)}, bf16[16,6528]{1,0:T(8,128)(2,1)S(1)}, u32[]{:S(2)}, u32[]{:S(2)}) collective-permute-start(bf16[16,6528]{1,0:T(8,128)(2,1)S(1)} %get-tuple-element.17), channel_id=1, source_target_pairs={{0,7},{1,2},{2,1},{3,4},{4,3},{5,6},{6,5},{7,0},{8,15},{9,10},{10,... | collective-permute-start | bytes 626696 | tf_op jit(solution)/shard_map/ppermute | solution.py:387
  20.8 8.4 %collective-permute-start.6 = (bf16[32,2944]{1,0:T(8,128)(2,1)S(1)}, bf16[32,2944]{1,0:T(8,128)(2,1)S(1)}, u32[]{:S(2)}, u32[]{:S(2)}) collective-permute-start(bf16[32,2944]{1,0:T(8,128)(2,1)S(1)} %shard_map.61.refs_0_.refs_1_), channel_id=1, source_target_pairs={{0,4},{1,5},{2,6},{3,7},{4,0},{5,1},{6,2},{7,3},{8,12},{9,13},{10,... | collective-permute-start | bytes 565256 | tf_op jit(solution)/shard_map/ppermute | solution.py:49
  21.2 9.0 %collective-permute-start.7 = (bf16[32,2944]{1,0:T(8,128)(2,1)S(1)}, bf16[32,2944]{1,0:T(8,128)(2,1)S(1)}, u32[]{:S(2)}, u32[]{:S(2)}) collective-permute-start(bf16[32,2944]{1,0:T(8,128)(2,1)S(1)} %shard_map.61.refs_0_.refs_1_), channel_id=1, source_target_pairs={{0,2},{1,3},{2,0},{3,1},{4,6},{5,7},{6,4},{7,5},{8,10},{9,11},{10,... | collective-permute-start | bytes 565256 | tf_op jit(solution)/shard_map/ppermute | solution.py:49
  21.4 11.2 %collective-permute-start.8 = (bf16[32,2944]{1,0:T(8,128)(2,1)S(1)}, bf16[32,2944]{1,0:T(8,128)(2,1)S(1)}, u32[]{:S(2)}, u32[]{:S(2)}) collective-permute-start(bf16[32,2944]{1,0:T(8,128)(2,1)S(1)} %shard_map.61.refs_0_.refs_1_), channel_id=1, source_target_pairs={{0,16},{1,17},{2,18},{3,19},{4,20},{5,21},{6,22},{7,23},{8,24},{9,... | collective-permute-start | bytes 565256 | tf_op jit(solution)/shard_map/ppermute | solution.py:49
  26.8 7.3 %collective-permute-start.4 = (bf16[4,4,16,384]{3,2,1,0:T(8,128)(2,1)S(1)}, bf16[4,4,16,384]{3,2,1,0:T(8,128)(2,1)S(1)}, u32[]{:S(2)}, u32[]{:S(2)}) collective-permute-start(bf16[4,4,16,384]{3,2,1,0:T(8,128)(2,1)S(1)} %get-tuple-element.20), channel_id=1, source_target_pairs={{0,8},{1,9},{2,10},{3,11},{4,12},{5,13},{6,14},{7,15},{8,0},{9,1},... | collective-permute-start | bytes 589832 | tf_op jit(solution)/shard_map/ppermute | solution.py:49
  29.2 8.8 %collective-permute-start.11 = (bf16[32,2944]{1,0:T(8,128)(2,1)S(1)}, bf16[32,2944]{1,0:T(8,128)(2,1)S(1)}, u32[]{:S(2)}, u32[]{:S(2)}) collective-permute-start(bf16[32,2944]{1,0:T(8,128)(2,1)S(1)} %shard_map.62.refs_1_.refs_2_), channel_id=1, source_target_pairs={{0,16},{1,17},{2,18},{3,19},{4,20},{5,21},{6,22},{7,23},{8,24},{9,... | collective-permute-start | bytes 565256 | tf_op jit(solution)/shard_map/ppermute | solution.py:49
  30.2 7.9 %collective-permute-start.12 = (bf16[32,2944]{1,0:T(8,128)(2,1)S(1)}, bf16[32,2944]{1,0:T(8,128)(2,1)S(1)}, u32[]{:S(2)}, u32[]{:S(2)}) collective-permute-start(bf16[32,2944]{1,0:T(8,128)(2,1)S(1)} %shard_map.63.refs_2_.refs_3_), channel_id=1, source_target_pairs={{0,16},{1,17},{2,18},{3,19},{4,20},{5,21},{6,22},{7,23},{8,24},{9,... | collective-permute-start | bytes 565256 | tf_op jit(solution)/shard_map/ppermute | solution.py:49
  31.4 6.7 %collective-permute-start.10 = (bf16[32,2944]{1,0:T(8,128)(2,1)S(1)}, bf16[32,2944]{1,0:T(8,128)(2,1)S(1)}, u32[]{:S(2)}, u32[]{:S(2)}) collective-permute-start(bf16[32,2944]{1,0:T(8,128)(2,1)S(1)} %collective-permute-done.6.refs_0_), channel_id=1, source_target_pairs={{0,2},{1,3},{2,0},{3,1},{4,6},{5,7},{6,4},{7,5},{8,10},{9,11},{10,... | collective-permute-start | bytes 565256 | tf_op jit(solution)/shard_map/ppermute | solution.py:49
  32.6 7.2 %collective-permute-start.9 = (bf16[4,32,2944]{2,1,0:T(8,128)(2,1)S(1)}, bf16[4,32,2944]{2,1,0:T(8,128)(2,1)S(1)}, u32[]{:S(2)}, u32[]{:S(2)}) collective-permute-start(bf16[4,32,2944]{2,1,0:T(8,128)(2,1)S(1)} %shard_map.64.refs_1_), channel_id=1, source_target_pairs={{0,8},{1,9},{2,10},{3,11},{4,12},{5,13},{6,14},{7,15},{8,0},{9,1},... | collective-permute-start | bytes 2261000 | tf_op jit(solution)/shard_map/ppermute | solution.py:49
  38.2 2.1 %collective-permute-start.13 = (bf16[3,32,2944]{2,1,0:T(8,128)(2,1)S(1)}, bf16[3,32,2944]{2,1,0:T(8,128)(2,1)S(1)}, u32[]{:S(2)}, u32[]{:S(2)}) collective-permute-start(bf16[3,32,2944]{2,1,0:T(8,128)(2,1)S(1)} %shard_map.66.refs_3_), channel_id=1, source_target_pairs={{0,8},{1,9},{2,10},{3,11},{4,12},{5,13},{6,14},{7,15},{8,0},{9,1},... | collective-permute-start | bytes 1695752 | tf_op jit(solution)/shard_map/ppermute | solution.py:49
  38.7 7.8 %collective-permute-start.14 = (bf16[32,2944]{1,0:T(8,128)(2,1)S(1)}, bf16[32,2944]{1,0:T(8,128)(2,1)S(1)}, u32[]{:S(2)}, u32[]{:S(2)}) collective-permute-start(bf16[32,2944]{1,0:T(8,128)(2,1)S(1)} %shard_map.65.refs_0_), channel_id=1, source_target_pairs={{0,16},{1,17},{2,18},{3,19},{4,20},{5,21},{6,22},{7,23},{8,24},{9,... | collective-permute-start | bytes 565256 | tf_op jit(solution)/shard_map/ppermute | solution.py:49
  41.7 12.6 %collective-permute-start.16 = (bf16[256,512]{1,0:T(8,128)(2,1)S(1)}, bf16[256,512]{1,0:T(8,128)(2,1)S(1)}, u32[]{:S(2)}, u32[]{:S(2)}) collective-permute-start(bf16[256,512]{1,0:T(8,128)(2,1)S(1)} %get-tuple-element.24.refs_1_), channel_id=1, source_target_pairs={{0,1},{1,0},{2,3},{3,2},{4,5},{5,4},{6,7},{7,6},{8,9},{9,8},{10,11... | collective-permute-start | bytes 786440 | tf_op jit(solution)/shard_map/ppermute | solution.py:49
  46.5 1.5 %collective-permute-start.15 = (bf16[1,32,2944]{2,1,0:T(8,128)(2,1)S(1)}, bf16[1,32,2944]{2,1,0:T(8,128)(2,1)S(1)}, u32[]{:S(2)}, u32[]{:S(2)}) collective-permute-start(bf16[1,32,2944]{2,1,0:T(8,128)(2,1)S(1)} %shard_map.68.refs_1_), channel_id=1, source_target_pairs={{0,8},{1,9},{2,10},{3,11},{4,12},{5,13},{6,14},{7,15},{8,0},{9,1},... | collective-permute-start | bytes 565256 | tf_op jit(solution)/shard_map/ppermute | solution.py:49
  48.6 5.7 %collective-permute-start.17 = (bf16[128,128]{1,0:T(8,128)(2,1)S(1)}, bf16[128,128]{1,0:T(8,128)(2,1)S(1)}, u32[]{:S(2)}, u32[]{:S(2)}) collective-permute-start(bf16[128,128]{1,0:T(8,128)(2,1)S(1)} %shard_map.69.refs_2_.refs_3_), channel_id=1, source_target_pairs={{0,1},{1,0},{2,3},{3,2},{4,5},{5,4},{6,7},{7,6},{8,9},{9,8},{10,11... | collective-permute-start | bytes 98312 | tf_op jit(solution)/shard_map/ppermute | solution.py:49
  53.3 0.9 %copy-start.4 = (f32[512]{0:T(512)S(1)}, f32[512]{0:T(512)}, u32[]{:S(2)}) copy-start(f32[512]{0:T(512)} %param.9) | copy-start | bytes 6148

commit v7 on v5

--- a/solution.py
+++ b/solution.py
@@ -301,31 +301,40 @@
     sum_ref[...] = jnp.concatenate([total[:count], total[count:]], axis=1).astype(sum_ref.dtype)
 
 
-def finish_kernel(last, block, keep_ref, got_ref, keep2_ref, got2_ref, bias_ref, out_ref):
+def grown(total):
+    return 0.5 * total * (1.0 + lax.erf(total * 0.5**0.5))
+
+
+def main_kernel(keep_ref, got_ref, bias_ref, out_ref):
+    total = keep_ref[...] + got_ref[...].astype(jnp.float32) + bias_ref[...]
+    out_ref[...] = grown(total).astype(out_ref.dtype)
+
+
+def finish_kernel(last, block, main_ref, keep_ref, got_ref, bias_ref, out_ref):
     lat, lon = lax.axis_index("lat"), lax.axis_index("lon")
-    wide = out_ref.shape[1] // 2
-
-    def save(rows, at, total):
-        total += bias_ref[:, at]
-        grown = 0.5 * total * (1.0 + lax.erf(total * 0.5**0.5))
-        out_ref[rows, at] = grown.astype(out_ref.dtype)
-
-    at = pl.ds(pl.multiple_of(lat // 2 * wide, LANES), wide)
-    save(slice(None), at, keep_ref[:, at] + got_ref[:, at].astype(jnp.float32))
-    rest = keep2_ref[...] + got2_ref[...].astype(jnp.float32)
+    out_ref[...] = main_ref[...]
+    rest = keep_ref[...] + got_ref[...].astype(jnp.float32)
     count = rest.shape[0]
     lane = lane_of(rest)
     start = ((lon // 2) ^ last) * block
     inside = (lane >= start) & (lane < start + block)
+    spots = []
     for crossed in range(2):
         tile = (1 - lat // 2) * 2 + (lat % 2 ^ crossed)
         at = pl.ds(pl.multiple_of(tile * LANES, LANES), LANES)
-        for part in range(2):
-            rows = slice(part * count, (part + 1) * count)
-            held = part * (2 * block) + crossed * block
-            moved = pltpu.roll(rest, lax.rem(start - held + LANES, LANES), 1)
-            total = keep_ref[rows, at] + got_ref[rows, at].astype(jnp.float32)
-            save(rows, at, jnp.where(inside, moved, total))
+        spots += [(at, part, part * (2 * block) + crossed * block) for part in range(2)]
+    bias = jnp.zeros((8, LANES), jnp.float32)
+    narrow = lane_of(bias)
+    for at, _, held in spots:
+        moved = jnp.broadcast_to(bias_ref[:, at], bias.shape)
+        moved = pltpu.roll(moved, lax.rem(held - start + LANES, LANES), 1)
+        bias = jnp.where((narrow >= held) & (narrow < held + block), moved, bias)
+    value = grown(rest + bias[:1])
+    for at, part, held in spots:
+        rows = slice(part * count, (part + 1) * count)
+        moved = pltpu.roll(value, lax.rem(start - held + LANES, LANES), 1)
+        merged = jnp.where(inside, moved, main_ref[rows, at].astype(jnp.float32))
+        out_ref[rows, at] = merged.astype(out_ref.dtype)
 
 
 def body(latent, filters, widths, mix_weight, mix_bias):
@@ -464,12 +473,14 @@
         *pieces,
         after=(rest_send,),
     )
+    done = call(
+        main_kernel, shape((points, out_columns)), [], keep, got, mix_bias[None]
+    )
     out = call(
         functools.partial(finish_kernel, last, 2 * share),
         shape((points, out_columns)),
         [],
-        keep,
-        got,
+        done,
         rest_keep,
         rest_got,
         mix_bias[None],

time: 54.7 us -> 54.6 us (level)
    pallas_call x18 -> x19, Pallas kernels: 10.5 us -> 10.7 us  [call(): pl.pallas_call(ordered, out_shape=outs, in_specs=[held] * count + [pl.Blo...]
  transfers between devices with their start and end apart: 18 -> 18, of which waited for: 9 -> 10; matrix products, arithmetic and copies ran while one was open for 0% -> 0% of each run, Pallas kernels for 17% -> 18%
where the time goes in v7:
time: 54.6 us; the launch traced here: 54.5 us
  starting transfers between devices  25.9 us (47%)
  waiting for transfers between devices  15.7 us (29%)
  Pallas kernels  10.7 us (20%)
  local copies, waits for them, and re-layouts  1.94 us (4%)
    ppermute x15, starting transfers between devices, swap(): lax.ppermute(block, AXES, route(lambda lat, lon, lats, lons: (lat ^ lat_b...  15.3 us
    pallas_call x19, Pallas kernels, call(): pl.pallas_call(ordered, out_shape=outs, in_specs=[held] * count + [pl.Blo...  10.7 us
    ppermute x15, waiting for transfers between devices, swap(): lax.ppermute(block, AXES, route(lambda lat, lon, lats, lons: (lat ^ lat_b...  10.4 us
    ppermute x1, starting transfers between devices, body(): across = lax.ppermute(other, AXES, route(across_move))  5.87 us
    ppermute x1, starting transfers between devices, body(): from_outer = lax.ppermute(outer, AXES, route(outer_move))  4.1 us
    ppermute x1, waiting for transfers between devices, body(): along = lax.ppermute(mine, AXES, route(along_move))  2.88 us
    ppermute x1, waiting for transfers between devices, body(): across = lax.ppermute(other, AXES, route(across_move))  2.47 us
    unnamed x10, local copies, waits for them, and re-layouts  1.94 us
  transfers between devices with their start and end apart: 18, of which 10 were waited for; matrix products, arithmetic and copies ran while one was open for 0% of the time, Pallas kernels for 18%

profile of v7, /device:TPU:0, one launch (start us, length us, event | category | flops | bytes accessed | tf_op | source)
XLA Modules:
  0.0 54.5 jit_solution(12944579000998643413)
XLA Ops:
  0.0 1.0 %copy-done = bf16[16,16,641]{2,1,0:T(8,128)(2,1)S(1)} copy-done((bf16[16,16,641]{2,1,0:T(8,128)(2,1)S(1)}, bf16[16,16,641]{2,1,0:T(8,128)(2,1)}, u32[]{:S(2)}) %copy-start) | copy-done | bytes 328216
  1.0 4.1 %collective-permute-start = (bf16[4,16,641]{2,1,0:T(8,128)(2,1)S(1)}, bf16[4,16,641]{2,1,0:T(8,128)(2,1)S(1)}, u32[]{:S(2)}, u32[]{:S(2)}) collective-permute-start(bf16[4,16,641]{2,1,0:T(8,128)(2,1)S(1)} %get-tuple-element.16), channel_id=1, source_target_pairs={{0,4},{1,5},{2,6},{3,7},{4,0},{5,1},{6,2},{7,3},{8,16},{9,17},{10,... | collective-permute-start | bytes 246152 | tf_op jit(solution)/shard_map/ppermute | solution.py:360
  5.1 0.9 %copy-done.2 = bf16[9,641,16]{1,2,0:T(8,128)(2,1)S(1)} copy-done((bf16[9,641,16]{1,2,0:T(8,128)(2,1)S(1)}, bf16[9,641,16]{1,2,0:T(8,128)(2,1)}, u32[]{:S(2)}) %copy-start.2) | copy-done | bytes 184632
  6.2 1.6 %collective-permute-start.5 = (bf16[16,2944]{1,0:T(8,128)(2,1)S(1)}, bf16[16,2944]{1,0:T(8,128)(2,1)S(1)}, u32[]{:S(2)}, u32[]{:S(2)}) collective-permute-start(bf16[16,2944]{1,0:T(8,128)(2,1)S(1)} %get-tuple-element.22), channel_id=1, source_target_pairs={{0,1},{1,0},{2,3},{3,2},{4,5},{5,4},{6,7},{7,6},{8,9},{9,8},{10,11... | collective-permute-start | bytes 282632 | tf_op jit(solution)/shard_map/ppermute | solution.py:49
  7.9 5.9 %collective-permute-start.3 = (bf16[16,6528]{1,0:T(8,128)(2,1)S(1)}, bf16[16,6528]{1,0:T(8,128)(2,1)S(1)}, u32[]{:S(2)}, u32[]{:S(2)}) collective-permute-start(bf16[16,6528]{1,0:T(8,128)(2,1)S(1)} %get-tuple-element.17), channel_id=1, source_target_pairs={{0,7},{1,2},{2,1},{3,4},{4,3},{5,6},{6,5},{7,0},{8,15},{9,10},{10,... | collective-permute-start | bytes 626696 | tf_op jit(solution)/shard_map/ppermute | solution.py:396
  13.8 0.6 %collective-permute-start.2 = (bf16[16,6528]{1,0:T(8,128)(2,1)S(1)}, bf16[16,6528]{1,0:T(8,128)(2,1)S(1)}, u32[]{:S(2)}, u32[]{:S(2)}) collective-permute-start(bf16[16,6528]{1,0:T(8,128)(2,1)S(1)} %get-tuple-element.18.refs_0_.refs_1_), channel_id=1, source_target_pairs={{0,6},{1,3},{2,0},{3,5},{4,2},{5,7},{6,4},{7,1},{8,14},{9,11},{10,... | collective-permute-start | bytes 626696 | tf_op jit(solution)/shard_map/ppermute | solution.py:395
  14.5 0.5 collective-permute-start.6
  15.0 2.0 %collective-permute-start.7 = (bf16[32,2944]{1,0:T(8,128)(2,1)S(1)}, bf16[32,2944]{1,0:T(8,128)(2,1)S(1)}, u32[]{:S(2)}, u32[]{:S(2)}) collective-permute-start(bf16[32,2944]{1,0:T(8,128)(2,1)S(1)} %shard_map.61.refs_1_.refs_0_), channel_id=1, source_target_pairs={{0,2},{1,3},{2,0},{3,1},{4,6},{5,7},{6,4},{7,5},{8,10},{9,11},{10,... | collective-permute-start | bytes 565256 | tf_op jit(solution)/shard_map/ppermute | solution.py:49
  17.0 2.5 %collective-permute-done.3.refs_3_ = bf16[16,6528]{1,0:T(8,128)(2,1)S(1)} collective-permute-done((bf16[16,6528]{1,0:T(8,128)(2,1)S(1)}, bf16[16,6528]{1,0:T(8,128)(2,1)S(1)}, u32[]{:S(2)}, u32[]{:S(2)}) %collective-permute-start.3) | collective-permute-done | bytes 208928 | tf_op jit(solution)/shard_map/ppermute | solution.py:396
  19.5 1.6 %collective-permute-done.1.refs_2_.refs_1_ = bf16[16,6528]{1,0:T(8,128)(2,1)S(1)} collective-permute-done((bf16[16,6528]{1,0:T(8,128)(2,1)S(1)}, bf16[16,6528]{1,0:T(8,128)(2,1)S(1)}, u32[]{:S(2)}, u32[]{:S(2)}) %collective-permute-start.1) | collective-permute-done | bytes 208928 | tf_op jit(solution)/shard_map/ppermute | solution.py:49
  21.1 2.9 %collective-permute-done.2.refs_2_ = bf16[16,6528]{1,0:T(8,128)(2,1)S(1)} collective-permute-done((bf16[16,6528]{1,0:T(8,128)(2,1)S(1)}, bf16[16,6528]{1,0:T(8,128)(2,1)S(1)}, u32[]{:S(2)}, u32[]{:S(2)}) %collective-permute-start.2) | collective-permute-done | bytes 208928 | tf_op jit(solution)/shard_map/ppermute | solution.py:395
  24.0 0.2 shard_map.58
  24.4 4.0 %collective-permute-done.6.refs_0_ = bf16[32,2944]{1,0:T(8,128)(2,1)S(1)} collective-permute-done((bf16[32,2944]{1,0:T(8,128)(2,1)S(1)}, bf16[32,2944]{1,0:T(8,128)(2,1)S(1)}, u32[]{:S(2)}, u32[]{:S(2)}) %collective-permute-start.6) | collective-permute-done | bytes 188448 | tf_op jit(solution)/shard_map/ppermute | solution.py:49
  28.4 2.3 %collective-permute-start.10 = (bf16[32,2944]{1,0:T(8,128)(2,1)S(1)}, bf16[32,2944]{1,0:T(8,128)(2,1)S(1)}, u32[]{:S(2)}, u32[]{:S(2)}) collective-permute-start(bf16[32,2944]{1,0:T(8,128)(2,1)S(1)} %shard_map.62.refs_2_.refs_1_), channel_id=1, source_target_pairs={{0,16},{1,17},{2,18},{3,19},{4,20},{5,21},{6,22},{7,23},{8,24},{9,... | collective-permute-start | bytes 565256 | tf_op jit(solution)/shard_map/ppermute | solution.py:49
  30.7 2.0 %collective-permute-start.8 = (bf16[32,2944]{1,0:T(8,128)(2,1)S(1)}, bf16[32,2944]{1,0:T(8,128)(2,1)S(1)}, u32[]{:S(2)}, u32[]{:S(2)}) collective-permute-start(bf16[32,2944]{1,0:T(8,128)(2,1)S(1)} %collective-permute-done.6.refs_0_), channel_id=1, source_target_pairs={{0,2},{1,3},{2,0},{3,1},{4,6},{5,7},{6,4},{7,5},{8,10},{9,11},{10,... | collective-permute-start | bytes 565256 | tf_op jit(solution)/shard_map/ppermute | solution.py:49
  32.8 1.4 %shard_map.57.refs_0_ = bf16[8,288,512]{2,1,0:T(8,128)(2,1)S(1)} custom-call(bf16[9,9,16,33]{3,2,1,0:T(8,128)(2,1)S(1)} %bitcast.10, s32[16,9]{1,0:T(8,128)S(1)} %copy-done.3, bf16[16,6528]{1,0:T(8,128)(2,1)S(1)} %collective-permute-done.1.refs_2_.refs_1_), custom_call_target="tpu_custom_call" | custom-call | tf_op jit(solution)/shard_map/pallas_call | solution.py:24
  34.2 3.9 %shard_map.59 = bf16[2,16,16,2944]{3,2,1,0:T(8,128)(2,1)S(1)} custom-call(bf16[8,288,512]{2,1,0:T(8,128)(2,1)S(1)} %shard_map.57.refs_0_, bf16[20,4,16,384]{3,2,1,0:T(8,128)(2,1)S(1)} %get-tuple-element.19.refs_1_, bf16[4,4,16,384]{3,2,1,0:T(8,128)(2,1)S(1)} %collective-permute-done.4.refs_2_), custom_call_target="tpu_custom_call" | custom-call | tf_op jit(solution)/shard_map/pallas_call | solution.py:24
  38.1 1.4 %collective-permute-done.11.refs_6_.refs_2_ = bf16[32,2944]{1,0:T(8,128)(2,1)S(1)} collective-permute-done((bf16[32,2944]{1,0:T(8,128)(2,1)S(1)}, bf16[32,2944]{1,0:T(8,128)(2,1)S(1)}, u32[]{:S(2)}, u32[]{:S(2)}) %collective-permute-start.11) | collective-permute-done | bytes 188448 | tf_op jit(solution)/shard_map/ppermute | solution.py:49
  39.7 0.6 %collective-permute-start.13 = (bf16[3,32,2944]{2,1,0:T(8,128)(2,1)S(1)}, bf16[3,32,2944]{2,1,0:T(8,128)(2,1)S(1)}, u32[]{:S(2)}, u32[]{:S(2)}) collective-permute-start(bf16[3,32,2944]{2,1,0:T(8,128)(2,1)S(1)} %shard_map.66.refs_3_), channel_id=1, source_target_pairs={{0,8},{1,9},{2,10},{3,11},{4,12},{5,13},{6,14},{7,15},{8,0},{9,1},... | collective-permute-start | bytes 1695752 | tf_op jit(solution)/shard_map/ppermute | solution.py:49
  40.3 1.7 %collective-permute-start.14 = (bf16[32,2944]{1,0:T(8,128)(2,1)S(1)}, bf16[32,2944]{1,0:T(8,128)(2,1)S(1)}, u32[]{:S(2)}, u32[]{:S(2)}) collective-permute-start(bf16[32,2944]{1,0:T(8,128)(2,1)S(1)} %shard_map.64.refs_3_.refs_4_), channel_id=1, source_target_pairs={{0,16},{1,17},{2,18},{3,19},{4,20},{5,21},{6,22},{7,23},{8,24},{9,... | collective-permute-start | bytes 565256 | tf_op jit(solution)/shard_map/ppermute | solution.py:49
  41.9 0.8 %collective-permute-done.13.refs_4_ = bf16[3,32,2944]{2,1,0:T(8,128)(2,1)S(1)} collective-permute-done((bf16[3,32,2944]{2,1,0:T(8,128)(2,1)S(1)}, bf16[3,32,2944]{2,1,0:T(8,128)(2,1)S(1)}, u32[]{:S(2)}, u32[]{:S(2)}) %collective-permute-start.13) | collective-permute-done | bytes 565280 | tf_op jit(solution)/shard_map/ppermute | solution.py:49
  42.7 1.4 %shard_map.67 = (bf16[256,512]{1,0:T(8,128)(2,1)S(1)}, bf16[16,32,2944]{2,1,0:T(8,128)(2,1)S(1)}) custom-call(bf16[2,256,2944]{2,1,0:T(8,128)(2,1)S(1)} %bitcast.6, bf16[4,32,2944]{2,1,0:T(8,128)(2,1)S(1)} %shard_map.65.refs_1_, bf16[4,32,2944]{2,1,0:T(8,128)(2,1)S(1)} %collective-permute-done.12.refs_2_, bf16[3,32,2944]{2,1,0:T(8,128)(2,1)S(1)} %shard_map.66.refs_3_, ...), custom_call_target="tpu_custom_call" | custom-call | tf_op jit(solution)/shard_map/pallas_call | solution.py:24
  44.1 2.1 %collective-permute-start.16 = (bf16[256,512]{1,0:T(8,128)(2,1)S(1)}, bf16[256,512]{1,0:T(8,128)(2,1)S(1)}, u32[]{:S(2)}, u32[]{:S(2)}) collective-permute-start(bf16[256,512]{1,0:T(8,128)(2,1)S(1)} %get-tuple-element.24.refs_1_), channel_id=1, source_target_pairs={{0,1},{1,0},{2,3},{3,2},{4,5},{5,4},{6,7},{7,6},{8,9},{9,8},{10,11... | collective-permute-start | bytes 786440 | tf_op jit(solution)/shard_map/ppermute | solution.py:49
  46.2 0.7 %collective-permute-done.14.refs_0_ = bf16[32,2944]{1,0:T(8,128)(2,1)S(1)} collective-permute-done((bf16[32,2944]{1,0:T(8,128)(2,1)S(1)}, bf16[32,2944]{1,0:T(8,128)(2,1)S(1)}, u32[]{:S(2)}, u32[]{:S(2)}) %collective-permute-start.14) | collective-permute-done | bytes 188448 | tf_op jit(solution)/shard_map/ppermute | solution.py:49
  47.1 1.4 %collective-permute-done.15.refs_2_ = bf16[1,32,2944]{2,1,0:T(8,128)(2,1)S(1)} collective-permute-done((bf16[1,32,2944]{2,1,0:T(8,128)(2,1)S(1)}, bf16[1,32,2944]{2,1,0:T(8,128)(2,1)S(1)}, u32[]{:S(2)}, u32[]{:S(2)}) %collective-permute-start.15) | collective-permute-done | bytes 188448 | tf_op jit(solution)/shard_map/ppermute | solution.py:49
  48.5 0.6 %shard_map.69.refs_2_.refs_3_ = bf16[128,128]{1,0:T(8,128)(2,1)S(1)} custom-call(bf16[2,256,2944]{2,1,0:T(8,128)(2,1)S(1)} %bitcast.7, bf16[1,32,2944]{2,1,0:T(8,128)(2,1)S(1)} %shard_map.68.refs_1_, bf16[1,32,2944]{2,1,0:T(8,128)(2,1)S(1)} %collective-permute-done.15.refs_2_), custom_call_target="tpu_custom_call" | custom-call | tf_op jit(solution)/shard_map/pallas_call | solution.py:24
  49.1 2.1 %collective-permute-start.17 = (bf16[128,128]{1,0:T(8,128)(2,1)S(1)}, bf16[128,128]{1,0:T(8,128)(2,1)S(1)}, u32[]{:S(2)}, u32[]{:S(2)}) collective-permute-start(bf16[128,128]{1,0:T(8,128)(2,1)S(1)} %shard_map.69.refs_2_.refs_3_), channel_id=1, source_target_pairs={{0,1},{1,0},{2,3},{3,2},{4,5},{5,4},{6,7},{7,6},{8,9},{9,8},{10,11... | collective-permute-start | bytes 98312 | tf_op jit(solution)/shard_map/ppermute | solution.py:49
  51.2 1.0 %shard_map.70.refs_0_ = f32[256,512]{1,0:T(8,128)S(1)} custom-call(bf16[2,256,2944]{2,1,0:T(8,128)(2,1)S(1)} %bitcast.8, bf16[16,32,2944]{2,1,0:T(8,128)(2,1)S(1)} %get-tuple-element.23.refs_1_, bf16[128,128]{1,0:T(8,128)(2,1)S(1)} %shard_map.69.refs_2_.refs_3_), custom_call_target="tpu_custom_call" | custom-call | tf_op jit(solution)/shard_map/pallas_call | solution.py:24
  52.2 0.6 %shard_map.72.refs_1_ = f32[128,128]{1,0:T(8,128)S(1)} custom-call(bf16[2,256,2944]{2,1,0:T(8,128)(2,1)S(1)} %bitcast.9, bf16[1,32,2944]{2,1,0:T(8,128)(2,1)S(1)} %shard_map.68.refs_1_, bf16[1,32,2944]{2,1,0:T(8,128)(2,1)S(1)} %collective-permute-done.15.refs_2_, bf16[128,128]{1,0:T(8,128)(2,1)S(1)} %shard_map.69.refs_2_.refs_3_), custom_call_target="tpu_custom_call" | custom-call | tf_op jit(solution)/shard_map/pallas_call | solution.py:24
  52.9 0.3 collective-permute-done.16.refs_1_
  53.4 0.2 collective-permute-done.17.refs_2_
  53.5 0.9 %shard_map.73 = bf16[256,512]{1,0:T(8,128)(2,1)} custom-call(bf16[256,512]{1,0:T(8,128)(2,1)S(1)} %shard_map.71.refs_0_, f32[128,128]{1,0:T(8,128)S(1)} %shard_map.72.refs_1_, bf16[128,128]{1,0:T(8,128)(2,1)S(1)} %collective-permute-done.17.refs_2_, f32[1,512]{1,0:T(1,128)S(1)} %bitcast.13), custom_call_target="tpu_custom_call" | custom-call | tf_op jit(solution)/shard_map/pallas_call | solution.py:24
  (33 shorter events, 1.1 us)
Async XLA Ops:
  0.0 1.0 %copy-start = (bf16[16,16,641]{2,1,0:T(8,128)(2,1)S(1)}, bf16[16,16,641]{2,1,0:T(8,128)(2,1)}, u32[]{:S(2)}) copy-start(bf16[16,16,641]{2,1,0:T(8,128)(2,1)} %refs_0_.1) | copy-start | bytes 984580
  1.0 31.8 %copy-start.1 = (bf16[9,16,9,33]{3,1,2,0:T(8,128)(2,1)S(1)}, bf16[9,16,9,33]{3,1,2,0:T(8,128)(2,1)}, u32[]{:S(2)}) copy-start(bf16[9,16,9,33]{3,1,2,0:T(8,128)(2,1)} %param.6) | copy-start | bytes 256612
  1.0 31.8 %copy-start.3 = (s32[16,9]{1,0:T(8,128)S(1)}, s32[16,9]{1,0:T(8,128)}, u32[]{:S(2)}) copy-start(s32[16,9]{1,0:T(8,128)} %refs_1_.1) | copy-start | bytes 1732
  1.0 6.7 %collective-permute-start = (bf16[4,16,641]{2,1,0:T(8,128)(2,1)S(1)}, bf16[4,16,641]{2,1,0:T(8,128)(2,1)S(1)}, u32[]{:S(2)}, u32[]{:S(2)}) collective-permute-start(bf16[4,16,641]{2,1,0:T(8,128)(2,1)S(1)} %get-tuple-element.16), channel_id=1, source_target_pairs={{0,4},{1,5},{2,6},{3,7},{4,0},{5,1},{6,2},{7,3},{8,16},{9,17},{10,... | collective-permute-start | bytes 246152 | tf_op jit(solution)/shard_map/ppermute | solution.py:360
  5.1 0.9 %copy-start.2 = (bf16[9,641,16]{1,2,0:T(8,128)(2,1)S(1)}, bf16[9,641,16]{1,2,0:T(8,128)(2,1)}, u32[]{:S(2)}) copy-start(bf16[9,641,16]{1,2,0:T(8,128)(2,1)} %param.8) | copy-start | bytes 553828
  6.2 8.3 %collective-permute-start.5 = (bf16[16,2944]{1,0:T(8,128)(2,1)S(1)}, bf16[16,2944]{1,0:T(8,128)(2,1)S(1)}, u32[]{:S(2)}, u32[]{:S(2)}) collective-permute-start(bf16[16,2944]{1,0:T(8,128)(2,1)S(1)} %get-tuple-element.22), channel_id=1, source_target_pairs={{0,1},{1,0},{2,3},{3,2},{4,5},{5,4},{6,7},{7,6},{8,9},{9,8},{10,11... | collective-permute-start | bytes 282632 | tf_op jit(solution)/shard_map/ppermute | solution.py:49
  7.9 11.5 %collective-permute-start.3 = (bf16[16,6528]{1,0:T(8,128)(2,1)S(1)}, bf16[16,6528]{1,0:T(8,128)(2,1)S(1)}, u32[]{:S(2)}, u32[]{:S(2)}) collective-permute-start(bf16[16,6528]{1,0:T(8,128)(2,1)S(1)} %get-tuple-element.17), channel_id=1, source_target_pairs={{0,7},{1,2},{2,1},{3,4},{4,3},{5,6},{6,5},{7,0},{8,15},{9,10},{10,... | collective-permute-start | bytes 626696 | tf_op jit(solution)/shard_map/ppermute | solution.py:396
  13.8 7.3 %collective-permute-start.1 = (bf16[16,6528]{1,0:T(8,128)(2,1)S(1)}, bf16[16,6528]{1,0:T(8,128)(2,1)S(1)}, u32[]{:S(2)}, u32[]{:S(2)}) collective-permute-start(bf16[16,6528]{1,0:T(8,128)(2,1)S(1)} %get-tuple-element.17), channel_id=1, source_target_pairs={{0,1},{1,0},{2,3},{3,2},{4,5},{5,4},{6,7},{7,6},{8,9},{9,8},{10,11... | collective-permute-start | bytes 626696 | tf_op jit(solution)/shard_map/ppermute | solution.py:49
  13.8 10.1 %collective-permute-start.2 = (bf16[16,6528]{1,0:T(8,128)(2,1)S(1)}, bf16[16,6528]{1,0:T(8,128)(2,1)S(1)}, u32[]{:S(2)}, u32[]{:S(2)}) collective-permute-start(bf16[16,6528]{1,0:T(8,128)(2,1)S(1)} %get-tuple-element.18.refs_0_.refs_1_), channel_id=1, source_target_pairs={{0,6},{1,3},{2,0},{3,5},{4,2},{5,7},{6,4},{7,1},{8,14},{9,11},{10,... | collective-permute-start | bytes 626696 | tf_op jit(solution)/shard_map/ppermute | solution.py:395
  14.5 13.9 %collective-permute-start.6 = (bf16[32,2944]{1,0:T(8,128)(2,1)S(1)}, bf16[32,2944]{1,0:T(8,128)(2,1)S(1)}, u32[]{:S(2)}, u32[]{:S(2)}) collective-permute-start(bf16[32,2944]{1,0:T(8,128)(2,1)S(1)} %shard_map.61.refs_1_.refs_0_), channel_id=1, source_target_pairs={{0,4},{1,5},{2,6},{3,7},{4,0},{5,1},{6,2},{7,3},{8,12},{9,13},{10,... | collective-permute-start | bytes 565256 | tf_op jit(solution)/shard_map/ppermute | solution.py:49
  15.0 17.7 %collective-permute-start.7 = (bf16[32,2944]{1,0:T(8,128)(2,1)S(1)}, bf16[32,2944]{1,0:T(8,128)(2,1)S(1)}, u32[]{:S(2)}, u32[]{:S(2)}) collective-permute-start(bf16[32,2944]{1,0:T(8,128)(2,1)S(1)} %shard_map.61.refs_1_.refs_0_), channel_id=1, source_target_pairs={{0,2},{1,3},{2,0},{3,1},{4,6},{5,7},{6,4},{7,5},{8,10},{9,11},{10,... | collective-permute-start | bytes 565256 | tf_op jit(solution)/shard_map/ppermute | solution.py:49
  24.2 10.0 %collective-permute-start.4 = (bf16[4,4,16,384]{3,2,1,0:T(8,128)(2,1)S(1)}, bf16[4,4,16,384]{3,2,1,0:T(8,128)(2,1)S(1)}, u32[]{:S(2)}, u32[]{:S(2)}) collective-permute-start(bf16[4,4,16,384]{3,2,1,0:T(8,128)(2,1)S(1)} %get-tuple-element.20), channel_id=1, source_target_pairs={{0,8},{1,9},{2,10},{3,11},{4,12},{5,13},{6,14},{7,15},{8,0},{9,1},... | collective-permute-start | bytes 589832 | tf_op jit(solution)/shard_map/ppermute | solution.py:49
  24.3 13.8 %collective-permute-start.9 = (bf16[32,2944]{1,0:T(8,128)(2,1)S(1)}, bf16[32,2944]{1,0:T(8,128)(2,1)S(1)}, u32[]{:S(2)}, u32[]{:S(2)}) collective-permute-start(bf16[32,2944]{1,0:T(8,128)(2,1)S(1)} %shard_map.61.refs_1_.refs_0_), channel_id=1, source_target_pairs={{0,16},{1,17},{2,18},{3,19},{4,20},{5,21},{6,22},{7,23},{8,24},{9,... | collective-permute-start | bytes 565256 | tf_op jit(solution)/shard_map/ppermute | solution.py:49
  28.4 9.8 %collective-permute-start.10 = (bf16[32,2944]{1,0:T(8,128)(2,1)S(1)}, bf16[32,2944]{1,0:T(8,128)(2,1)S(1)}, u32[]{:S(2)}, u32[]{:S(2)}) collective-permute-start(bf16[32,2944]{1,0:T(8,128)(2,1)S(1)} %shard_map.62.refs_2_.refs_1_), channel_id=1, source_target_pairs={{0,16},{1,17},{2,18},{3,19},{4,20},{5,21},{6,22},{7,23},{8,24},{9,... | collective-permute-start | bytes 565256 | tf_op jit(solution)/shard_map/ppermute | solution.py:49
  30.7 7.5 %collective-permute-start.8 = (bf16[32,2944]{1,0:T(8,128)(2,1)S(1)}, bf16[32,2944]{1,0:T(8,128)(2,1)S(1)}, u32[]{:S(2)}, u32[]{:S(2)}) collective-permute-start(bf16[32,2944]{1,0:T(8,128)(2,1)S(1)} %collective-permute-done.6.refs_0_), channel_id=1, source_target_pairs={{0,2},{1,3},{2,0},{3,1},{4,6},{5,7},{6,4},{7,5},{8,10},{9,11},{10,... | collective-permute-start | bytes 565256 | tf_op jit(solution)/shard_map/ppermute | solution.py:49
  32.7 6.8 %collective-permute-start.11 = (bf16[32,2944]{1,0:T(8,128)(2,1)S(1)}, bf16[32,2944]{1,0:T(8,128)(2,1)S(1)}, u32[]{:S(2)}, u32[]{:S(2)}) collective-permute-start(bf16[32,2944]{1,0:T(8,128)(2,1)S(1)} %shard_map.63.refs_3_.refs_2_), channel_id=1, source_target_pairs={{0,16},{1,17},{2,18},{3,19},{4,20},{5,21},{6,22},{7,23},{8,24},{9,... | collective-permute-start | bytes 565256 | tf_op jit(solution)/shard_map/ppermute | solution.py:49
  39.6 3.1 %collective-permute-start.12 = (bf16[4,32,2944]{2,1,0:T(8,128)(2,1)S(1)}, bf16[4,32,2944]{2,1,0:T(8,128)(2,1)S(1)}, u32[]{:S(2)}, u32[]{:S(2)}) collective-permute-start(bf16[4,32,2944]{2,1,0:T(8,128)(2,1)S(1)} %shard_map.65.refs_1_), channel_id=1, source_target_pairs={{0,8},{1,9},{2,10},{3,11},{4,12},{5,13},{6,14},{7,15},{8,0},{9,1},... | collective-permute-start | bytes 2261000 | tf_op jit(solution)/shard_map/ppermute | solution.py:49
  39.7 3.0 %collective-permute-start.13 = (bf16[3,32,2944]{2,1,0:T(8,128)(2,1)S(1)}, bf16[3,32,2944]{2,1,0:T(8,128)(2,1)S(1)}, u32[]{:S(2)}, u32[]{:S(2)}) collective-permute-start(bf16[3,32,2944]{2,1,0:T(8,128)(2,1)S(1)} %shard_map.66.refs_3_), channel_id=1, source_target_pairs={{0,8},{1,9},{2,10},{3,11},{4,12},{5,13},{6,14},{7,15},{8,0},{9,1},... | collective-permute-start | bytes 1695752 | tf_op jit(solution)/shard_map/ppermute | solution.py:49
  40.3 6.7 %collective-permute-start.14 = (bf16[32,2944]{1,0:T(8,128)(2,1)S(1)}, bf16[32,2944]{1,0:T(8,128)(2,1)S(1)}, u32[]{:S(2)}, u32[]{:S(2)}) collective-permute-start(bf16[32,2944]{1,0:T(8,128)(2,1)S(1)} %shard_map.64.refs_3_.refs_4_), channel_id=1, source_target_pairs={{0,16},{1,17},{2,18},{3,19},{4,20},{5,21},{6,22},{7,23},{8,24},{9,... | collective-permute-start | bytes 565256 | tf_op jit(solution)/shard_map/ppermute | solution.py:49
  44.1 9.1 %collective-permute-start.16 = (bf16[256,512]{1,0:T(8,128)(2,1)S(1)}, bf16[256,512]{1,0:T(8,128)(2,1)S(1)}, u32[]{:S(2)}, u32[]{:S(2)}) collective-permute-start(bf16[256,512]{1,0:T(8,128)(2,1)S(1)} %get-tuple-element.24.refs_1_), channel_id=1, source_target_pairs={{0,1},{1,0},{2,3},{3,2},{4,5},{5,4},{6,7},{7,6},{8,9},{9,8},{10,11... | collective-permute-start | bytes 786440 | tf_op jit(solution)/shard_map/ppermute | solution.py:49
  47.0 1.5 %collective-permute-start.15 = (bf16[1,32,2944]{2,1,0:T(8,128)(2,1)S(1)}, bf16[1,32,2944]{2,1,0:T(8,128)(2,1)S(1)}, u32[]{:S(2)}, u32[]{:S(2)}) collective-permute-start(bf16[1,32,2944]{2,1,0:T(8,128)(2,1)S(1)} %shard_map.68.refs_1_), channel_id=1, source_target_pairs={{0,8},{1,9},{2,10},{3,11},{4,12},{5,13},{6,14},{7,15},{8,0},{9,1},... | collective-permute-start | bytes 565256 | tf_op jit(solution)/shard_map/ppermute | solution.py:49
  49.1 4.5 %collective-permute-start.17 = (bf16[128,128]{1,0:T(8,128)(2,1)S(1)}, bf16[128,128]{1,0:T(8,128)(2,1)S(1)}, u32[]{:S(2)}, u32[]{:S(2)}) collective-permute-start(bf16[128,128]{1,0:T(8,128)(2,1)S(1)} %shard_map.69.refs_2_.refs_3_), channel_id=1, source_target_pairs={{0,1},{1,0},{2,3},{3,2},{4,5},{5,4},{6,7},{7,6},{8,9},{9,8},{10,11... | collective-permute-start | bytes 98312 | tf_op jit(solution)/shard_map/ppermute | solution.py:49
  52.2 1.0 %copy-start.4 = (f32[512]{0:T(512)S(1)}, f32[512]{0:T(512)}, u32[]{:S(2)}) copy-start(f32[512]{0:T(512)} %param.9) | copy-start | bytes 6148

commit v8 on v7

--- a/solution.py
+++ b/solution.py
@@ -356,8 +356,8 @@
         functools.partial(weight_kernel, main), (halves, halves), [], weights
     )
     outer, held_latent = call(edge_kernel, (edge, shape(latent.shape)), [], latent)
+    from_outer = lax.ppermute(outer, AXES, route(outer_move))
     got_weight = swap(pair_weight, 0, 1)
-    from_outer = lax.ppermute(outer, AXES, route(outer_move))
     block = shape((2 * share, depth))
     first = call(join_kernel, block, [], own_weight, got_weight)
 
@@ -391,9 +391,9 @@
     for mask in order[1:-1]:
         blocks[0, mask] = call(copy_kernel, block, [], blocks[0, mask], after=(mine,))
     cross(order[1:-1])
+    across = lax.ppermute(other, AXES, route(across_move))
+    along = lax.ppermute(mine, AXES, route(along_move))
     pair_strip = swap(other, 0, 1)
-    along = lax.ppermute(mine, AXES, route(along_move))
-    across = lax.ppermute(other, AXES, route(across_move))
     deep = -(-(span + 1) * 3 * columns // LANES) * LANES
     band = call(
         functools.partial(band_kernel, reach),

time: 54.6 us -> 54.6 us (level)
  no operation moved by 1% of the time
where the time goes in v8:
time: 54.6 us; the launch traced here: 54.5 us
  starting transfers between devices  25.9 us (47%)
  waiting for transfers between devices  15.7 us (29%)
  Pallas kernels  10.7 us (20%)
  local copies, waits for them, and re-layouts  1.94 us (4%)
    ppermute x15, starting transfers between devices, swap(): lax.ppermute(block, AXES, route(lambda lat, lon, lats, lons: (lat ^ lat_b...  15.3 us
    pallas_call x19, Pallas kernels, call(): pl.pallas_call(ordered, out_shape=outs, in_specs=[held] * count + [pl.Blo...  10.7 us
    ppermute x15, waiting for transfers between devices, swap(): lax.ppermute(block, AXES, route(lambda lat, lon, lats, lons: (lat ^ lat_b...  10.4 us
    ppermute x1, starting transfers between devices, body(): across = lax.ppermute(other, AXES, route(across_move))  5.87 us
    ppermute x1, starting transfers between devices, body(): from_outer = lax.ppermute(outer, AXES, route(outer_move))  4.1 us
    ppermute x1, waiting for transfers between devices, body(): along = lax.ppermute(mine, AXES, route(along_move))  2.88 us
    ppermute x1, waiting for transfers between devices, body(): across = lax.ppermute(other, AXES, route(across_move))  2.47 us
    unnamed x10, local copies, waits for them, and re-layouts  1.94 us
  transfers between devices with their start and end apart: 18, of which 10 were waited for; matrix products, arithmetic and copies ran while one was open for 0% of the time, Pallas kernels for 18%

profile of v8, /device:TPU:0, one launch (start us, length us, event | category | flops | bytes accessed | tf_op | source)
XLA Modules:
  0.0 54.5 jit_solution(12944579000998643413)
XLA Ops:
  0.0 1.0 %copy-done = bf16[16,16,641]{2,1,0:T(8,128)(2,1)S(1)} copy-done((bf16[16,16,641]{2,1,0:T(8,128)(2,1)S(1)}, bf16[16,16,641]{2,1,0:T(8,128)(2,1)}, u32[]{:S(2)}) %copy-start) | copy-done | bytes 328216
  1.0 4.1 %collective-permute-start = (bf16[4,16,641]{2,1,0:T(8,128)(2,1)S(1)}, bf16[4,16,641]{2,1,0:T(8,128)(2,1)S(1)}, u32[]{:S(2)}, u32[]{:S(2)}) collective-permute-start(bf16[4,16,641]{2,1,0:T(8,128)(2,1)S(1)} %get-tuple-element.16), channel_id=1, source_target_pairs={{0,4},{1,5},{2,6},{3,7},{4,0},{5,1},{6,2},{7,3},{8,16},{9,17},{10,... | collective-permute-start | bytes 246152 | tf_op jit(solution)/shard_map/ppermute | solution.py:359
  5.1 0.9 %copy-done.2 = bf16[9,641,16]{1,2,0:T(8,128)(2,1)S(1)} copy-done((bf16[9,641,16]{1,2,0:T(8,128)(2,1)S(1)}, bf16[9,641,16]{1,2,0:T(8,128)(2,1)}, u32[]{:S(2)}) %copy-start.2) | copy-done | bytes 184632
  6.2 1.6 %collective-permute-start.5 = (bf16[16,2944]{1,0:T(8,128)(2,1)S(1)}, bf16[16,2944]{1,0:T(8,128)(2,1)S(1)}, u32[]{:S(2)}, u32[]{:S(2)}) collective-permute-start(bf16[16,2944]{1,0:T(8,128)(2,1)S(1)} %get-tuple-element.22), channel_id=1, source_target_pairs={{0,1},{1,0},{2,3},{3,2},{4,5},{5,4},{6,7},{7,6},{8,9},{9,8},{10,11... | collective-permute-start | bytes 282632 | tf_op jit(solution)/shard_map/ppermute | solution.py:49
  7.9 5.9 %collective-permute-start.3 = (bf16[16,6528]{1,0:T(8,128)(2,1)S(1)}, bf16[16,6528]{1,0:T(8,128)(2,1)S(1)}, u32[]{:S(2)}, u32[]{:S(2)}) collective-permute-start(bf16[16,6528]{1,0:T(8,128)(2,1)S(1)} %get-tuple-element.17), channel_id=1, source_target_pairs={{0,7},{1,2},{2,1},{3,4},{4,3},{5,6},{6,5},{7,0},{8,15},{9,10},{10,... | collective-permute-start | bytes 626696 | tf_op jit(solution)/shard_map/ppermute | solution.py:394
  13.8 0.6 %collective-permute-start.2 = (bf16[16,6528]{1,0:T(8,128)(2,1)S(1)}, bf16[16,6528]{1,0:T(8,128)(2,1)S(1)}, u32[]{:S(2)}, u32[]{:S(2)}) collective-permute-start(bf16[16,6528]{1,0:T(8,128)(2,1)S(1)} %get-tuple-element.18.refs_0_.refs_1_), channel_id=1, source_target_pairs={{0,6},{1,3},{2,0},{3,5},{4,2},{5,7},{6,4},{7,1},{8,14},{9,11},{10,... | collective-permute-start | bytes 626696 | tf_op jit(solution)/shard_map/ppermute | solution.py:395
  14.5 0.5 collective-permute-start.6
  15.0 2.0 %collective-permute-start.7 = (bf16[32,2944]{1,0:T(8,128)(2,1)S(1)}, bf16[32,2944]{1,0:T(8,128)(2,1)S(1)}, u32[]{:S(2)}, u32[]{:S(2)}) collective-permute-start(bf16[32,2944]{1,0:T(8,128)(2,1)S(1)} %shard_map.61.refs_1_.refs_0_), channel_id=1, source_target_pairs={{0,2},{1,3},{2,0},{3,1},{4,6},{5,7},{6,4},{7,5},{8,10},{9,11},{10,... | collective-permute-start | bytes 565256 | tf_op jit(solution)/shard_map/ppermute | solution.py:49
  17.0 2.5 %collective-permute-done.3.refs_3_ = bf16[16,6528]{1,0:T(8,128)(2,1)S(1)} collective-permute-done((bf16[16,6528]{1,0:T(8,128)(2,1)S(1)}, bf16[16,6528]{1,0:T(8,128)(2,1)S(1)}, u32[]{:S(2)}, u32[]{:S(2)}) %collective-permute-start.3) | collective-permute-done | bytes 208928 | tf_op jit(solution)/shard_map/ppermute | solution.py:394
  19.5 1.6 %collective-permute-done.1.refs_2_.refs_1_ = bf16[16,6528]{1,0:T(8,128)(2,1)S(1)} collective-permute-done((bf16[16,6528]{1,0:T(8,128)(2,1)S(1)}, bf16[16,6528]{1,0:T(8,128)(2,1)S(1)}, u32[]{:S(2)}, u32[]{:S(2)}) %collective-permute-start.1) | collective-permute-done | bytes 208928 | tf_op jit(solution)/shard_map/ppermute | solution.py:49
  21.1 2.9 %collective-permute-done.2.refs_2_ = bf16[16,6528]{1,0:T(8,128)(2,1)S(1)} collective-permute-done((bf16[16,6528]{1,0:T(8,128)(2,1)S(1)}, bf16[16,6528]{1,0:T(8,128)(2,1)S(1)}, u32[]{:S(2)}, u32[]{:S(2)}) %collective-permute-start.2) | collective-permute-done | bytes 208928 | tf_op jit(solution)/shard_map/ppermute | solution.py:395
  24.0 0.2 shard_map.58
  24.4 4.0 %collective-permute-done.6.refs_0_ = bf16[32,2944]{1,0:T(8,128)(2,1)S(1)} collective-permute-done((bf16[32,2944]{1,0:T(8,128)(2,1)S(1)}, bf16[32,2944]{1,0:T(8,128)(2,1)S(1)}, u32[]{:S(2)}, u32[]{:S(2)}) %collective-permute-start.6) | collective-permute-done | bytes 188448 | tf_op jit(solution)/shard_map/ppermute | solution.py:49
  28.4 2.3 %collective-permute-start.10 = (bf16[32,2944]{1,0:T(8,128)(2,1)S(1)}, bf16[32,2944]{1,0:T(8,128)(2,1)S(1)}, u32[]{:S(2)}, u32[]{:S(2)}) collective-permute-start(bf16[32,2944]{1,0:T(8,128)(2,1)S(1)} %shard_map.62.refs_2_.refs_1_), channel_id=1, source_target_pairs={{0,16},{1,17},{2,18},{3,19},{4,20},{5,21},{6,22},{7,23},{8,24},{9,... | collective-permute-start | bytes 565256 | tf_op jit(solution)/shard_map/ppermute | solution.py:49
  30.7 2.0 %collective-permute-start.8 = (bf16[32,2944]{1,0:T(8,128)(2,1)S(1)}, bf16[32,2944]{1,0:T(8,128)(2,1)S(1)}, u32[]{:S(2)}, u32[]{:S(2)}) collective-permute-start(bf16[32,2944]{1,0:T(8,128)(2,1)S(1)} %collective-permute-done.6.refs_0_), channel_id=1, source_target_pairs={{0,2},{1,3},{2,0},{3,1},{4,6},{5,7},{6,4},{7,5},{8,10},{9,11},{10,... | collective-permute-start | bytes 565256 | tf_op jit(solution)/shard_map/ppermute | solution.py:49
  32.8 1.4 %shard_map.57.refs_0_ = bf16[8,288,512]{2,1,0:T(8,128)(2,1)S(1)} custom-call(bf16[9,9,16,33]{3,2,1,0:T(8,128)(2,1)S(1)} %bitcast.10, s32[16,9]{1,0:T(8,128)S(1)} %copy-done.3, bf16[16,6528]{1,0:T(8,128)(2,1)S(1)} %collective-permute-done.1.refs_2_.refs_1_), custom_call_target="tpu_custom_call" | custom-call | tf_op jit(solution)/shard_map/pallas_call | solution.py:24
  34.2 3.9 %shard_map.59 = bf16[2,16,16,2944]{3,2,1,0:T(8,128)(2,1)S(1)} custom-call(bf16[8,288,512]{2,1,0:T(8,128)(2,1)S(1)} %shard_map.57.refs_0_, bf16[20,4,16,384]{3,2,1,0:T(8,128)(2,1)S(1)} %get-tuple-element.19.refs_1_, bf16[4,4,16,384]{3,2,1,0:T(8,128)(2,1)S(1)} %collective-permute-done.4.refs_2_), custom_call_target="tpu_custom_call" | custom-call | tf_op jit(solution)/shard_map/pallas_call | solution.py:24
  38.1 1.4 %collective-permute-done.11.refs_6_.refs_2_ = bf16[32,2944]{1,0:T(8,128)(2,1)S(1)} collective-permute-done((bf16[32,2944]{1,0:T(8,128)(2,1)S(1)}, bf16[32,2944]{1,0:T(8,128)(2,1)S(1)}, u32[]{:S(2)}, u32[]{:S(2)}) %collective-permute-start.11) | collective-permute-done | bytes 188448 | tf_op jit(solution)/shard_map/ppermute | solution.py:49
  39.7 0.6 %collective-permute-start.13 = (bf16[3,32,2944]{2,1,0:T(8,128)(2,1)S(1)}, bf16[3,32,2944]{2,1,0:T(8,128)(2,1)S(1)}, u32[]{:S(2)}, u32[]{:S(2)}) collective-permute-start(bf16[3,32,2944]{2,1,0:T(8,128)(2,1)S(1)} %shard_map.66.refs_3_), channel_id=1, source_target_pairs={{0,8},{1,9},{2,10},{3,11},{4,12},{5,13},{6,14},{7,15},{8,0},{9,1},... | collective-permute-start | bytes 1695752 | tf_op jit(solution)/shard_map/ppermute | solution.py:49
  40.3 1.7 %collective-permute-start.14 = (bf16[32,2944]{1,0:T(8,128)(2,1)S(1)}, bf16[32,2944]{1,0:T(8,128)(2,1)S(1)}, u32[]{:S(2)}, u32[]{:S(2)}) collective-permute-start(bf16[32,2944]{1,0:T(8,128)(2,1)S(1)} %shard_map.64.refs_3_.refs_4_), channel_id=1, source_target_pairs={{0,16},{1,17},{2,18},{3,19},{4,20},{5,21},{6,22},{7,23},{8,24},{9,... | collective-permute-start | bytes 565256 | tf_op jit(solution)/shard_map/ppermute | solution.py:49
  41.9 0.8 %collective-permute-done.13.refs_4_ = bf16[3,32,2944]{2,1,0:T(8,128)(2,1)S(1)} collective-permute-done((bf16[3,32,2944]{2,1,0:T(8,128)(2,1)S(1)}, bf16[3,32,2944]{2,1,0:T(8,128)(2,1)S(1)}, u32[]{:S(2)}, u32[]{:S(2)}) %collective-permute-start.13) | collective-permute-done | bytes 565280 | tf_op jit(solution)/shard_map/ppermute | solution.py:49
  42.7 1.4 %shard_map.67 = (bf16[256,512]{1,0:T(8,128)(2,1)S(1)}, bf16[16,32,2944]{2,1,0:T(8,128)(2,1)S(1)}) custom-call(bf16[2,256,2944]{2,1,0:T(8,128)(2,1)S(1)} %bitcast.6, bf16[4,32,2944]{2,1,0:T(8,128)(2,1)S(1)} %shard_map.65.refs_1_, bf16[4,32,2944]{2,1,0:T(8,128)(2,1)S(1)} %collective-permute-done.12.refs_2_, bf16[3,32,2944]{2,1,0:T(8,128)(2,1)S(1)} %shard_map.66.refs_3_, ...), custom_call_target="tpu_custom_call" | custom-call | tf_op jit(solution)/shard_map/pallas_call | solution.py:24
  44.1 2.1 %collective-permute-start.16 = (bf16[256,512]{1,0:T(8,128)(2,1)S(1)}, bf16[256,512]{1,0:T(8,128)(2,1)S(1)}, u32[]{:S(2)}, u32[]{:S(2)}) collective-permute-start(bf16[256,512]{1,0:T(8,128)(2,1)S(1)} %get-tuple-element.24.refs_1_), channel_id=1, source_target_pairs={{0,1},{1,0},{2,3},{3,2},{4,5},{5,4},{6,7},{7,6},{8,9},{9,8},{10,11... | collective-permute-start | bytes 786440 | tf_op jit(solution)/shard_map/ppermute | solution.py:49
  46.2 0.7 %collective-permute-done.14.refs_0_ = bf16[32,2944]{1,0:T(8,128)(2,1)S(1)} collective-permute-done((bf16[32,2944]{1,0:T(8,128)(2,1)S(1)}, bf16[32,2944]{1,0:T(8,128)(2,1)S(1)}, u32[]{:S(2)}, u32[]{:S(2)}) %collective-permute-start.14) | collective-permute-done | bytes 188448 | tf_op jit(solution)/shard_map/ppermute | solution.py:49
  47.1 1.4 %collective-permute-done.15.refs_2_ = bf16[1,32,2944]{2,1,0:T(8,128)(2,1)S(1)} collective-permute-done((bf16[1,32,2944]{2,1,0:T(8,128)(2,1)S(1)}, bf16[1,32,2944]{2,1,0:T(8,128)(2,1)S(1)}, u32[]{:S(2)}, u32[]{:S(2)}) %collective-permute-start.15) | collective-permute-done | bytes 188448 | tf_op jit(solution)/shard_map/ppermute | solution.py:49
  48.5 0.6 %shard_map.69.refs_2_.refs_3_ = bf16[128,128]{1,0:T(8,128)(2,1)S(1)} custom-call(bf16[2,256,2944]{2,1,0:T(8,128)(2,1)S(1)} %bitcast.7, bf16[1,32,2944]{2,1,0:T(8,128)(2,1)S(1)} %shard_map.68.refs_1_, bf16[1,32,2944]{2,1,0:T(8,128)(2,1)S(1)} %collective-permute-done.15.refs_2_), custom_call_target="tpu_custom_call" | custom-call | tf_op jit(solution)/shard_map/pallas_call | solution.py:24
  49.1 2.1 %collective-permute-start.17 = (bf16[128,128]{1,0:T(8,128)(2,1)S(1)}, bf16[128,128]{1,0:T(8,128)(2,1)S(1)}, u32[]{:S(2)}, u32[]{:S(2)}) collective-permute-start(bf16[128,128]{1,0:T(8,128)(2,1)S(1)} %shard_map.69.refs_2_.refs_3_), channel_id=1, source_target_pairs={{0,1},{1,0},{2,3},{3,2},{4,5},{5,4},{6,7},{7,6},{8,9},{9,8},{10,11... | collective-permute-start | bytes 98312 | tf_op jit(solution)/shard_map/ppermute | solution.py:49
  51.2 1.0 %shard_map.70.refs_0_ = f32[256,512]{1,0:T(8,128)S(1)} custom-call(bf16[2,256,2944]{2,1,0:T(8,128)(2,1)S(1)} %bitcast.8, bf16[16,32,2944]{2,1,0:T(8,128)(2,1)S(1)} %get-tuple-element.23.refs_1_, bf16[128,128]{1,0:T(8,128)(2,1)S(1)} %shard_map.69.refs_2_.refs_3_), custom_call_target="tpu_custom_call" | custom-call | tf_op jit(solution)/shard_map/pallas_call | solution.py:24
  52.2 0.6 %shard_map.72.refs_1_ = f32[128,128]{1,0:T(8,128)S(1)} custom-call(bf16[2,256,2944]{2,1,0:T(8,128)(2,1)S(1)} %bitcast.9, bf16[1,32,2944]{2,1,0:T(8,128)(2,1)S(1)} %shard_map.68.refs_1_, bf16[1,32,2944]{2,1,0:T(8,128)(2,1)S(1)} %collective-permute-done.15.refs_2_, bf16[128,128]{1,0:T(8,128)(2,1)S(1)} %shard_map.69.refs_2_.refs_3_), custom_call_target="tpu_custom_call" | custom-call | tf_op jit(solution)/shard_map/pallas_call | solution.py:24
  52.9 0.3 collective-permute-done.16.refs_1_
  53.4 0.2 collective-permute-done.17.refs_2_
  53.5 0.9 %shard_map.73 = bf16[256,512]{1,0:T(8,128)(2,1)} custom-call(bf16[256,512]{1,0:T(8,128)(2,1)S(1)} %shard_map.71.refs_0_, f32[128,128]{1,0:T(8,128)S(1)} %shard_map.72.refs_1_, bf16[128,128]{1,0:T(8,128)(2,1)S(1)} %collective-permute-done.17.refs_2_, f32[1,512]{1,0:T(1,128)S(1)} %bitcast.13), custom_call_target="tpu_custom_call" | custom-call | tf_op jit(solution)/shard_map/pallas_call | solution.py:24
  (33 shorter events, 1.1 us)
Async XLA Ops:
  0.0 1.0 %copy-start = (bf16[16,16,641]{2,1,0:T(8,128)(2,1)S(1)}, bf16[16,16,641]{2,1,0:T(8,128)(2,1)}, u32[]{:S(2)}) copy-start(bf16[16,16,641]{2,1,0:T(8,128)(2,1)} %refs_0_.1) | copy-start | bytes 984580
  1.0 31.8 %copy-start.1 = (bf16[9,16,9,33]{3,1,2,0:T(8,128)(2,1)S(1)}, bf16[9,16,9,33]{3,1,2,0:T(8,128)(2,1)}, u32[]{:S(2)}) copy-start(bf16[9,16,9,33]{3,1,2,0:T(8,128)(2,1)} %param.6) | copy-start | bytes 256612
  1.0 31.8 %copy-start.3 = (s32[16,9]{1,0:T(8,128)S(1)}, s32[16,9]{1,0:T(8,128)}, u32[]{:S(2)}) copy-start(s32[16,9]{1,0:T(8,128)} %refs_1_.1) | copy-start | bytes 1732
  1.0 6.7 %collective-permute-start = (bf16[4,16,641]{2,1,0:T(8,128)(2,1)S(1)}, bf16[4,16,641]{2,1,0:T(8,128)(2,1)S(1)}, u32[]{:S(2)}, u32[]{:S(2)}) collective-permute-start(bf16[4,16,641]{2,1,0:T(8,128)(2,1)S(1)} %get-tuple-element.16), channel_id=1, source_target_pairs={{0,4},{1,5},{2,6},{3,7},{4,0},{5,1},{6,2},{7,3},{8,16},{9,17},{10,... | collective-permute-start | bytes 246152 | tf_op jit(solution)/shard_map/ppermute | solution.py:359
  5.1 0.9 %copy-start.2 = (bf16[9,641,16]{1,2,0:T(8,128)(2,1)S(1)}, bf16[9,641,16]{1,2,0:T(8,128)(2,1)}, u32[]{:S(2)}) copy-start(bf16[9,641,16]{1,2,0:T(8,128)(2,1)} %param.8) | copy-start | bytes 553828
  6.2 8.3 %collective-permute-start.5 = (bf16[16,2944]{1,0:T(8,128)(2,1)S(1)}, bf16[16,2944]{1,0:T(8,128)(2,1)S(1)}, u32[]{:S(2)}, u32[]{:S(2)}) collective-permute-start(bf16[16,2944]{1,0:T(8,128)(2,1)S(1)} %get-tuple-element.22), channel_id=1, source_target_pairs={{0,1},{1,0},{2,3},{3,2},{4,5},{5,4},{6,7},{7,6},{8,9},{9,8},{10,11... | collective-permute-start | bytes 282632 | tf_op jit(solution)/shard_map/ppermute | solution.py:49
  7.9 11.5 %collective-permute-start.3 = (bf16[16,6528]{1,0:T(8,128)(2,1)S(1)}, bf16[16,6528]{1,0:T(8,128)(2,1)S(1)}, u32[]{:S(2)}, u32[]{:S(2)}) collective-permute-start(bf16[16,6528]{1,0:T(8,128)(2,1)S(1)} %get-tuple-element.17), channel_id=1, source_target_pairs={{0,7},{1,2},{2,1},{3,4},{4,3},{5,6},{6,5},{7,0},{8,15},{9,10},{10,... | collective-permute-start | bytes 626696 | tf_op jit(solution)/shard_map/ppermute | solution.py:394
  13.8 7.3 %collective-permute-start.1 = (bf16[16,6528]{1,0:T(8,128)(2,1)S(1)}, bf16[16,6528]{1,0:T(8,128)(2,1)S(1)}, u32[]{:S(2)}, u32[]{:S(2)}) collective-permute-start(bf16[16,6528]{1,0:T(8,128)(2,1)S(1)} %get-tuple-element.17), channel_id=1, source_target_pairs={{0,1},{1,0},{2,3},{3,2},{4,5},{5,4},{6,7},{7,6},{8,9},{9,8},{10,11... | collective-permute-start | bytes 626696 | tf_op jit(solution)/shard_map/ppermute | solution.py:49
  13.8 10.1 %collective-permute-start.2 = (bf16[16,6528]{1,0:T(8,128)(2,1)S(1)}, bf16[16,6528]{1,0:T(8,128)(2,1)S(1)}, u32[]{:S(2)}, u32[]{:S(2)}) collective-permute-start(bf16[16,6528]{1,0:T(8,128)(2,1)S(1)} %get-tuple-element.18.refs_0_.refs_1_), channel_id=1, source_target_pairs={{0,6},{1,3},{2,0},{3,5},{4,2},{5,7},{6,4},{7,1},{8,14},{9,11},{10,... | collective-permute-start | bytes 626696 | tf_op jit(solution)/shard_map/ppermute | solution.py:395
  14.5 13.9 %collective-permute-start.6 = (bf16[32,2944]{1,0:T(8,128)(2,1)S(1)}, bf16[32,2944]{1,0:T(8,128)(2,1)S(1)}, u32[]{:S(2)}, u32[]{:S(2)}) collective-permute-start(bf16[32,2944]{1,0:T(8,128)(2,1)S(1)} %shard_map.61.refs_1_.refs_0_), channel_id=1, source_target_pairs={{0,4},{1,5},{2,6},{3,7},{4,0},{5,1},{6,2},{7,3},{8,12},{9,13},{10,... | collective-permute-start | bytes 565256 | tf_op jit(solution)/shard_map/ppermute | solution.py:49
  15.0 17.7 %collective-permute-start.7 = (bf16[32,2944]{1,0:T(8,128)(2,1)S(1)}, bf16[32,2944]{1,0:T(8,128)(2,1)S(1)}, u32[]{:S(2)}, u32[]{:S(2)}) collective-permute-start(bf16[32,2944]{1,0:T(8,128)(2,1)S(1)} %shard_map.61.refs_1_.refs_0_), channel_id=1, source_target_pairs={{0,2},{1,3},{2,0},{3,1},{4,6},{5,7},{6,4},{7,5},{8,10},{9,11},{10,... | collective-permute-start | bytes 565256 | tf_op jit(solution)/shard_map/ppermute | solution.py:49
  24.2 10.0 %collective-permute-start.4 = (bf16[4,4,16,384]{3,2,1,0:T(8,128)(2,1)S(1)}, bf16[4,4,16,384]{3,2,1,0:T(8,128)(2,1)S(1)}, u32[]{:S(2)}, u32[]{:S(2)}) collective-permute-start(bf16[4,4,16,384]{3,2,1,0:T(8,128)(2,1)S(1)} %get-tuple-element.20), channel_id=1, source_target_pairs={{0,8},{1,9},{2,10},{3,11},{4,12},{5,13},{6,14},{7,15},{8,0},{9,1},... | collective-permute-start | bytes 589832 | tf_op jit(solution)/shard_map/ppermute | solution.py:49
  24.3 13.8 %collective-permute-start.9 = (bf16[32,2944]{1,0:T(8,128)(2,1)S(1)}, bf16[32,2944]{1,0:T(8,128)(2,1)S(1)}, u32[]{:S(2)}, u32[]{:S(2)}) collective-permute-start(bf16[32,2944]{1,0:T(8,128)(2,1)S(1)} %shard_map.61.refs_1_.refs_0_), channel_id=1, source_target_pairs={{0,16},{1,17},{2,18},{3,19},{4,20},{5,21},{6,22},{7,23},{8,24},{9,... | collective-permute-start | bytes 565256 | tf_op jit(solution)/shard_map/ppermute | solution.py:49
  28.4 9.8 %collective-permute-start.10 = (bf16[32,2944]{1,0:T(8,128)(2,1)S(1)}, bf16[32,2944]{1,0:T(8,128)(2,1)S(1)}, u32[]{:S(2)}, u32[]{:S(2)}) collective-permute-start(bf16[32,2944]{1,0:T(8,128)(2,1)S(1)} %shard_map.62.refs_2_.refs_1_), channel_id=1, source_target_pairs={{0,16},{1,17},{2,18},{3,19},{4,20},{5,21},{6,22},{7,23},{8,24},{9,... | collective-permute-start | bytes 565256 | tf_op jit(solution)/shard_map/ppermute | solution.py:49
  30.7 7.5 %collective-permute-start.8 = (bf16[32,2944]{1,0:T(8,128)(2,1)S(1)}, bf16[32,2944]{1,0:T(8,128)(2,1)S(1)}, u32[]{:S(2)}, u32[]{:S(2)}) collective-permute-start(bf16[32,2944]{1,0:T(8,128)(2,1)S(1)} %collective-permute-done.6.refs_0_), channel_id=1, source_target_pairs={{0,2},{1,3},{2,0},{3,1},{4,6},{5,7},{6,4},{7,5},{8,10},{9,11},{10,... | collective-permute-start | bytes 565256 | tf_op jit(solution)/shard_map/ppermute | solution.py:49
  32.7 6.8 %collective-permute-start.11 = (bf16[32,2944]{1,0:T(8,128)(2,1)S(1)}, bf16[32,2944]{1,0:T(8,128)(2,1)S(1)}, u32[]{:S(2)}, u32[]{:S(2)}) collective-permute-start(bf16[32,2944]{1,0:T(8,128)(2,1)S(1)} %shard_map.63.refs_3_.refs_2_), channel_id=1, source_target_pairs={{0,16},{1,17},{2,18},{3,19},{4,20},{5,21},{6,22},{7,23},{8,24},{9,... | collective-permute-start | bytes 565256 | tf_op jit(solution)/shard_map/ppermute | solution.py:49
  39.6 3.1 %collective-permute-start.12 = (bf16[4,32,2944]{2,1,0:T(8,128)(2,1)S(1)}, bf16[4,32,2944]{2,1,0:T(8,128)(2,1)S(1)}, u32[]{:S(2)}, u32[]{:S(2)}) collective-permute-start(bf16[4,32,2944]{2,1,0:T(8,128)(2,1)S(1)} %shard_map.65.refs_1_), channel_id=1, source_target_pairs={{0,8},{1,9},{2,10},{3,11},{4,12},{5,13},{6,14},{7,15},{8,0},{9,1},... | collective-permute-start | bytes 2261000 | tf_op jit(solution)/shard_map/ppermute | solution.py:49
  39.7 3.0 %collective-permute-start.13 = (bf16[3,32,2944]{2,1,0:T(8,128)(2,1)S(1)}, bf16[3,32,2944]{2,1,0:T(8,128)(2,1)S(1)}, u32[]{:S(2)}, u32[]{:S(2)}) collective-permute-start(bf16[3,32,2944]{2,1,0:T(8,128)(2,1)S(1)} %shard_map.66.refs_3_), channel_id=1, source_target_pairs={{0,8},{1,9},{2,10},{3,11},{4,12},{5,13},{6,14},{7,15},{8,0},{9,1},... | collective-permute-start | bytes 1695752 | tf_op jit(solution)/shard_map/ppermute | solution.py:49
  40.3 6.7 %collective-permute-start.14 = (bf16[32,2944]{1,0:T(8,128)(2,1)S(1)}, bf16[32,2944]{1,0:T(8,128)(2,1)S(1)}, u32[]{:S(2)}, u32[]{:S(2)}) collective-permute-start(bf16[32,2944]{1,0:T(8,128)(2,1)S(1)} %shard_map.64.refs_3_.refs_4_), channel_id=1, source_target_pairs={{0,16},{1,17},{2,18},{3,19},{4,20},{5,21},{6,22},{7,23},{8,24},{9,... | collective-permute-start | bytes 565256 | tf_op jit(solution)/shard_map/ppermute | solution.py:49
  44.1 9.1 %collective-permute-start.16 = (bf16[256,512]{1,0:T(8,128)(2,1)S(1)}, bf16[256,512]{1,0:T(8,128)(2,1)S(1)}, u32[]{:S(2)}, u32[]{:S(2)}) collective-permute-start(bf16[256,512]{1,0:T(8,128)(2,1)S(1)} %get-tuple-element.24.refs_1_), channel_id=1, source_target_pairs={{0,1},{1,0},{2,3},{3,2},{4,5},{5,4},{6,7},{7,6},{8,9},{9,8},{10,11... | collective-permute-start | bytes 786440 | tf_op jit(solution)/shard_map/ppermute | solution.py:49
  47.0 1.5 %collective-permute-start.15 = (bf16[1,32,2944]{2,1,0:T(8,128)(2,1)S(1)}, bf16[1,32,2944]{2,1,0:T(8,128)(2,1)S(1)}, u32[]{:S(2)}, u32[]{:S(2)}) collective-permute-start(bf16[1,32,2944]{2,1,0:T(8,128)(2,1)S(1)} %shard_map.68.refs_1_), channel_id=1, source_target_pairs={{0,8},{1,9},{2,10},{3,11},{4,12},{5,13},{6,14},{7,15},{8,0},{9,1},... | collective-permute-start | bytes 565256 | tf_op jit(solution)/shard_map/ppermute | solution.py:49
  49.1 4.5 %collective-permute-start.17 = (bf16[128,128]{1,0:T(8,128)(2,1)S(1)}, bf16[128,128]{1,0:T(8,128)(2,1)S(1)}, u32[]{:S(2)}, u32[]{:S(2)}) collective-permute-start(bf16[128,128]{1,0:T(8,128)(2,1)S(1)} %shard_map.69.refs_2_.refs_3_), channel_id=1, source_target_pairs={{0,1},{1,0},{2,3},{3,2},{4,5},{5,4},{6,7},{7,6},{8,9},{9,8},{10,11... | collective-permute-start | bytes 98312 | tf_op jit(solution)/shard_map/ppermute | solution.py:49
  52.2 1.0 %copy-start.4 = (f32[512]{0:T(512)S(1)}, f32[512]{0:T(512)}, u32[]{:S(2)}) copy-start(f32[512]{0:T(512)} %param.9) | copy-start | bytes 6148
